TPU v7x, 512 devices: a whole 4x4x16 slice. The times are simulated.
512 devices in a mesh: dp: 32 (over z, x_hi), seq: 16 (over y, x_lo, core).
Axes of the slice: x: 4 (x_hi: 2, x_lo: 2; x = x_hi * 2 + x_lo), y: 4, z: 16, core: 2. Of those that a mesh axis runs over, the one named last changes fastest.
Arguments:
- queries: bfloat16 [32, 4096, 1024], P('dp', 'seq'), may hold values from -6 to 6
- keys: bfloat16 [32, 4096, 1024], P('dp', 'seq'), may hold values from -6 to 6
- values: bfloat16 [32, 4096, 1024], P('dp', 'seq'), may hold values from -6 to 6
- out_grad: bfloat16 [32, 4096, 1024], P('dp', 'seq'), may hold values from -6 to 6
- out_weight: bfloat16 [1024, 1024], P(('dp', 'seq')), may hold values from -0.1875 to 0.1875
- layout: int32 [32, 4], replicated, may hold values from 0 to 31, as said below
Outputs:
- mixed: bfloat16 [32, 4096, 1024], P('dp', 'seq')
- query_grad: bfloat16 [32, 4096, 1024], P('dp', 'seq')
- key_grad: bfloat16 [32, 4096, 1024], P('dp', 'seq')
- value_grad: bfloat16 [32, 4096, 1024], P('dp', 'seq')
- weight_grad: float32 [1024, 1024], P(('dp', 'seq'))
Inputs may be any that keep to these rules, and one draw needn't show every extreme that they name: `layout`: row b lists 4 distinct blocks, the first being b.
All inputs are finite; a program needn't handle non-finite values.
Results may differ from a plain program's by a relative error of at most 0.015.
Values may be sent and summed in bfloat16 or wider, within the bound.
No kernel may reach another device: no remote copies, remote signals or barrier semaphores. Data moves between devices by JAX's collectives and lax.ppermute only.
A program may use at most 64 MiB of HBM per device.

v0:
```python
import math

import jax
import jax.numpy as jnp
from jax import lax
from jax.sharding import PartitionSpec as P

H = 16


def sparse_attention(query, keyset, values, grad_out, layout):
    seq_len, head_count, head_size = query.shape
    block_count, per_row = layout.shape
    block_len = seq_len // block_count
    scale = 1.0 / math.sqrt(head_size)
    group_shape = (block_count // 4, 4, block_len, head_count, head_size)
    key_blocks = keyset.reshape(block_count, block_len, head_count, head_size)
    value_blocks = values.reshape(block_count, block_len, head_count, head_size)
    block_ids = jnp.arange(block_count)

    def per_group(totals, pieces):
        key_total, value_total = totals
        query_group, grad_group, chosen = pieces
        flat_ids = chosen.reshape(-1)
        key_sel = jnp.take(key_blocks, flat_ids, axis=0).reshape(
            4, per_row * block_len, head_count, head_size
        )
        value_sel = jnp.take(value_blocks, flat_ids, axis=0).reshape(
            4, per_row * block_len, head_count, head_size
        )
        scores = (
            jnp.einsum("gqhe,gkhe->ghqk", query_group, key_sel, preferred_element_type=jnp.float32)
            * scale
        )
        top = jnp.max(scores, axis=-1, keepdims=True)
        expo = jnp.exp(scores - top)
        probs = expo / jnp.sum(expo, axis=-1, keepdims=True)
        probs_low = probs.astype(jnp.bfloat16)
        attended = jnp.einsum(
            "ghqk,gkhe->gqhe", probs_low, value_sel, preferred_element_type=jnp.float32
        ).astype(jnp.bfloat16)
        dprob = jnp.einsum(
            "gqhe,gkhe->ghqk", grad_group, value_sel, preferred_element_type=jnp.float32
        )
        inner = jnp.sum(probs * dprob, axis=-1, keepdims=True)
        dscore = (probs * (dprob - inner) * scale).astype(jnp.bfloat16)
        grad_query = jnp.einsum(
            "ghqk,gkhe->gqhe", dscore, key_sel, preferred_element_type=jnp.float32
        ).astype(jnp.bfloat16)
        key_part = jnp.einsum(
            "ghqk,gqhe->gkhe", dscore, query_group, preferred_element_type=jnp.float32
        )
        value_part = jnp.einsum(
            "ghqk,gqhe->gkhe", probs_low, grad_group, preferred_element_type=jnp.float32
        )
        key_part = key_part.reshape(4 * per_row, block_len * head_count * head_size)
        value_part = value_part.reshape(4 * per_row, block_len * head_count * head_size)
        onehot = (flat_ids[:, None] == block_ids[None, :]).astype(jnp.float32)
        contract = (((0,), (0,)), ((), ()))
        key_total = key_total + lax.dot_general(
            onehot, key_part, contract, precision=lax.Precision.HIGHEST
        )
        value_total = value_total + lax.dot_general(
            onehot, value_part, contract, precision=lax.Precision.HIGHEST
        )
        return ((key_total, value_total), (attended, grad_query))

    zeros = jnp.zeros((block_count, block_len * head_count * head_size), jnp.float32)
    totals, outputs = lax.scan(
        per_group,
        (zeros, zeros),
        (
            query.reshape(group_shape),
            grad_out.reshape(group_shape),
            layout.reshape(block_count // 4, 4, per_row),
        ),
    )
    attended = outputs[0].reshape(seq_len, head_count, head_size)
    grad_query = outputs[1].reshape(seq_len, head_count, head_size)
    grad_key = totals[0].reshape(seq_len, head_count, head_size).astype(jnp.bfloat16)
    grad_value = totals[1].reshape(seq_len, head_count, head_size).astype(jnp.bfloat16)
    return (attended, grad_query, grad_key, grad_value)


def body(queries, keys, values, out_grad, out_weight, layout):
    tok_rows = queries.shape[1]
    model_width = queries.shape[2]
    head_size = model_width // H
    split_shape = (tok_rows, H, head_size)
    full_weight = lax.all_gather(out_weight, ("dp", "seq"), axis=0, tiled=True)
    grad_rows = out_grad[0]
    grad_attention = lax.dot_general(
        grad_rows, full_weight, (((1,), (1,)), ((), ())), preferred_element_type=jnp.float32
    ).astype(jnp.bfloat16)
    query_heads, key_heads, value_heads = (
        lax.all_to_all(
            queries[0].reshape(split_shape), "seq", split_axis=1, concat_axis=0, tiled=True
        ),
        lax.all_to_all(
            keys[0].reshape(split_shape), "seq", split_axis=1, concat_axis=0, tiled=True
        ),
        lax.all_to_all(
            values[0].reshape(split_shape), "seq", split_axis=1, concat_axis=0, tiled=True
        ),
    )
    grad_heads = lax.all_to_all(
        grad_attention.reshape(split_shape), "seq", split_axis=1, concat_axis=0, tiled=True
    )
    attended_heads, query_part, key_part, value_part = sparse_attention(
        query_heads, key_heads, value_heads, grad_heads, layout
    )
    attended, grad_query, grad_key, grad_value = (
        lax.all_to_all(attended_heads, "seq", split_axis=0, concat_axis=1, tiled=True),
        lax.all_to_all(query_part, "seq", split_axis=0, concat_axis=1, tiled=True),
        lax.all_to_all(key_part, "seq", split_axis=0, concat_axis=1, tiled=True),
        lax.all_to_all(value_part, "seq", split_axis=0, concat_axis=1, tiled=True),
    )
    attended_flat = attended.reshape(tok_rows, model_width)
    mixed = jnp.dot(attended_flat, full_weight, preferred_element_type=jnp.float32).astype(
        jnp.bfloat16
    )
    weight_grad = lax.psum_scatter(
        lax.dot_general(
            attended_flat, grad_rows, (((0,), (0,)), ((), ())), preferred_element_type=jnp.float32
        ),
        ("dp", "seq"),
        scatter_dimension=0,
        tiled=True,
    )
    out_shape = (1, tok_rows, model_width)
    return (
        mixed.reshape(out_shape),
        grad_query.reshape(out_shape),
        grad_key.reshape(out_shape),
        grad_value.reshape(out_shape),
        weight_grad,
    )


def solution(mesh):
    in_specs = (
        P("dp", "seq", None),
        P("dp", "seq", None),
        P("dp", "seq", None),
        P("dp", "seq", None),
        P(("dp", "seq"), None),
        P(),
    )
    out_specs = (
        P("dp", "seq", None),
        P("dp", "seq", None),
        P("dp", "seq", None),
        P("dp", "seq", None),
        P(("dp", "seq"), None),
    )
    return jax.shard_map(body, mesh=mesh, in_specs=in_specs, out_specs=out_specs, check_vma=False)
```

profile of v0, /device:TPU:1, one launch (start us, length us, event | category | flops | bytes accessed | tf_op | source)
XLA Modules:
  0.0 1541.7 jit_solution(11276180676085692954)
XLA Ops:
  10.0 10.2 all-to-all-start
  21.3 8.9 all-to-all-done
  30.2 4.5 all-to-all-start.1
  35.7 9.0 all-to-all-done.1
  44.7 4.5 all-to-all-start.3
  49.2 729.1 %all-gather.3.cloned.1.call-done = bf16[512,2,1024]{2,1,0:T(2,128)(2,1)} async-done(((bf16[1,2,1024]{2,1,0:T(2,128)(2,1)}), bf16[512,2,1024]{2,1,0:T(2,128)(2,1)}) %all-gather.3.cloned.1.call-update) | async-done | bytes 2097168 | tf_op jit(solution)/shard_map/all_gather | solution.py:90
  778.3 4.1 reshape.213
  782.4 2.3 convolution_convert_fusion.3
  785.8 4.2 all-to-all-start.2
  795.4 4.6 all-to-all-done.2
  802.3 195.0 %while.17 = (s32[]{:T(128)}, f32[32,8192]{1,0:T(8,128)}, f32[32,8192]{1,0:T(8,128)S(1)}, bf16[8,4,128,1,64]{2,4,1,3,0:T(8,128)(2,1)}, bf16[8,4,128,1,64]{2,4,1,3...) while((s32[]{:T(128)}, f32[32,8192]{1,0:T(8,128)}, ...), condition=%wide.region_4.6_spmd.clone, body=%wide.region_0.5_spmd.clone.sunk | while | flops 308875904 | bytes 35275788 | solution.py:69
  808.5 4.7 fusion.80
  813.1 4.9 convolution_bitcast_fusion.4
  818.1 2.3 fusion.79
  831.7 4.7 fusion.80
  836.4 4.9 convolution_bitcast_fusion.4
  841.3 2.3 fusion.79
  847.2 3.0 convolution_add_fusion.4
  856.2 4.7 fusion.80
  860.8 4.9 convolution_bitcast_fusion.4
  865.8 2.3 fusion.79
  871.7 3.0 convolution_add_fusion.4
  880.7 4.7 fusion.80
  885.3 4.9 convolution_bitcast_fusion.4
  890.3 2.3 fusion.79
  896.2 3.0 convolution_add_fusion.4
  905.2 4.7 fusion.80
  909.8 4.9 convolution_bitcast_fusion.4
  914.8 2.3 fusion.79
  920.7 3.0 convolution_add_fusion.4
  929.7 4.7 fusion.80
  934.3 4.9 convolution_bitcast_fusion.4
  939.3 2.3 fusion.79
  945.2 3.0 convolution_add_fusion.4
  954.2 4.7 fusion.80
  958.8 4.9 convolution_bitcast_fusion.4
  969.7 3.0 convolution_add_fusion.4
  978.6 4.7 fusion.80
  983.3 4.9 convolution_bitcast_fusion.4
  988.3 2.3 fusion.79
  994.2 3.0 convolution_add_fusion.4
  998.8 3.1 reshape.228
  1002.4 24.0 %reduce.6 = bf16[4096,64]{1,0:T(8,128)(2,1)S(1)} reduce(bf16[4096,1,64]{2,1,0:T(2,128)(2,1)} %reshape.228, bf16[]{:T(256)} %broadcast.99), dimensions={1}, to_apply=%reshape.228.reduce_sub_computation | reduce | bytes 1048578 | tf_op jit(solution)/shard_map/reshape | solution.py:78
  1027.1 13.5 all_to_all.120
  1040.6 3.5 reshape.231
  1044.1 4.6 copy.99
  1049.0 2.7 fusion.41
  1053.2 3.1 reshape.229
  1056.4 23.4 %reduce.7 = bf16[4096,64]{1,0:T(8,128)(2,1)S(1)} reduce(bf16[4096,1,64]{2,1,0:T(2,128)(2,1)} %reshape.229, bf16[]{:T(256)} %broadcast.99), dimensions={1}, to_apply=%reshape.229.reduce_sub_computation | reduce | bytes 1048578 | tf_op jit(solution)/shard_map/reshape | solution.py:79
  1081.3 5.5 all-to-all-start.5
  1086.9 2.4 convert_element_type.76
  1089.3 23.5 %reduce.9 = bf16[4096,64]{1,0:T(8,128)(2,1)S(1)} reduce(bf16[4096,1,64]{2,1,0:T(2,128)(2,1)} %convert_element_type.76, bf16[]{:T(256)} %broadcast.99), dimensions={1}, to_apply=%convert_element_type.76.reduce_sub_computation | reduce | bytes 1048578 | tf_op jit(solution)/shard_map/convert_element_type | solution.py:81
  1114.3 6.1 all-to-all-start.7
  1120.4 2.4 convert_element_type.75
  1122.9 23.5 %reduce.8 = bf16[4096,64]{1,0:T(8,128)(2,1)S(1)} reduce(bf16[4096,1,64]{2,1,0:T(2,128)(2,1)} %convert_element_type.75, bf16[]{:T(256)} %broadcast.99), dimensions={1}, to_apply=%convert_element_type.75.reduce_sub_computation | reduce | bytes 1048578 | tf_op jit(solution)/shard_map/convert_element_type | solution.py:80
  1147.8 5.7 all-to-all-start.6
  1153.6 5.5 reshape.233
  1159.1 4.6 copy.103
  1165.0 3.5 reshape.237
  1168.5 4.6 copy.109
  1174.4 3.5 reshape.235
  1177.9 4.6 copy.106
  1183.8 3.1 fusion.40
  1186.9 346.4 %all-reduce.3.cloned.1.call-done = f32[1024,1024]{1,0:T(8,128)} async-done(((f32[1024,1024]{1,0:T(8,128)}), f32[1024,1024]{1,0:T(8,128)}) %all-reduce.3.cloned.1.call-update) | async-done | bytes 4194320
  (276 shorter events, 107.1 us)
Async XLA Ops:
  7.2 775.2 %copy-start = (bf16[1,256,1024]{2,1,0:T(8,128)(2,1)S(1)}, bf16[1,256,1024]{2,1,0:T(8,128)(2,1)}, u32[]{:S(2)}) copy-start(bf16[1,256,1024]{2,1,0:T(8,128)(2,1)} %param.13) | copy-start | bytes 1572868
  7.2 13.1 copy-start.4
  7.2 771.1 %all-gather.3.cloned.1.call-start = ((), (), s32[]{:S(2)}) async-start(), calls=%async_computation.8 | async-start | bytes 2101248 | tf_op jit(solution)/shard_map/all_gather | solution.py:90
  7.9 26.8 %copy-start.5 = (bf16[1,256,1024]{2,1,0:T(8,128)(2,1)S(1)}, bf16[1,256,1024]{2,1,0:T(8,128)(2,1)}, u32[]{:S(2)}) copy-start(bf16[1,256,1024]{2,1,0:T(8,128)(2,1)} %param.12) | copy-start | bytes 1572868
  10.0 20.1 %all-to-all-start = ((bf16[256,16,64]{0,2,1:T(8,128)(2,1)}), bf16[256,16,64]{0,2,1:T(8,128)(2,1)S(1)}, u32[]{:S(2)}, u32[]{:S(2)}) async-start(bf16[256,16,64]{0,2,1:T(8,128)(2,1)} %bitcast.1), calls=%async_computation | async-start | bytes 1048576 | tf_op jit(solution)/shard_map/all_to_all | solution.py:96
  30.2 14.5 all-to-all-start.1
  44.7 741.1 %all-to-all-start.3 = ((bf16[256,16,64]{0,2,1:T(8,128)(2,1)}), bf16[256,16,64]{0,2,1:T(8,128)(2,1)S(1)}, u32[]{:S(2)}, u32[]{:S(2)}) async-start(bf16[256,16,64]{0,2,1:T(8,128)(2,1)} %bitcast.12), calls=%async_computation.3 | async-start | bytes 1048576 | tf_op jit(solution)/shard_map/all_to_all | solution.py:102
  782.4 7.7 copy-start.6
  785.8 14.2 all-to-all-start.2
  790.0 743.2 %all-reduce.3.cloned.1.call-start = ((), (), s32[]{:S(2)}) async-start(), calls=%async_computation.9 | async-start | bytes 8388608
  802.6 2.8 copy-start.2
  818.1 2.3 copy-start.7
  824.0 1.8 copy-start.3
  825.8 2.8 copy-start.2
  841.3 2.3 copy-start.7
  847.2 3.0 copy-start.3
  850.3 2.8 copy-start.2
  865.8 2.3 copy-start.7
  871.7 3.0 copy-start.3
  874.8 2.8 copy-start.2
  890.3 2.3 copy-start.7
  896.2 3.0 copy-start.3
  899.3 2.8 copy-start.2
  914.8 2.3 copy-start.7
  920.7 3.0 copy-start.3
  923.8 2.8 copy-start.2
  939.3 2.3 copy-start.7
  945.2 3.0 copy-start.3
  948.3 2.8 copy-start.2
  963.8 2.3 copy-start.7
  969.7 3.0 copy-start.3
  972.8 2.8 copy-start.2
  988.3 2.3 copy-start.7
  994.2 3.0 copy-start.3
  1081.3 32.9 %all-to-all-start.5 = ((bf16[16,2,8192]{2,1,0:T(2,128)(2,1)}), bf16[16,2,8192]{2,1,0:T(2,128)(2,1)}, u32[]{:S(2)}, u32[]{:S(2)}) async-start(bf16[16,2,8192]{2,1,0:T(2,128)(2,1)} %reshape.232), calls=%async_computation.5 | async-start | bytes 1048576 | tf_op jit(solution)/shard_map/all_to_all | solution.py:114
  1112.8 7.6 copy-start.1
  1114.3 33.6 %all-to-all-start.7 = ((bf16[16,2,8192]{2,1,0:T(2,128)(2,1)}), bf16[16,2,8192]{2,1,0:T(2,128)(2,1)S(1)}, u32[]{:S(2)}, u32[]{:S(2)}) async-start(bf16[16,2,8192]{2,1,0:T(2,128)(2,1)} %reshape.236), calls=%async_computation.7 | async-start | bytes 1048576 | tf_op jit(solution)/shard_map/all_to_all | solution.py:116
  1147.8 26.5 %all-to-all-start.6 = ((bf16[16,2,8192]{2,1,0:T(2,128)(2,1)}), bf16[16,2,8192]{2,1,0:T(2,128)(2,1)S(1)}, u32[]{:S(2)}, u32[]{:S(2)}) async-start(bf16[16,2,8192]{2,1,0:T(2,128)(2,1)} %reshape.234), calls=%async_computation.6 | async-start | bytes 1048576 | tf_op jit(solution)/shard_map/all_to_all | solution.py:115
Sparse Core Ops, SparseCore 0:
  10.1 768.0 all-gather.2
  1051.8 481.4 all-reduce.2
where the time goes:
time: 1550 us; the launch traced here: 1540 us
  waiting for transfers between devices  1100 us (71%)
  matrix products  150 us (10%)
  local copies, waits for them, and re-layouts  127 us (8%)
  other arithmetic  95.5 us (6%)
  starting transfers between devices  40.9 us (3%)
    all_gather x1, waiting for transfers between devices, body(): full_weight = lax.all_gather(out_weight, ('dp', 'seq'), axis=0, tiled=True)  729 us
    unnamed x3, waiting for transfers between devices  347 us
    dot_general x8, matrix products, per_group(): jnp.einsum('ghqk,gqhe->gkhe', dscore, query_group, preferred_element_type...  39.6 us
    dot_general x8, matrix products, per_group(): jnp.einsum('ghqk,gkhe->gqhe', dscore, key_sel, preferred_element_type=jnp...  37.4 us
    unnamed x33, local copies, waits for them, and re-layouts  35.7 us
  transfers between devices with their start and end apart: 9, of which 5 were waited for; matrix products, arithmetic and copies ran while one was open for 9% of the time, Pallas kernels for 0%

commit v1 on v0

v1 whole, which is shorter than its diff:
```python
import jax
import jax.numpy as jnp
from jax import lax
from jax.experimental import pallas as pl
from jax.experimental.pallas import tpu as pltpu
from jax.sharding import PartitionSpec as P

H = 16
E = 64
B = 128
BF = jnp.bfloat16
F32 = jnp.float32
NT = (((1,), (1,)), ((), ()))
NN = (((1,), (0,)), ((), ()))
TN = (((0,), (0,)), ((), ()))
VM = pl.BlockSpec(memory_space=pltpu.VMEM)
SM = pl.BlockSpec(memory_space=pltpu.SMEM)


def call(kernel, outs, in_specs, scratch=(), flops=0, moved=0):
    return pl.pallas_call(
        kernel,
        out_shape=[jax.ShapeDtypeStruct(shape, dtype) for shape, dtype in outs],
        in_specs=in_specs,
        out_specs=[VM] * len(outs),
        scratch_shapes=list(scratch),
        compiler_params=pltpu.CompilerParams(vmem_limit_bytes=48 * 2**20),
        cost_estimate=pl.CostEstimate(flops=flops, bytes_accessed=moved, transcendentals=0),
    )


def low_lanes(rows):
    return lax.broadcasted_iota(jnp.int32, (rows, 2 * E), 1) < E


def interleave(a, b):
    low = low_lanes(a.shape[0])
    return jnp.where(low, a, pltpu.roll(b, E, 1)), jnp.where(low, pltpu.roll(a, E, 1), b)


def pack_kernel(q_ref, k_ref, v_ref, qs_ref, kvs_ref):
    for pair in range(H // 2):
        cols = slice(pair * 2 * E, (pair + 1) * 2 * E)
        even, odd = interleave(q_ref[:B, cols].astype(F32), q_ref[B:, cols].astype(F32))
        qs_ref[2 * pair] = even.astype(BF)
        qs_ref[2 * pair + 1] = odd.astype(BF)
        even, odd = interleave(k_ref[:, cols].astype(F32), v_ref[:, cols].astype(F32))
        kvs_ref[2 * pair] = even.astype(BF)
        kvs_ref[2 * pair + 1] = odd.astype(BF)


def grad_kernel(og_ref, w_ref, perm_ref, gs_ref, tmp_ref):
    for quad in range(H // 4):
        rows = slice(quad * 4 * E, (quad + 1) * 4 * E)
        g = lax.dot_general(og_ref[...], w_ref[rows, :], NT, preferred_element_type=F32)
        tmp_ref[:, rows] = g.astype(BF)
    for quad in range(H // 4):
        rows = slice(quad * 4 * E, (quad + 1) * 4 * E)
        g = lax.dot_general(tmp_ref[...], perm_ref[rows, :], NT, preferred_element_type=F32)
        for i in range(2):
            part = g[:, i * 2 * E:(i + 1) * 2 * E]
            even, odd = interleave(part[:B], part[B:])
            gs_ref[4 * quad + 2 * i] = even.astype(BF)
            gs_ref[4 * quad + 2 * i + 1] = odd.astype(BF)


def attention_kernel(layout_ref, q_ref, g_ref, kv_ref, att_ref, dq_ref, dkv_ref, kvt_ref, acc_ref):
    blocks = layout_ref.shape[0]
    scale = 1.0 / E**0.5
    log2e = 1.4426950408889634

    def prepare(b, carry):
        at = pl.multiple_of(b * B, B)
        kvt_ref[b] = kv_ref[pl.ds(at, B), :].T
        acc_ref[pl.ds(at, B), :] = jnp.zeros((B, 2 * E), F32)
        return carry

    lax.fori_loop(0, blocks, prepare, 0, unroll=4)

    def per_pair(s, carry):
        at = pl.multiple_of(s * B, B)
        qt = q_ref[pl.ds(at, B), :].T
        gt = g_ref[pl.ds(at, B), :].T
        zero = jnp.zeros((E, B), BF)
        att_t, dq_t = [], []
        for p in range(2):
            ids = [layout_ref[2 * s + p, j] for j in range(4)]
            starts = [pl.multiple_of(i * B, B) for i in ids]
            rows = slice(p * E, (p + 1) * E)
            xt = jnp.concatenate(
                [
                    jnp.concatenate([qt[rows], zero], axis=1),
                    jnp.concatenate([zero, gt[rows]], axis=1),
                ],
                axis=0,
            )
            kv = jnp.concatenate([kv_ref[pl.ds(i, B), :] for i in starts], axis=0)
            both = lax.dot_general(kv, xt, NN, preferred_element_type=F32)
            scores, dprob = both[:, :B], both[:, B:]
            top = jnp.max(scores, axis=0, keepdims=True)
            expo = jnp.exp2((scores - top) * (scale * log2e))
            inverse = 1.0 / jnp.sum(expo, axis=0, keepdims=True)
            inner = jnp.sum(expo * dprob, axis=0, keepdims=True) * inverse
            probs = (expo * inverse).astype(BF)
            dscore = (expo * ((dprob - inner) * (inverse * scale))).astype(BF)
            yt = jnp.concatenate([dscore, probs], axis=1)
            kvt = jnp.concatenate([kvt_ref[i] for i in ids], axis=1)
            out = lax.dot_general(kvt, yt, NN, preferred_element_type=F32)
            dq_t.append(out[:E, :B])
            att_t.append(out[E:, B:])
            part = lax.dot_general(yt, xt, NT, preferred_element_type=F32)
            for j in range(4):
                acc_ref[pl.ds(starts[j], B), :] += part[j * B:(j + 1) * B]
        att_ref[pl.ds(at, B), :] = jnp.concatenate(att_t, axis=0).T.astype(BF)
        dq_ref[pl.ds(at, B), :] = jnp.concatenate(dq_t, axis=0).T.astype(BF)
        return carry

    lax.fori_loop(0, blocks // 2, per_pair, 0)
    dkv_ref[...] = acc_ref[...].astype(BF)


def unpack_tokens(src_ref, dst_ref):
    for pair in range(H // 2):
        cols = slice(pair * 2 * E, (pair + 1) * 2 * E)
        first, second = interleave(src_ref[2 * pair].astype(F32), src_ref[2 * pair + 1].astype(F32))
        dst_ref[:B, cols] = first.astype(BF)
        dst_ref[B:, cols] = second.astype(BF)


def project_kernel(as_ref, og_ref, w_ref, perm_ref, mixed_ref, part_ref, tmp_ref, att_ref):
    unpack_tokens(as_ref, tmp_ref)
    wide = 4 * E
    for i in range(H // 4):
        cols = slice(i * wide, (i + 1) * wide)
        att_ref[:, cols] = lax.dot_general(
            tmp_ref[...], perm_ref[:, cols], NN, preferred_element_type=F32
        ).astype(BF)
    for i in range(H // 4):
        cols = slice(i * wide, (i + 1) * wide)
        mixed_ref[:, cols] = lax.dot_general(
            att_ref[...], w_ref[:, cols], NN, preferred_element_type=F32
        ).astype(BF)
    for i in range(H // 4):
        cols = slice(i * wide, (i + 1) * wide)
        part_ref[cols, :] = lax.dot_general(
            att_ref[:, cols], og_ref[...], TN, preferred_element_type=F32
        ).astype(part_ref.dtype)


def unpack_kernel(dqs_ref, dkvs_ref, dq_ref, dk_ref, dv_ref):
    unpack_tokens(dqs_ref, dq_ref)
    for pair in range(H // 2):
        cols = slice(pair * 2 * E, (pair + 1) * 2 * E)
        dk, dv = interleave(dkvs_ref[2 * pair].astype(F32), dkvs_ref[2 * pair + 1].astype(F32))
        dk_ref[:, cols] = dk.astype(BF)
        dv_ref[:, cols] = dv.astype(BF)


def sum_kernel(parts_ref, total_ref):
    total_ref[...] = jnp.sum(parts_ref[...].astype(F32), axis=0).astype(total_ref.dtype)


def add_up(parts, dtype):
    return call(sum_kernel, [(parts.shape[1:], dtype)], [VM], moved=2 * parts.size)(parts)[0]


def attend(layout, q, g, kv):
    tokens = kv.shape[0]
    half = (tokens // 2, 2 * E)
    return call(
        attention_kernel,
        [(half, BF), (half, BF), ((tokens, 2 * E), BF)],
        [SM, VM, VM, VM],
        [pltpu.VMEM((tokens // B, 2 * E, B), BF), pltpu.VMEM((tokens, 2 * E), F32)],
        flops=12 * tokens * 512 * E,
        moved=5 * 2**20,
    )(layout, q, g, kv)


def exchange(x, axis):
    return lax.all_to_all(x, axis, split_axis=0, concat_axis=0, tiled=True)


def row_order(width, dp, seq):
    each = width // (dp * seq)
    place = lax.broadcasted_iota(jnp.int32, (width, width), 1)
    inner = place % (dp * each)
    owner = (inner // each) * seq + place // (dp * each)
    feature = lax.broadcasted_iota(jnp.int32, (width, width), 0)
    return (feature == owner * each + inner % each).astype(BF)


def gather_weight(rows, dp):
    column = exchange(jnp.tile(rows[None], (dp, 1, 1)), "dp")
    return lax.all_gather(column.reshape(-1, rows.shape[1]), "seq", axis=0, tiled=True)


def reduce_weight(part, dp, seq):
    width = part.shape[1]
    part = add_up(exchange(part.reshape(seq, -1, width), "seq"), BF)
    return exchange(part.reshape(dp, -1, width), "dp").astype(F32).sum(axis=0)


def body(dp, seq, queries, keys, values, out_grad, out_weight, layout):
    tokens, width = queries.shape[1:]
    grad = out_grad[0]
    weight = gather_weight(out_weight, dp)
    perm = row_order(width, dp, seq)
    qs, kvs = call(
        pack_kernel, [((H, B, 2 * E), BF), ((H, tokens, 2 * E), BF)], [VM] * 3, moved=3 * 2**20
    )(queries[0], keys[0], values[0])
    kv = exchange(kvs, "seq").reshape(-1, 2 * E)
    q = exchange(qs, "seq").reshape(-1, 2 * E)
    gs = call(
        grad_kernel, [((H, B, 2 * E), BF)], [VM] * 3, [pltpu.VMEM((tokens, width), BF)],
        flops=2 * tokens * width * width, moved=3 * 2**20,
    )(grad, weight, perm)[0]
    g = exchange(gs, "seq").reshape(-1, 2 * E)
    att, dq, dkv = attend(layout, q, g, kv)
    att = exchange(att.reshape(H, B, 2 * E), "seq")
    mixed, part = call(
        project_kernel, [((tokens, width), BF), ((width, width), BF)], [VM] * 4,
        [pltpu.VMEM((tokens, width), BF)] * 2,
        flops=4 * tokens * width * width, moved=6 * 2**20,
    )(att, grad, weight, perm)
    weight_grad = reduce_weight(part, dp, seq)
    dq = exchange(dq.reshape(H, B, 2 * E), "seq")
    dkv = exchange(dkv.reshape(H, 2 * B, 2 * E), "seq")
    dq, dk, dv = call(
        unpack_kernel, [((tokens, width), BF)] * 3, [VM] * 2, moved=3 * 2**20
    )(dq, dkv)
    return mixed[None], dq[None], dk[None], dv[None], weight_grad


def solution(mesh):
    rows = P("dp", "seq", None)
    split = P(("dp", "seq"), None)
    sizes = mesh.shape["dp"], mesh.shape["seq"]
    return jax.shard_map(
        lambda *args: body(*sizes, *args),
        mesh=mesh,
        in_specs=(rows, rows, rows, rows, split, P()),
        out_specs=(rows, rows, rows, rows, split),
        check_vma=False,
    )
```

time: 1550 us -> 240 us (0.15)
  waiting for transfers between devices: 1100 us -> 65.5 us
  matrix products: 150 us -> 0 us
  local copies, waits for them, and re-layouts: 127 us -> 11.4 us
  other arithmetic: 95.5 us -> 1.32 us
  blocking collectives: 13.5 us -> 78.8 us
  Pallas kernels: 0 us -> 26.7 us
    all_gather x1, waiting for transfers between devices: 729 us -> 10.7 us  [gather_weight(): lax.all_gather(column.reshape(-1, rows.shape[1]), 'seq', axis=0, tiled=True)]
    unnamed x3 -> x1, waiting for transfers between devices: 347 us -> 0.02 us
    dot_general x59 -> x0, matrix products: 139 us -> none  [the longest x8 39.6 us: per_group(): jnp.einsum('ghqk,gqhe->gkhe', dscore, query_group, preferred_element_type...]
    all_to_all x1 -> x3, blocking collectives: 13.5 us -> 78.8 us  [exchange(): return lax.all_to_all(x, axis, split_axis=0, concat_axis=0, tiled=True)]
    reshape x2 -> x0, other arithmetic: 47.4 us -> none  [the longest x1 24 us: sparse_attention(): attended = outputs[0].reshape(seq_len, head_count, head_size)]
    convert_element_type x4 -> x1, other arithmetic: 47 us -> 0.58 us  [row_order(): return (feature == owner * each + inner % each).astype(BF)]
    all_to_all x7 -> x6, waiting for transfers between devices: 22.5 us -> 54.8 us  [exchange(): return lax.all_to_all(x, axis, split_axis=0, concat_axis=0, tiled=True)]
    pallas_call x0 -> x6, Pallas kernels: none -> 26.7 us  [the longest x1 17.1 us: attend(): call(attention_kernel, [(half, BF), (half, BF), ((tokens, 2 * E), BF)], [...]
  transfers between devices with their start and end apart: 9 -> 7, of which waited for: 5 -> 7; matrix products, arithmetic and copies ran while one was open for 9% -> 1% of each run, Pallas kernels for 0% -> 4%
where the time goes in v1:
time: 240 us; the launch traced here: 238 us
  blocking collectives  78.8 us (33%)
  waiting for transfers between devices  65.5 us (27%)
  starting transfers between devices  40.2 us (17%)
  Pallas kernels  26.7 us (11%)
  between operations  14.1 us (6%)
  local copies, waits for them, and re-layouts  11.4 us (5%)
    all_to_all x3, blocking collectives, exchange(): return lax.all_to_all(x, axis, split_axis=0, concat_axis=0, tiled=True)  78.8 us
    all_to_all x6, waiting for transfers between devices, exchange(): return lax.all_to_all(x, axis, split_axis=0, concat_axis=0, tiled=True)  54.8 us
    all_to_all x6, starting transfers between devices, exchange(): return lax.all_to_all(x, axis, split_axis=0, concat_axis=0, tiled=True)  40.1 us
    pallas_call x1, Pallas kernels, attend(): call(attention_kernel, [(half, BF), (half, BF), ((tokens, 2 * E), BF)], [...  17.1 us
    all_gather x1, waiting for transfers between devices, gather_weight(): lax.all_gather(column.reshape(-1, rows.shape[1]), 'seq', axis=0, tiled=True)  10.7 us
    unnamed x29, local copies, waits for them, and re-layouts  9.27 us
  transfers between devices with their start and end apart: 7, of which 7 were waited for; matrix products, arithmetic and copies ran while one was open for 1% of the time, Pallas kernels for 4%

profile of v1, /device:TPU:1, one launch (start us, length us, event | category | flops | bytes accessed | tf_op | source)
XLA Modules:
  0.0 238.2 jit_solution(18327717959243578002)
XLA Ops:
  7.2 0.0 all-gather.2.cloned.1.call-start
  7.2 0.8 tile.2
  8.0 33.0 %all_to_all.45 = bf16[32,2,1024]{2,1,0:T(2,128)(2,1)S(1)} all-to-all(bf16[32,2,1024]{2,1,0:T(2,128)(2,1)S(1)} %tile.2), channel_id=1, replica_groups=mesh['dp'=32,'seq'=16] {'dp'}, dimensions={0} | all-to-all | bytes 262144 | tf_op jit(solution)/shard_map/all_to_all | solution.py:181
  41.0 0.7 reshape.41
  41.7 0.0 all-gather.2.cloned.1.call-update
  41.7 0.0 copy-start.9
  41.8 1.0 copy-done.9
  42.8 0.0 copy-start.10
  42.8 1.0 copy-done.10
  43.8 0.0 copy-start.11
  43.8 1.0 copy-done.11
  44.9 1.8 shard_map.101
  46.7 8.2 %all-to-all-start = ((bf16[16,128,128]{2,1,0:T(8,128)(2,1)}), bf16[16,128,128]{2,1,0:T(8,128)(2,1)S(1)}, u32[]{:S(2)}, u32[]{:S(2)}) async-start(bf16[16,128,128]{2,1,0:T(8,128)(2,1)} %get-tuple-element.15), calls=%async_computation | async-start | bytes 1048576 | tf_op jit(solution)/shard_map/all_to_all | solution.py:181
  55.0 12.9 %all-to-all-done = bf16[16,128,128]{2,1,0:T(8,128)(2,1)S(1)} async-done(((bf16[16,128,128]{2,1,0:T(8,128)(2,1)}), bf16[16,128,128]{2,1,0:T(8,128)(2,1)S(1)}, u32[]{:S(2)}, u32[]{:S(2)}) %all-to-all-start) | async-done | bytes 524320 | tf_op jit(solution)/shard_map/all_to_all | solution.py:181
  67.8 0.0 copy-start.3
  67.8 4.7 %all-to-all-start.3 = ((bf16[16,256,128]{2,1,0:T(8,128)(2,1)}), bf16[16,256,128]{2,1,0:T(8,128)(2,1)}, u32[]{:S(2)}, u32[]{:S(2)}) async-start(bf16[16,256,128]{2,1,0:T(8,128)(2,1)} %get-tuple-element.16), calls=%async_computation.3 | async-start | bytes 2097152 | tf_op jit(solution)/shard_map/all_to_all | solution.py:181
  72.6 0.6 fusion.9.perm_ref
  73.1 0.0 copy-start
  73.2 10.7 %all-gather.2.cloned.1.call-done.w_ref = bf16[1024,1024]{1,0:T(8,128)(2,1)} async-done(((bf16[64,1024]{1,0:T(8,128)(2,1)}), bf16[1024,1024]{1,0:T(8,128)(2,1)}) %all-gather.2.cloned.1.call-update) | async-done | bytes 2097168 | tf_op jit(solution)/shard_map/all_gather | solution.py:195
  83.9 0.0 copy-done.3
  83.9 0.0 copy-start.1
  83.9 1.6 copy-done.1
  85.5 0.0 copy-start.13
  85.5 2.2 shard_map.102
  87.6 0.0 copy-done
  87.6 1.6 all-to-all-done.3
  89.2 5.7 %all-to-all-start.2 = ((bf16[16,128,128]{2,1,0:T(8,128)(2,1)}), bf16[16,128,128]{2,1,0:T(8,128)(2,1)S(1)}, u32[]{:S(2)}, u32[]{:S(2)}) async-start(bf16[16,128,128]{2,1,0:T(8,128)(2,1)} %shard_map.102), calls=%async_computation.2 | async-start | bytes 1048576 | tf_op jit(solution)/shard_map/all_to_all | solution.py:181
  94.8 0.0 copy-done.13
  94.8 0.1 copy.11.layout_ref
  94.9 9.7 %all-to-all-done.2 = bf16[16,128,128]{2,1,0:T(8,128)(2,1)S(1)} async-done(((bf16[16,128,128]{2,1,0:T(8,128)(2,1)}), bf16[16,128,128]{2,1,0:T(8,128)(2,1)S(1)}, u32[]{:S(2)}, u32[]{:S(2)}) %all-to-all-start.2) | async-done | bytes 524320 | tf_op jit(solution)/shard_map/all_to_all | solution.py:181
  104.6 17.1 %shard_map.103 = (bf16[2048,128]{1,0:T(8,128)(2,1)S(1)}, bf16[2048,128]{1,0:T(8,128)(2,1)S(1)}, bf16[4096,128]{1,0:T(8,128)(2,1)S(1)}) custom-call(s32[32,4]{1,0:T(8,128)S(1)} %copy.11.layout_ref, bf16[2048,128]{1,0:T(8,128)(2,1)S(1)} %bitcast.22, bf16[2048,128]{1,0:T(8,128)(2,1)S(1)} %bitcast.24, bf16[4096,128]{1,0:T(8,128)(2,1)} %bitcast.6.kv_ref), custom_call_target="tpu_custom_call" | custom-call | flops 1610612736 | bytes 5242880 | tf_op jit(solution)/shard_map/pallas_call | solution.py:170
  121.7 0.0 copy-start.8
  121.7 1.0 copy-done.8
  122.7 0.0 copy-start.12
  122.7 0.0 copy-start.2
  122.7 14.4 %all_to_all.46.as_ref = bf16[16,128,128]{2,1,0:T(8,128)(2,1)} all-to-all(bf16[16,128,128]{2,1,0:T(8,128)(2,1)S(1)} %bitcast.25), channel_id=1, replica_groups=mesh['dp'=32,'seq'=16] {'seq'}, dimensions={0} | all-to-all | bytes 1048576 | tf_op jit(solution)/shard_map/all_to_all | solution.py:181
  137.1 0.0 copy-done.12
  137.1 4.5 %all-to-all-start.5 = ((bf16[16,128,128]{2,1,0:T(8,128)(2,1)}), bf16[16,128,128]{2,1,0:T(8,128)(2,1)S(1)}, u32[]{:S(2)}, u32[]{:S(2)}) async-start(bf16[16,128,128]{2,1,0:T(8,128)(2,1)} %bitcast.23), calls=%async_computation.5 | async-start | bytes 1048576 | tf_op jit(solution)/shard_map/all_to_all | solution.py:181
  141.7 0.0 copy-done.2
  141.7 0.0 copy-start.6
  141.7 1.0 copy-done.6
  142.7 3.7 %shard_map.104 = (bf16[256,1024]{1,0:T(8,128)(2,1)}, bf16[1024,1024]{1,0:T(8,128)(2,1)S(1)}) custom-call(bf16[16,128,128]{2,1,0:T(8,128)(2,1)S(1)} %copy-done.6, bf16[256,1024]{1,0:T(8,128)(2,1)S(1)} %bitcast.16, bf16[1024,1024]{1,0:T(8,128)(2,1)S(1)} %copy-done.2, bf16[1024,1024]{1,0:T(8,128)(2,1)} %copy-done), custom_call_target="tpu_custom_call" | custom-call | flops 1073741824 | bytes 6291456 | tf_op jit(solution)/shard_map/pallas_call | solution.py:221
  146.4 0.0 copy-start.7
  146.4 1.4 copy-done.7
  147.8 3.8 %all-to-all-done.5.dqs_ref = bf16[16,128,128]{2,1,0:T(8,128)(2,1)S(1)} async-done(((bf16[16,128,128]{2,1,0:T(8,128)(2,1)}), bf16[16,128,128]{2,1,0:T(8,128)(2,1)S(1)}, u32[]{:S(2)}, u32[]{:S(2)}) %all-to-all-start.5) | async-done | bytes 524320 | tf_op jit(solution)/shard_map/all_to_all | solution.py:181
  151.6 0.0 copy-start.4
  151.6 31.4 %all_to_all.47.parts_ref = bf16[16,64,1024]{2,1,0:T(8,128)(2,1)S(1)} all-to-all(bf16[16,64,1024]{2,1,0:T(8,128)(2,1)} %bitcast.17), channel_id=1, replica_groups=mesh['dp'=32,'seq'=16] {'seq'}, dimensions={0} | all-to-all | bytes 4194304 | tf_op jit(solution)/shard_map/all_to_all | solution.py:181
  183.0 0.0 copy-done.4
  183.0 4.6 %all-to-all-start.6 = ((bf16[16,256,128]{2,1,0:T(8,128)(2,1)}), bf16[16,256,128]{2,1,0:T(8,128)(2,1)S(1)}, u32[]{:S(2)}, u32[]{:S(2)}) async-start(bf16[16,256,128]{2,1,0:T(8,128)(2,1)} %bitcast.18), calls=%async_computation.6 | async-start | bytes 2097152 | tf_op jit(solution)/shard_map/all_to_all | solution.py:181
  187.6 0.3 shard_map.106
  187.8 0.7 reshape.48
  188.5 14.9 %all-to-all-done.6.dkvs_ref = bf16[16,256,128]{2,1,0:T(8,128)(2,1)S(1)} async-done(((bf16[16,256,128]{2,1,0:T(8,128)(2,1)}), bf16[16,256,128]{2,1,0:T(8,128)(2,1)S(1)}, u32[]{:S(2)}, u32[]{:S(2)}) %all-to-all-start.6) | async-done | bytes 1048608 | tf_op jit(solution)/shard_map/all_to_all | solution.py:181
  203.5 12.3 %all-to-all-start.8 = ((bf16[32,2,1024]{2,1,0:T(2,128)(2,1)}), bf16[32,2,1024]{2,1,0:T(2,128)(2,1)S(1)}, u32[]{:S(2)}, u32[]{:S(2)}) async-start(bf16[32,2,1024]{2,1,0:T(2,128)(2,1)} %reshape.48), calls=%async_computation.8 | async-start | bytes 262144 | tf_op jit(solution)/shard_map/all_to_all | solution.py:181
  215.8 0.0 copy-start.5
  215.8 1.0 copy-done.5
  216.9 1.7 shard_map.105
  218.6 12.0 %all-to-all-done.8 = bf16[32,2,1024]{2,1,0:T(2,128)(2,1)S(1)} async-done(((bf16[32,2,1024]{2,1,0:T(2,128)(2,1)}), bf16[32,2,1024]{2,1,0:T(2,128)(2,1)S(1)}, u32[]{:S(2)}, u32[]{:S(2)}) %all-to-all-start.8) | async-done | bytes 131104 | tf_op jit(solution)/shard_map/all_to_all | solution.py:181
  230.6 0.7 convert_reduce_fusion
  (3 shorter events, 0.0 us)
Async XLA Ops:
  7.2 76.7 %all-gather.2.cloned.1.call-start = ((), (), s32[]{:S(2)}) async-start(), calls=%async_computation.9 | async-start | bytes 2228224 | tf_op jit(solution)/shard_map/all_gather | solution.py:195
  41.7 1.0 copy-start.9
  42.8 1.0 copy-start.10
  43.8 1.0 copy-start.11
  46.7 21.1 %all-to-all-start = ((bf16[16,128,128]{2,1,0:T(8,128)(2,1)}), bf16[16,128,128]{2,1,0:T(8,128)(2,1)S(1)}, u32[]{:S(2)}, u32[]{:S(2)}) async-start(bf16[16,128,128]{2,1,0:T(8,128)(2,1)} %get-tuple-element.15), calls=%async_computation | async-start | bytes 1048576 | tf_op jit(solution)/shard_map/all_to_all | solution.py:181
  67.8 16.1 %copy-start.3 = (bf16[1,256,1024]{2,1,0:T(8,128)(2,1)S(1)}, bf16[1,256,1024]{2,1,0:T(8,128)(2,1)}, u32[]{:S(2)}) copy-start(bf16[1,256,1024]{2,1,0:T(8,128)(2,1)} %param.9) | copy-start | bytes 1572868
  67.8 21.4 %all-to-all-start.3 = ((bf16[16,256,128]{2,1,0:T(8,128)(2,1)}), bf16[16,256,128]{2,1,0:T(8,128)(2,1)}, u32[]{:S(2)}, u32[]{:S(2)}) async-start(bf16[16,256,128]{2,1,0:T(8,128)(2,1)} %get-tuple-element.16), calls=%async_computation.3 | async-start | bytes 2097152 | tf_op jit(solution)/shard_map/all_to_all | solution.py:181
  73.1 14.5 %copy-start = (bf16[1024,1024]{1,0:T(8,128)(2,1)}, bf16[1024,1024]{1,0:T(8,128)(2,1)S(1)}, u32[]{:S(2)}) copy-start(bf16[1024,1024]{1,0:T(8,128)(2,1)S(1)} %fusion.9.perm_ref) | copy-start | bytes 6291460
  83.9 1.6 copy-start.1
  85.5 9.4 %copy-start.13 = (s32[32,4]{0,1:T(4,128)S(1)}, s32[32,4]{0,1:T(4,128)}, u32[]{:S(2)}) copy-start(s32[32,4]{0,1:T(4,128)} %param.11) | copy-start | bytes 1540
  89.2 15.5 %all-to-all-start.2 = ((bf16[16,128,128]{2,1,0:T(8,128)(2,1)}), bf16[16,128,128]{2,1,0:T(8,128)(2,1)S(1)}, u32[]{:S(2)}, u32[]{:S(2)}) async-start(bf16[16,128,128]{2,1,0:T(8,128)(2,1)} %shard_map.102), calls=%async_computation.2 | async-start | bytes 1048576 | tf_op jit(solution)/shard_map/all_to_all | solution.py:181
  121.7 1.0 copy-start.8
  122.7 14.4 %copy-start.12 = (bf16[2048,128]{1,0:T(8,128)(2,1)}, bf16[2048,128]{1,0:T(8,128)(2,1)S(1)}, u32[]{:S(2)}) copy-start(bf16[2048,128]{1,0:T(8,128)(2,1)S(1)} %get-tuple-element.19) | copy-start | bytes 1572868
  122.7 18.9 %copy-start.2 = (bf16[1024,1024]{1,0:T(8,128)(2,1)S(1)}, bf16[1024,1024]{1,0:T(8,128)(2,1)}, u32[]{:S(2)}) copy-start(bf16[1024,1024]{1,0:T(8,128)(2,1)} %all-gather.2.cloned.1.call-done.w_ref) | copy-start | bytes 6291460
  137.1 14.4 %all-to-all-start.5 = ((bf16[16,128,128]{2,1,0:T(8,128)(2,1)}), bf16[16,128,128]{2,1,0:T(8,128)(2,1)S(1)}, u32[]{:S(2)}, u32[]{:S(2)}) async-start(bf16[16,128,128]{2,1,0:T(8,128)(2,1)} %bitcast.23), calls=%async_computation.5 | async-start | bytes 1048576 | tf_op jit(solution)/shard_map/all_to_all | solution.py:181
  141.7 1.0 copy-start.6
  146.4 1.4 copy-start.7
  151.6 31.4 %copy-start.4 = (bf16[16,128,128]{2,1,0:T(8,128)(2,1)}, bf16[16,128,128]{2,1,0:T(8,128)(2,1)S(1)}, u32[]{:S(2)}) copy-start(bf16[16,128,128]{2,1,0:T(8,128)(2,1)S(1)} %all-to-all-done.5.dqs_ref) | copy-start | bytes 1572868
  183.0 20.5 %all-to-all-start.6 = ((bf16[16,256,128]{2,1,0:T(8,128)(2,1)}), bf16[16,256,128]{2,1,0:T(8,128)(2,1)S(1)}, u32[]{:S(2)}, u32[]{:S(2)}) async-start(bf16[16,256,128]{2,1,0:T(8,128)(2,1)} %bitcast.18), calls=%async_computation.6 | async-start | bytes 2097152 | tf_op jit(solution)/shard_map/all_to_all | solution.py:181
  203.5 27.1 %all-to-all-start.8 = ((bf16[32,2,1024]{2,1,0:T(2,128)(2,1)}), bf16[32,2,1024]{2,1,0:T(2,128)(2,1)S(1)}, u32[]{:S(2)}, u32[]{:S(2)}) async-start(bf16[32,2,1024]{2,1,0:T(2,128)(2,1)} %reshape.48), calls=%async_computation.8 | async-start | bytes 262144 | tf_op jit(solution)/shard_map/all_to_all | solution.py:181
  215.8 1.0 copy-start.5
Sparse Core Ops, SparseCore 0:
  41.9 41.9 all-gather.1

commit v2 on v1

v2 whole, which is shorter than its diff:
```python
import functools

import jax
import jax.numpy as jnp
from jax import lax
from jax.experimental import pallas as pl
from jax.experimental.pallas import tpu as pltpu
from jax.sharding import PartitionSpec as P

H = 16
E = 64
B = 128
BF = jnp.bfloat16
F32 = jnp.float32
NT = (((1,), (1,)), ((), ()))
NN = (((1,), (0,)), ((), ()))
TN = (((0,), (0,)), ((), ()))
VM = pl.BlockSpec(memory_space=pltpu.VMEM)
SM = pl.BlockSpec(memory_space=pltpu.SMEM)


def call(kernel, outs, in_specs, scratch=(), flops=0, moved=0):
    return pl.pallas_call(
        kernel,
        out_shape=[jax.ShapeDtypeStruct(shape, dtype) for shape, dtype in outs],
        in_specs=in_specs,
        out_specs=[VM] * len(outs),
        scratch_shapes=list(scratch),
        compiler_params=pltpu.CompilerParams(vmem_limit_bytes=48 * 2**20),
        cost_estimate=pl.CostEstimate(flops=flops, bytes_accessed=moved, transcendentals=0),
    )


def low_lanes(rows):
    return lax.broadcasted_iota(jnp.int32, (rows, 2 * E), 1) < E


def interleave(a, b):
    low = low_lanes(a.shape[0])
    return jnp.where(low, a, pltpu.roll(b, E, 1)), jnp.where(low, pltpu.roll(a, E, 1), b)


def key_rows(b):
    return pl.multiple_of((b // 2) * (3 * B) + B + (b % 2) * B, B)


def pack_kernel(q_ref, k_ref, v_ref, out_ref):
    for pair in range(H // 2):
        cols = slice(pair * 2 * E, (pair + 1) * 2 * E)
        for rows, (even, odd) in (
            (slice(0, B), interleave(q_ref[:B, cols].astype(F32), q_ref[B:, cols].astype(F32))),
            (slice(B, 3 * B), interleave(k_ref[:, cols].astype(F32), v_ref[:, cols].astype(F32))),
        ):
            out_ref[2 * pair, rows] = even.astype(BF)
            out_ref[2 * pair + 1, rows] = odd.astype(BF)


def grad_kernel(og_ref, w_ref, perm_ref, att_ref, out_ref, tmp_ref):
    out_ref[:, :B] = att_ref[...]
    for quad in range(H // 4):
        rows = slice(quad * 4 * E, (quad + 1) * 4 * E)
        g = lax.dot_general(og_ref[...], w_ref[rows, :], NT, preferred_element_type=F32)
        tmp_ref[:, rows] = g.astype(BF)
    for quad in range(H // 4):
        rows = slice(quad * 4 * E, (quad + 1) * 4 * E)
        g = lax.dot_general(tmp_ref[...], perm_ref[rows, :], NT, preferred_element_type=F32)
        for i in range(2):
            part = g[:, i * 2 * E:(i + 1) * 2 * E]
            even, odd = interleave(part[:B], part[B:])
            out_ref[4 * quad + 2 * i, B:] = even.astype(BF)
            out_ref[4 * quad + 2 * i + 1, B:] = odd.astype(BF)


def forward_kernel(unroll, layout_ref, qkv_ref, att_ref, stat_ref, kvt_ref):
    blocks = layout_ref.shape[0]
    scale = 1.0 / E**0.5
    log2e = 1.4426950408889634

    def prepare(b, carry):
        kvt_ref[b] = qkv_ref[pl.ds(key_rows(b), B), :].T
        return carry

    lax.fori_loop(0, blocks, prepare, 0, unroll=4)

    def per_pair(s, carry):
        at = pl.multiple_of(s * B, B)
        qt = qkv_ref[pl.ds(pl.multiple_of(s * 3 * B, B), B), :].T
        zero = jnp.zeros((E, B), BF)
        att_t = []
        for p in range(2):
            ids = [layout_ref[2 * s + p, j] for j in range(4)]
            rhs = jnp.concatenate([qt[p * E:(p + 1) * E], zero], axis=0)
            kv = jnp.concatenate([qkv_ref[pl.ds(key_rows(i), B), :] for i in ids], axis=0)
            scores = lax.dot_general(kv, rhs, NN, preferred_element_type=F32)
            top = jnp.max(scores, axis=0, keepdims=True)
            expo = jnp.exp2((scores - top) * (scale * log2e))
            inverse = 1.0 / jnp.sum(expo, axis=0, keepdims=True)
            probs = (expo * inverse).astype(BF)
            stat_ref[2 * s + p] = jnp.concatenate([top, inverse], axis=0)
            vt = jnp.concatenate([kvt_ref[i, E:, :] for i in ids], axis=1)
            att_t.append(lax.dot_general(vt, probs, NN, preferred_element_type=F32))
        att_ref[pl.ds(at, B), :] = jnp.concatenate(att_t, axis=0).T.astype(BF)
        return carry

    lax.fori_loop(0, blocks // 2, per_pair, 0, unroll=unroll)


def backward_kernel(unroll, layout_ref, qkv_ref, attg_ref, kvt_ref, stat_ref, out_ref, acc_ref):
    blocks = layout_ref.shape[0]
    scale = 1.0 / E**0.5
    log2e = 1.4426950408889634
    acc_ref[...] = jnp.zeros(acc_ref.shape, F32)

    def per_pair(s, carry):
        at = pl.multiple_of(s * 3 * B, B)
        qt = qkv_ref[pl.ds(at, B), :].T
        gt = attg_ref[pl.ds(pl.multiple_of(s * 2 * B + B, B), B), :].T
        zero = jnp.zeros((E, B), BF)
        dq_t = []
        for p in range(2):
            ids = [layout_ref[2 * s + p, j] for j in range(4)]
            starts = [key_rows(i) for i in ids]
            rows = slice(p * E, (p + 1) * E)
            left = jnp.concatenate([qt[rows], zero], axis=0)
            right = jnp.concatenate([zero, gt[rows]], axis=0)
            kv = jnp.concatenate([qkv_ref[pl.ds(i, B), :] for i in starts], axis=0)
            xt = jnp.concatenate([left, right], axis=1)
            both = lax.dot_general(kv, xt, NN, preferred_element_type=F32)
            scores, dprob = both[:, :B], both[:, B:]
            stat = stat_ref[2 * s + p]
            expo = jnp.exp2((scores - stat[:1]) * (scale * log2e))
            inverse = stat[1:]
            inner = jnp.sum(expo * dprob, axis=0, keepdims=True) * inverse
            probs = (expo * inverse).astype(BF)
            dscore = (expo * ((dprob - inner) * (inverse * scale))).astype(BF)
            kt = jnp.concatenate([kvt_ref[i, :E, :] for i in ids], axis=1)
            dq_t.append(lax.dot_general(kt, dscore, NN, preferred_element_type=F32))
            yt = jnp.concatenate([dscore, probs], axis=1)
            part = lax.dot_general(yt, xt, NT, preferred_element_type=F32)
            for j in range(4):
                acc_ref[pl.ds(starts[j], B), :] += part[j * B:(j + 1) * B]
        out_ref[pl.ds(at, B), :] = jnp.concatenate(dq_t, axis=0).T.astype(BF)
        return carry

    lax.fori_loop(0, blocks // 2, per_pair, 0, unroll=unroll)

    def finish(s, carry):
        at = pl.multiple_of(s * 3 * B + B, B)
        out_ref[pl.ds(at, 2 * B), :] = acc_ref[pl.ds(at, 2 * B), :].astype(BF)
        return carry

    lax.fori_loop(0, blocks // 2, finish, 0, unroll=4)

def unpack_tokens(src_ref, dst_ref):
    for pair in range(H // 2):
        cols = slice(pair * 2 * E, (pair + 1) * 2 * E)
        first, second = interleave(
            src_ref[2 * pair, :B].astype(F32), src_ref[2 * pair + 1, :B].astype(F32)
        )
        dst_ref[:B, cols] = first.astype(BF)
        dst_ref[B:, cols] = second.astype(BF)


def reorder(att_ref, perm_ref, out_ref):
    for i in range(H // 4):
        cols = slice(i * 4 * E, (i + 1) * 4 * E)
        out_ref[:, cols] = lax.dot_general(
            att_ref[...], perm_ref[:, cols], NN, preferred_element_type=F32
        ).astype(BF)


def partial_kernel(attg_ref, og_ref, perm_ref, own_ref, other_ref, tmp_ref, att_ref):
    unpack_tokens(attg_ref, tmp_ref)
    reorder(tmp_ref, perm_ref, att_ref)
    half = own_ref.shape[0]
    for ref, base in ((other_ref, half), (own_ref, 0)):
        for i in range(half // (4 * E)):
            cols = slice(base + i * 4 * E, base + (i + 1) * 4 * E)
            ref[i * 4 * E:(i + 1) * 4 * E, :] = lax.dot_general(
                att_ref[:, cols], og_ref[...], TN, preferred_element_type=F32
            ).astype(BF)


def mixed_kernel(attg_ref, w_ref, perm_ref, mixed_ref, tmp_ref, att_ref):
    unpack_tokens(attg_ref, tmp_ref)
    reorder(tmp_ref, perm_ref, att_ref)
    for i in range(H // 4):
        cols = slice(i * 4 * E, (i + 1) * 4 * E)
        mixed_ref[:, cols] = lax.dot_general(
            att_ref[...], w_ref[:, cols], NN, preferred_element_type=F32
        ).astype(BF)


def add_kernel(a_ref, b_ref, out_ref):
    out_ref[...] = (a_ref[...].astype(F32) + b_ref[...].astype(F32)).astype(BF)


def unpack_kernel(src_ref, dq_ref, dk_ref, dv_ref):
    unpack_tokens(src_ref, dq_ref)
    for pair in range(H // 2):
        cols = slice(pair * 2 * E, (pair + 1) * 2 * E)
        dk, dv = interleave(
            src_ref[2 * pair, B:].astype(F32), src_ref[2 * pair + 1, B:].astype(F32)
        )
        dk_ref[:, cols] = dk.astype(BF)
        dv_ref[:, cols] = dv.astype(BF)


def sum_kernel(parts_ref, total_ref):
    total_ref[...] = jnp.sum(parts_ref[...].astype(F32), axis=0).astype(total_ref.dtype)


def add_up(parts, dtype):
    return call(sum_kernel, [(parts.shape[1:], dtype)], [VM], moved=2 * parts.size)(parts)[0]


def forward(layout, qkv):
    rows = qkv.shape[0]
    blocks = layout.shape[0]
    return call(
        functools.partial(forward_kernel, 4),
        [((rows // 3, 2 * E), BF), ((blocks, 2, B), F32), ((blocks, 2 * E, B), BF)],
        [SM, VM],
        flops=2 * rows * 512 * 128 * 2,
        moved=4 * 2**20,
    )(layout, qkv)


def backward(layout, qkv, attg, kvt, stats):
    return call(
        functools.partial(backward_kernel, 4),
        [(qkv.shape, BF)],
        [SM] + [VM] * 4,
        [pltpu.VMEM(qkv.shape, F32)],
        flops=4 * qkv.shape[0] * 512 * 128 * 2,
        moved=6 * 2**20,
    )(layout, qkv, attg, kvt, stats)[0]


def exchange(x, axis, groups=None):
    return lax.all_to_all(
        x, axis, split_axis=0, concat_axis=0, tiled=True, axis_index_groups=groups
    )


def one_hot(width, rows):
    feature = lax.broadcasted_iota(jnp.int32, (width, width), 0)
    return (feature == rows[None, :]).astype(BF)


def gathered_order(width, dp, seq):
    each = width // (dp * seq)
    place = jnp.arange(width)
    owner = (place % (dp * each) // each) * seq + place // (dp * each)
    return owner * each + place % each


def reduced_order(width, dp, seq):
    each = width // (dp * seq)
    place = jnp.arange(width)
    core = (place // (width // 2) + lax.axis_index("seq")) % 2
    inner = place % (width // 2)
    owner = (inner % (dp * each) // each) * seq + inner // (dp * each) * 2 + core
    return owner * each + place % each


def body(dp, seq, queries, keys, values, out_grad, out_weight, layout):
    tokens, width = queries.shape[1:]
    grad = out_grad[0]
    square = 2 * tokens * width * width
    scratch = [pltpu.VMEM((tokens, width), BF)]
    slabs = call(pack_kernel, [((H, 3 * B, 2 * E), BF)], [VM] * 3, moved=3 * 2**20)(
        queries[0], keys[0], values[0]
    )[0]
    column = exchange(jnp.tile(out_weight[None], (dp, 1, 1)), "dp").reshape(-1, width)
    column, slabs = lax.optimization_barrier((column, slabs))
    weight = lax.all_gather(column, "seq", axis=0, tiled=True)
    qkv = exchange(slabs, "seq").reshape(-1, 2 * E)
    att, stats, kvt = forward(layout, qkv)
    gathered = one_hot(width, gathered_order(width, dp, seq))
    reduced = one_hot(width, reduced_order(width, dp, seq))
    attg = call(
        grad_kernel, [((H, 2 * B, 2 * E), BF)], [VM] * 4, scratch, flops=2 * square, moved=6 * 2**20
    )(grad, weight, gathered, att.reshape(H, B, 2 * E))[0]
    attg = exchange(attg, "seq")
    half = (width // 2, width)
    own, other = call(
        partial_kernel, [(half, BF)] * 2, [VM] * 3, scratch * 2, flops=2 * square, moved=6 * 2**20
    )(attg, grad, reduced)
    other = lax.ppermute(other, "seq", [(i, i ^ 1) for i in range(seq)])
    own = call(add_kernel, [(half, BF)], [VM] * 2, moved=3 * 2**20)(own, other)[0]
    groups = [list(range(c, seq, 2)) for c in range(2)]
    terms = exchange(own.reshape(seq // 2, -1, width), "seq", groups)
    total = add_up(terms, BF).reshape(dp, -1, width)
    attg, total = lax.optimization_barrier((attg, total))
    total = exchange(total, "dp")
    slabs = backward(layout, qkv, attg.reshape(-1, 2 * E), kvt, stats)
    mixed = call(
        mixed_kernel, [((tokens, width), BF)], [VM] * 3, scratch * 2,
        flops=2 * square, moved=5 * 2**20,
    )(attg, weight, gathered)[0]
    slabs, total = lax.optimization_barrier((slabs, total))
    weight_grad = total.astype(F32).sum(axis=0)
    slabs = exchange(slabs.reshape(H, 3 * B, 2 * E), "seq")
    dq, dk, dv = call(unpack_kernel, [((tokens, width), BF)] * 3, [VM], moved=3 * 2**20)(slabs)
    return mixed[None], dq[None], dk[None], dv[None], weight_grad


def solution(mesh):
    rows = P("dp", "seq", None)
    split = P(("dp", "seq"), None)
    sizes = mesh.shape["dp"], mesh.shape["seq"]
    return jax.shard_map(
        lambda *args: body(*sizes, *args),
        mesh=mesh,
        in_specs=(rows, rows, rows, rows, split, P()),
        out_specs=(rows, rows, rows, rows, split),
        check_vma=False,
    )
```

time: 240 us -> 205 us (0.85)
  blocking collectives: 78.8 us -> 18 us
  Pallas kernels: 26.7 us -> 38.2 us
  starting transfers between devices: 40.2 us -> 46 us
  waiting for transfers between devices: 65.5 us -> 70.7 us
  other arithmetic: 1.32 us -> 3.83 us
    all_to_all x3 -> x1, blocking collectives: 78.8 us -> 18 us  [exchange(): lax.all_to_all(x, axis, split_axis=0, concat_axis=0, tiled=True, axis_ind...]
    all_to_all x6 -> x5, waiting for transfers between devices: 54.8 us -> 68.4 us  [exchange(): lax.all_to_all(x, axis, split_axis=0, concat_axis=0, tiled=True, axis_ind...]
    pallas_call x5 -> x8, Pallas kernels: 26.5 us -> 38.1 us  [the longest x1 13.2 us: forward(): call(functools.partial(forward_kernel, 4), [((rows // 3, 2 * E), BF), ((b...]
    all_gather x1, waiting for transfers between devices: 10.7 us -> 0.01 us  [body(): weight = lax.all_gather(column, 'seq', axis=0, tiled=True)]
    all_to_all x6 -> x5, starting transfers between devices: 40.1 us -> 43.2 us  [exchange(): lax.all_to_all(x, axis, split_axis=0, concat_axis=0, tiled=True, axis_ind...]
    ppermute x0 -> x1, starting transfers between devices: none -> 2.78 us  [body(): other = lax.ppermute(other, 'seq', [(i, i ^ 1) for i in range(seq)])]
    convert_element_type x1 -> x2, other arithmetic: 0.58 us -> 3.08 us  [one_hot(): return (feature == rows[None, :]).astype(BF)]
  transfers between devices with their start and end apart: 7 -> 7, of which waited for: 7 -> 5; matrix products, arithmetic and copies ran while one was open for 1% -> 2% of each run, Pallas kernels for 4% -> 14%
where the time goes in v2:
time: 205 us
  waiting for transfers between devices  70.7 us (34%)
  starting transfers between devices  46 us (22%)
  Pallas kernels  38.2 us (19%)
  blocking collectives  18 us (9%)
  between operations  14.2 us (7%)
  local copies, waits for them, and re-layouts  13.6 us (7%)
  other arithmetic  3.83 us (2%)
    all_to_all x5, waiting for transfers between devices, exchange(): lax.all_to_all(x, axis, split_axis=0, concat_axis=0, tiled=True, axis_ind...  68.4 us
    all_to_all x5, starting transfers between devices, exchange(): lax.all_to_all(x, axis, split_axis=0, concat_axis=0, tiled=True, axis_ind...  43.2 us
    all_to_all x1, blocking collectives, exchange(): lax.all_to_all(x, axis, split_axis=0, concat_axis=0, tiled=True, axis_ind...  18 us
    pallas_call x1, Pallas kernels, forward(): call(functools.partial(forward_kernel, 4), [((rows // 3, 2 * E), BF), ((b...  13.2 us
    pallas_call x1, Pallas kernels, backward(): call(functools.partial(backward_kernel, 4), [(qkv.shape, BF)], [SM] + [VM...  12.2 us
    unnamed x29, local copies, waits for them, and re-layouts  10.8 us
  transfers between devices with their start and end apart: 7, of which 5 were waited for; matrix products, arithmetic and copies ran while one was open for 2% of the time, Pallas kernels for 14%

profile of v2, /device:TPU:1, one launch (start us, length us, event | category | flops | bytes accessed | tf_op | source)
XLA Modules:
  0.0 204.5 jit_solution(765331863332693430)
XLA Ops:
  7.2 1.4 tile.2
  8.6 18.5 %all-to-all-start = ((bf16[32,2,1024]{2,1,0:T(2,128)(2,1)}), bf16[32,2,1024]{2,1,0:T(2,128)(2,1)S(1)}, u32[]{:S(2)}, u32[]{:S(2)}) async-start(bf16[32,2,1024]{2,1,0:T(2,128)(2,1)} %tile.2), calls=%async_computation | async-start | bytes 262144 | tf_op jit(solution)/shard_map/all_to_all | solution.py:241
  27.1 0.0 all-gather.2.cloned.1.call-start
  27.1 0.0 copy-start.8
  27.1 1.0 copy-done.8
  28.2 0.0 copy-start.9
  28.2 1.0 copy-done.9
  29.2 0.0 copy-start.10
  29.2 1.0 copy-done.10
  30.3 1.9 shard_map.101
  32.1 0.0 copy-start.13
  32.1 9.7 %all-to-all-done = bf16[32,2,1024]{2,1,0:T(2,128)(2,1)S(1)} async-done(((bf16[32,2,1024]{2,1,0:T(2,128)(2,1)}), bf16[32,2,1024]{2,1,0:T(2,128)(2,1)S(1)}, u32[]{:S(2)}, u32[]{:S(2)}) %all-to-all-start) | async-done | bytes 131104 | tf_op jit(solution)/shard_map/all_to_all | solution.py:241
  41.8 0.7 reshape.158
  42.5 0.0 all-gather.2.cloned.1.call-update
  42.6 8.3 %all-to-all-start.1 = ((bf16[16,384,128]{2,1,0:T(8,128)(2,1)}), bf16[16,384,128]{2,1,0:T(8,128)(2,1)S(1)}, u32[]{:S(2)}, u32[]{:S(2)}) async-start(bf16[16,384,128]{2,1,0:T(8,128)(2,1)} %shard_map.101), calls=%async_computation.1 | async-start | bytes 3145728 | tf_op jit(solution)/shard_map/all_to_all | solution.py:241
  50.8 0.0 copy-done.13
  50.8 0.1 copy.11.layout_ref
  50.9 2.2 %fusion.perm_ref = bf16[1024,1024]{1,0:T(8,128)(2,1)} fusion(s32[1024]{0:T(1024)S(1)} %fusion.16), kind=kLoop, calls=%fused_computation.2 | loop fusion | flops 2097152 | bytes 2101248 | tf_op jit(solution)/shard_map/convert_element_type | solution.py:248
  53.1 26.4 %all-to-all-done.1 = bf16[16,384,128]{2,1,0:T(8,128)(2,1)S(1)} async-done(((bf16[16,384,128]{2,1,0:T(8,128)(2,1)}), bf16[16,384,128]{2,1,0:T(8,128)(2,1)S(1)}, u32[]{:S(2)}, u32[]{:S(2)}) %all-to-all-start.1) | async-done | bytes 1572896 | tf_op jit(solution)/shard_map/all_to_all | solution.py:241
  79.6 0.0 copy-start.3
  79.6 0.0 copy-start.6
  79.6 13.2 %shard_map.102 = (bf16[2048,128]{1,0:T(8,128)(2,1)S(1)}, f32[32,2,128]{2,1,0:T(2,128)S(1)}, bf16[32,128,128]{2,1,0:T(8,128)(2,1)S(1)}) custom-call(s32[32,4]{1,0:T(8,128)S(1)} %copy.11.layout_ref, bf16[6144,128]{1,0:T(8,128)(2,1)S(1)} %bitcast.15), custom_call_target="tpu_custom_call" | custom-call | flops 1610612736 | bytes 4194304 | tf_op jit(solution)/shard_map/pallas_call | solution.py:220
  92.7 0.0 copy-done.3
  92.7 0.0 copy-start.11
  92.8 1.0 copy-done.11
  93.7 0.0 all-gather.2.cloned.1.call-done.w_ref
  93.8 0.0 copy-done.6
  93.8 0.0 copy-start.1
  93.8 1.6 copy-done.1
  95.3 3.9 %shard_map.103 = bf16[16,256,128]{2,1,0:T(8,128)(2,1)} custom-call(bf16[256,1024]{1,0:T(8,128)(2,1)S(1)} %bitcast.18, bf16[1024,1024]{1,0:T(8,128)(2,1)S(1)} %copy-done.1, bf16[1024,1024]{1,0:T(8,128)(2,1)} %fusion.perm_ref, bf16[16,128,128]{2,1,0:T(8,128)(2,1)S(1)} %bitcast.20), custom_call_target="tpu_custom_call" | custom-call | flops 1073741824 | bytes 6291456 | tf_op jit(solution)/shard_map/pallas_call | solution.py:282
  99.3 4.6 %all-to-all-start.2 = ((bf16[16,256,128]{2,1,0:T(8,128)(2,1)}), bf16[16,256,128]{2,1,0:T(8,128)(2,1)S(1)}, u32[]{:S(2)}, u32[]{:S(2)}) async-start(bf16[16,256,128]{2,1,0:T(8,128)(2,1)} %shard_map.103), calls=%async_computation.2 | async-start | bytes 2097152 | tf_op jit(solution)/shard_map/all_to_all | solution.py:241
  103.9 0.9 fusion.1.perm_ref
  104.8 15.0 %all-to-all-done.2.attg_ref = bf16[16,256,128]{2,1,0:T(8,128)(2,1)S(1)} async-done(((bf16[16,256,128]{2,1,0:T(8,128)(2,1)}), bf16[16,256,128]{2,1,0:T(8,128)(2,1)S(1)}, u32[]{:S(2)}, u32[]{:S(2)}) %all-to-all-start.2) | async-done | bytes 1048608 | tf_op jit(solution)/shard_map/all_to_all | solution.py:241
  119.8 0.0 copy-start.7
  119.9 1.0 copy-done.7
  120.9 1.5 shard_map.104
  122.4 2.8 %collective-permute-start = (bf16[512,1024]{1,0:T(8,128)(2,1)S(1)}, bf16[512,1024]{1,0:T(8,128)(2,1)S(1)}, u32[]{:S(2)}, u32[]{:S(2)}) collective-permute-start(bf16[512,1024]{1,0:T(8,128)(2,1)S(1)} %get-tuple-element.23), channel_id=1, source_target_pairs={{0,1},{1,0},{2,3},{3,2},{4,5},{5,4},{6,7},{7,6},{8,9},{9,8},{10,11... | collective-permute-start | bytes 3145736 | tf_op jit(solution)/shard_map/ppermute | solution.py:290
  125.2 2.3 %collective-permute-done.b_ref = bf16[512,1024]{1,0:T(8,128)(2,1)S(1)} collective-permute-done((bf16[512,1024]{1,0:T(8,128)(2,1)S(1)}, bf16[512,1024]{1,0:T(8,128)(2,1)S(1)}, u32[]{:S(2)}, u32[]{:S(2)}) %collective-permute-start) | collective-permute-done | bytes 1048608 | tf_op jit(solution)/shard_map/ppermute | solution.py:290
  127.5 0.2 shard_map.105
  127.7 0.0 copy-start.4
  127.7 18.0 %all_to_all.30.parts_ref = bf16[8,64,1024]{2,1,0:T(8,128)(2,1)S(1)} all-to-all(bf16[8,64,1024]{2,1,0:T(8,128)(2,1)S(1)} %bitcast.13), channel_id=1, replica_groups={{0,2,4,6,8,10,12,14},{1,3,5,7,9,11,13,15},{16,18,20,22,24,26,28,30},{17..., dimensions={0} | all-to-all | bytes 2097152 | tf_op jit(solution)/shard_map/all_to_all | solution.py:241
  145.7 0.1 shard_map.106
  145.9 0.7 reshape.162
  146.6 4.0 %all-to-all-start.4 = ((bf16[32,2,1024]{2,1,0:T(2,128)(2,1)}), bf16[32,2,1024]{2,1,0:T(2,128)(2,1)S(1)}, u32[]{:S(2)}, u32[]{:S(2)}) async-start(bf16[32,2,1024]{2,1,0:T(2,128)(2,1)} %reshape.162), calls=%async_computation.4 | async-start | bytes 262144 | tf_op jit(solution)/shard_map/all_to_all | solution.py:241
  150.6 0.0 copy-done.4
  150.6 0.0 copy-start.12
  150.6 1.2 copy-done.12
  151.8 12.2 %shard_map.108 = bf16[6144,128]{1,0:T(8,128)(2,1)S(1)} custom-call(s32[32,4]{1,0:T(8,128)S(1)} %copy.11.layout_ref, bf16[6144,128]{1,0:T(8,128)(2,1)S(1)} %bitcast.16, bf16[4096,128]{1,0:T(8,128)(2,1)S(1)} %bitcast.14, bf16[32,128,128]{2,1,0:T(8,128)(2,1)S(1)} %copy-done.12, f32[32,2,128]{2,1,0:T(2,128)S(1)} %get-tuple-element.26.stat_ref), custom_call_target="tpu_custom_call" | custom-call | flops 3221225472 | bytes 6291456 | tf_op jit(solution)/shard_map/pallas_call | solution.py:230
  164.1 0.0 copy-start.5
  164.1 1.1 copy-done.5
  165.2 0.0 copy-start
  165.2 0.0 all-to-all-done.4
  165.2 7.8 %all-to-all-start.5 = ((bf16[16,384,128]{2,1,0:T(8,128)(2,1)}), bf16[16,384,128]{2,1,0:T(8,128)(2,1)}, u32[]{:S(2)}, u32[]{:S(2)}) async-start(bf16[16,384,128]{2,1,0:T(8,128)(2,1)} %bitcast.17), calls=%async_computation.5 | async-start | bytes 3145728 | tf_op jit(solution)/shard_map/all_to_all | solution.py:241
  173.0 0.0 copy-done
  173.0 0.0 copy-start.2
  173.0 1.6 copy-done.2
  174.6 2.1 %shard_map.107 = bf16[256,1024]{1,0:T(8,128)(2,1)} custom-call(bf16[16,256,128]{2,1,0:T(8,128)(2,1)S(1)} %all-to-all-done.2.attg_ref, bf16[1024,1024]{1,0:T(8,128)(2,1)S(1)} %copy-done.2, bf16[1024,1024]{1,0:T(8,128)(2,1)S(1)} %copy-done), custom_call_target="tpu_custom_call" | custom-call | flops 1073741824 | bytes 5242880 | tf_op jit(solution)/shard_map/pallas_call | solution.py:298
  176.7 0.7 convert_reduce_fusion
  177.5 17.2 %all-to-all-done.5.src_ref = bf16[16,384,128]{2,1,0:T(8,128)(2,1)} async-done(((bf16[16,384,128]{2,1,0:T(8,128)(2,1)}), bf16[16,384,128]{2,1,0:T(8,128)(2,1)}, u32[]{:S(2)}, u32[]{:S(2)}) %all-to-all-start.5) | async-done | bytes 1572896 | tf_op jit(solution)/shard_map/all_to_all | solution.py:241
  194.7 3.0 %shard_map.109 = (bf16[256,1024]{1,0:T(8,128)(2,1)}, bf16[256,1024]{1,0:T(8,128)(2,1)}, bf16[256,1024]{1,0:T(8,128)(2,1)}) custom-call(bf16[16,384,128]{2,1,0:T(8,128)(2,1)} %all-to-all-done.5.src_ref), custom_call_target="tpu_custom_call" | custom-call | bytes 3145728 | tf_op jit(solution)/shard_map/pallas_call | solution.py:305
  (2 shorter events, 0.0 us)
Async XLA Ops:
  8.6 33.2 %all-to-all-start = ((bf16[32,2,1024]{2,1,0:T(2,128)(2,1)}), bf16[32,2,1024]{2,1,0:T(2,128)(2,1)S(1)}, u32[]{:S(2)}, u32[]{:S(2)}) async-start(bf16[32,2,1024]{2,1,0:T(2,128)(2,1)} %tile.2), calls=%async_computation | async-start | bytes 262144 | tf_op jit(solution)/shard_map/all_to_all | solution.py:241
  27.1 66.7 %all-gather.2.cloned.1.call-start = ((), (), s32[]{:S(2)}) async-start(), calls=%async_computation.6 | async-start | bytes 2228224 | tf_op jit(solution)/shard_map/all_gather | solution.py:277
  27.1 1.0 copy-start.8
  28.2 1.0 copy-start.9
  29.2 1.0 copy-start.10
  32.1 18.7 %copy-start.13 = (s32[32,4]{0,1:T(4,128)S(1)}, s32[32,4]{0,1:T(4,128)}, u32[]{:S(2)}) copy-start(s32[32,4]{0,1:T(4,128)} %param.11) | copy-start | bytes 1540
  42.6 37.0 %all-to-all-start.1 = ((bf16[16,384,128]{2,1,0:T(8,128)(2,1)}), bf16[16,384,128]{2,1,0:T(8,128)(2,1)S(1)}, u32[]{:S(2)}, u32[]{:S(2)}) async-start(bf16[16,384,128]{2,1,0:T(8,128)(2,1)} %shard_map.101), calls=%async_computation.1 | async-start | bytes 3145728 | tf_op jit(solution)/shard_map/all_to_all | solution.py:241
  79.6 13.2 %copy-start.3 = (bf16[16,384,128]{2,1,0:T(8,128)(2,1)}, bf16[16,384,128]{2,1,0:T(8,128)(2,1)S(1)}, u32[]{:S(2)}) copy-start(bf16[16,384,128]{2,1,0:T(8,128)(2,1)S(1)} %all-to-all-done.1) | copy-start | bytes 4718596
  79.6 14.2 %copy-start.6 = (bf16[1,256,1024]{2,1,0:T(8,128)(2,1)S(1)}, bf16[1,256,1024]{2,1,0:T(8,128)(2,1)}, u32[]{:S(2)}) copy-start(bf16[1,256,1024]{2,1,0:T(8,128)(2,1)} %param.9) | copy-start | bytes 1572868
  92.7 1.0 copy-start.11
  93.8 1.6 copy-start.1
  99.3 20.6 %all-to-all-start.2 = ((bf16[16,256,128]{2,1,0:T(8,128)(2,1)}), bf16[16,256,128]{2,1,0:T(8,128)(2,1)S(1)}, u32[]{:S(2)}, u32[]{:S(2)}) async-start(bf16[16,256,128]{2,1,0:T(8,128)(2,1)} %shard_map.103), calls=%async_computation.2 | async-start | bytes 2097152 | tf_op jit(solution)/shard_map/all_to_all | solution.py:241
  119.8 1.0 copy-start.7
  122.4 5.1 %collective-permute-start = (bf16[512,1024]{1,0:T(8,128)(2,1)S(1)}, bf16[512,1024]{1,0:T(8,128)(2,1)S(1)}, u32[]{:S(2)}, u32[]{:S(2)}) collective-permute-start(bf16[512,1024]{1,0:T(8,128)(2,1)S(1)} %get-tuple-element.23), channel_id=1, source_target_pairs={{0,1},{1,0},{2,3},{3,2},{4,5},{5,4},{6,7},{7,6},{8,9},{9,8},{10,11... | collective-permute-start | bytes 3145736 | tf_op jit(solution)/shard_map/ppermute | solution.py:290
  127.7 22.9 %copy-start.4 = (bf16[16,384,128]{2,1,0:T(8,128)(2,1)S(1)}, bf16[16,384,128]{2,1,0:T(8,128)(2,1)}, u32[]{:S(2)}) copy-start(bf16[16,384,128]{2,1,0:T(8,128)(2,1)} %copy-done.3) | copy-start | bytes 4718596
  146.6 18.7 %all-to-all-start.4 = ((bf16[32,2,1024]{2,1,0:T(2,128)(2,1)}), bf16[32,2,1024]{2,1,0:T(2,128)(2,1)S(1)}, u32[]{:S(2)}, u32[]{:S(2)}) async-start(bf16[32,2,1024]{2,1,0:T(2,128)(2,1)} %reshape.162), calls=%async_computation.4 | async-start | bytes 262144 | tf_op jit(solution)/shard_map/all_to_all | solution.py:241
  150.6 1.2 copy-start.12
  164.1 1.1 copy-start.5
  165.2 7.8 %copy-start = (bf16[1024,1024]{1,0:T(8,128)(2,1)S(1)}, bf16[1024,1024]{1,0:T(8,128)(2,1)}, u32[]{:S(2)}) copy-start(bf16[1024,1024]{1,0:T(8,128)(2,1)} %fusion.perm_ref) | copy-start | bytes 6291460
  165.2 29.5 %all-to-all-start.5 = ((bf16[16,384,128]{2,1,0:T(8,128)(2,1)}), bf16[16,384,128]{2,1,0:T(8,128)(2,1)}, u32[]{:S(2)}, u32[]{:S(2)}) async-start(bf16[16,384,128]{2,1,0:T(8,128)(2,1)} %bitcast.17), calls=%async_computation.5 | async-start | bytes 3145728 | tf_op jit(solution)/shard_map/all_to_all | solution.py:241
  173.0 1.6 copy-start.2
Sparse Core Ops, SparseCore 0:
  42.7 46.9 all-gather.1

commit v3 on v2

--- a/solution.py
+++ b/solution.py
@@ -55,8 +55,7 @@
             out_ref[2 * pair + 1, rows] = odd.astype(BF)
 
 
-def grad_kernel(og_ref, w_ref, perm_ref, att_ref, out_ref, tmp_ref):
-    out_ref[:, :B] = att_ref[...]
+def grad_kernel(og_ref, w_ref, perm_ref, out_ref, tmp_ref):
     for quad in range(H // 4):
         rows = slice(quad * 4 * E, (quad + 1) * 4 * E)
         g = lax.dot_general(og_ref[...], w_ref[rows, :], NT, preferred_element_type=F32)
@@ -67,8 +66,8 @@
         for i in range(2):
             part = g[:, i * 2 * E:(i + 1) * 2 * E]
             even, odd = interleave(part[:B], part[B:])
-            out_ref[4 * quad + 2 * i, B:] = even.astype(BF)
-            out_ref[4 * quad + 2 * i + 1, B:] = odd.astype(BF)
+            out_ref[4 * quad + 2 * i] = even.astype(BF)
+            out_ref[4 * quad + 2 * i + 1] = odd.astype(BF)
 
 
 def forward_kernel(unroll, layout_ref, qkv_ref, att_ref, stat_ref, kvt_ref):
@@ -105,7 +104,7 @@
     lax.fori_loop(0, blocks // 2, per_pair, 0, unroll=unroll)
 
 
-def backward_kernel(unroll, layout_ref, qkv_ref, attg_ref, kvt_ref, stat_ref, out_ref, acc_ref):
+def backward_kernel(unroll, layout_ref, qkv_ref, g_ref, kvt_ref, stat_ref, out_ref, acc_ref):
     blocks = layout_ref.shape[0]
     scale = 1.0 / E**0.5
     log2e = 1.4426950408889634
@@ -114,7 +113,7 @@
     def per_pair(s, carry):
         at = pl.multiple_of(s * 3 * B, B)
         qt = qkv_ref[pl.ds(at, B), :].T
-        gt = attg_ref[pl.ds(pl.multiple_of(s * 2 * B + B, B), B), :].T
+        gt = g_ref[pl.ds(pl.multiple_of(s * B, B), B), :].T
         zero = jnp.zeros((E, B), BF)
         dq_t = []
         for p in range(2):
@@ -169,8 +168,8 @@
         ).astype(BF)
 
 
-def partial_kernel(attg_ref, og_ref, perm_ref, own_ref, other_ref, tmp_ref, att_ref):
-    unpack_tokens(attg_ref, tmp_ref)
+def partial_kernel(att_in_ref, og_ref, perm_ref, own_ref, other_ref, tmp_ref, att_ref):
+    unpack_tokens(att_in_ref, tmp_ref)
     reorder(tmp_ref, perm_ref, att_ref)
     half = own_ref.shape[0]
     for ref, base in ((other_ref, half), (own_ref, 0)):
@@ -181,8 +180,8 @@
             ).astype(BF)
 
 
-def mixed_kernel(attg_ref, w_ref, perm_ref, mixed_ref, tmp_ref, att_ref):
-    unpack_tokens(attg_ref, tmp_ref)
+def mixed_kernel(att_in_ref, w_ref, perm_ref, mixed_ref, tmp_ref, att_ref):
+    unpack_tokens(att_in_ref, tmp_ref)
     reorder(tmp_ref, perm_ref, att_ref)
     for i in range(H // 4):
         cols = slice(i * 4 * E, (i + 1) * 4 * E)
@@ -226,7 +225,7 @@
     )(layout, qkv)
 
 
-def backward(layout, qkv, attg, kvt, stats):
+def backward(layout, qkv, g, kvt, stats):
     return call(
         functools.partial(backward_kernel, 4),
         [(qkv.shape, BF)],
@@ -234,7 +233,7 @@
         [pltpu.VMEM(qkv.shape, F32)],
         flops=4 * qkv.shape[0] * 512 * 128 * 2,
         moved=6 * 2**20,
-    )(layout, qkv, attg, kvt, stats)[0]
+    )(layout, qkv, g, kvt, stats)[0]
 
 
 def exchange(x, axis, groups=None):
@@ -272,33 +271,36 @@
     slabs = call(pack_kernel, [((H, 3 * B, 2 * E), BF)], [VM] * 3, moved=3 * 2**20)(
         queries[0], keys[0], values[0]
     )[0]
+    qkv = exchange(slabs, "seq").reshape(-1, 2 * E)
+    out_weight, qkv = lax.optimization_barrier((out_weight, qkv))
     column = exchange(jnp.tile(out_weight[None], (dp, 1, 1)), "dp").reshape(-1, width)
-    column, slabs = lax.optimization_barrier((column, slabs))
+    att, stats, kvt = forward(layout, qkv)
+    att, column = lax.optimization_barrier((att, column))
     weight = lax.all_gather(column, "seq", axis=0, tiled=True)
-    qkv = exchange(slabs, "seq").reshape(-1, 2 * E)
-    att, stats, kvt = forward(layout, qkv)
+    att = exchange(att.reshape(H, B, 2 * E), "seq")
     gathered = one_hot(width, gathered_order(width, dp, seq))
     reduced = one_hot(width, reduced_order(width, dp, seq))
-    attg = call(
-        grad_kernel, [((H, 2 * B, 2 * E), BF)], [VM] * 4, scratch, flops=2 * square, moved=6 * 2**20
-    )(grad, weight, gathered, att.reshape(H, B, 2 * E))[0]
-    attg = exchange(attg, "seq")
     half = (width // 2, width)
     own, other = call(
         partial_kernel, [(half, BF)] * 2, [VM] * 3, scratch * 2, flops=2 * square, moved=6 * 2**20
-    )(attg, grad, reduced)
+    )(att, grad, reduced)
     other = lax.ppermute(other, "seq", [(i, i ^ 1) for i in range(seq)])
     own = call(add_kernel, [(half, BF)], [VM] * 2, moved=3 * 2**20)(own, other)[0]
     groups = [list(range(c, seq, 2)) for c in range(2)]
     terms = exchange(own.reshape(seq // 2, -1, width), "seq", groups)
     total = add_up(terms, BF).reshape(dp, -1, width)
-    attg, total = lax.optimization_barrier((attg, total))
+    g = call(
+        grad_kernel, [((H, B, 2 * E), BF)], [VM] * 3, scratch, flops=2 * square, moved=5 * 2**20
+    )(grad, weight, gathered)[0]
+    g, terms = lax.optimization_barrier((g, terms))
+    g = exchange(g, "seq").reshape(-1, 2 * E)
+    g, total = lax.optimization_barrier((g, total))
     total = exchange(total, "dp")
-    slabs = backward(layout, qkv, attg.reshape(-1, 2 * E), kvt, stats)
+    slabs = backward(layout, qkv, g, kvt, stats)
     mixed = call(
         mixed_kernel, [((tokens, width), BF)], [VM] * 3, scratch * 2,
         flops=2 * square, moved=5 * 2**20,
-    )(attg, weight, gathered)[0]
+    )(att, weight, gathered)[0]
     slabs, total = lax.optimization_barrier((slabs, total))
     weight_grad = total.astype(F32).sum(axis=0)
     slabs = exchange(slabs.reshape(H, 3 * B, 2 * E), "seq")

time: 205 us -> 212 us (1.034)
  waiting for transfers between devices: 70.7 us -> 57.1 us
  blocking collectives: 18 us -> 30.4 us
  starting transfers between devices: 46 us -> 55.2 us
    all_to_all x5 -> x6, waiting for transfers between devices: 68.4 us -> 35.3 us  [exchange(): lax.all_to_all(x, axis, split_axis=0, concat_axis=0, tiled=True, axis_ind...]
    all_gather x1, waiting for transfers between devices: 0.01 us -> 19.6 us  [body(): weight = lax.all_gather(column, 'seq', axis=0, tiled=True)]
    all_to_all x1, blocking collectives: 18 us -> 30.4 us  [exchange(): lax.all_to_all(x, axis, split_axis=0, concat_axis=0, tiled=True, axis_ind...]
    all_to_all x5 -> x6, starting transfers between devices: 43.2 us -> 52.1 us  [exchange(): lax.all_to_all(x, axis, split_axis=0, concat_axis=0, tiled=True, axis_ind...]
    pallas_call x1, Pallas kernels: 3.94 us -> 1.36 us  [body(): call(grad_kernel, [((H, B, 2 * E), BF)], [VM] * 3, scratch, flops=2 * squ...]
    unnamed x29 -> x35, local copies, waits for them, and re-layouts: 10.8 us -> 13 us
  transfers between devices with their start and end apart: 7 -> 8, of which waited for: 5 -> 5; matrix products, arithmetic and copies ran while one was open for 2% -> 2% of each run, Pallas kernels for 14% -> 16%
where the time goes in v3:
time: 212 us; the launch traced here: 211 us
  waiting for transfers between devices  57.1 us (27%)
  starting transfers between devices  55.2 us (26%)
  Pallas kernels  36.5 us (17%)
  blocking collectives  30.4 us (14%)
  local copies, waits for them, and re-layouts  15.2 us (7%)
  between operations  14.2 us (7%)
  other arithmetic  2.52 us (1%)
    all_to_all x6, starting transfers between devices, exchange(): lax.all_to_all(x, axis, split_axis=0, concat_axis=0, tiled=True, axis_ind...  52.1 us
    all_to_all x6, waiting for transfers between devices, exchange(): lax.all_to_all(x, axis, split_axis=0, concat_axis=0, tiled=True, axis_ind...  35.3 us
    all_to_all x1, blocking collectives, exchange(): lax.all_to_all(x, axis, split_axis=0, concat_axis=0, tiled=True, axis_ind...  30.4 us
    all_gather x1, waiting for transfers between devices, body(): weight = lax.all_gather(column, 'seq', axis=0, tiled=True)  19.6 us
    pallas_call x1, Pallas kernels, forward(): call(functools.partial(forward_kernel, 4), [((rows // 3, 2 * E), BF), ((b...  14 us
    unnamed x35, local copies, waits for them, and re-layouts  13 us
    pallas_call x1, Pallas kernels, backward(): call(functools.partial(backward_kernel, 4), [(qkv.shape, BF)], [SM] + [VM...  12.5 us
  transfers between devices with their start and end apart: 8, of which 5 were waited for; matrix products, arithmetic and copies ran while one was open for 2% of the time, Pallas kernels for 16%

profile of v3, /device:TPU:1, one launch (start us, length us, event | category | flops | bytes accessed | tf_op | source)
XLA Modules:
  0.0 211.2 jit_solution(12827941245666887119)
XLA Ops:
  7.2 0.0 copy-start.10
  7.2 1.0 copy-done.10
  8.2 0.0 copy-start.11
  8.2 1.0 copy-done.11
  9.3 0.0 copy-start.12
  9.3 1.0 copy-done.12
  10.3 0.7 shard_map.101
  11.0 0.0 copy-start.15
  11.0 0.0 copy-start.16
  11.0 30.4 %all_to_all.35 = bf16[16,384,128]{2,1,0:T(8,128)(2,1)S(1)} all-to-all(bf16[16,384,128]{2,1,0:T(8,128)(2,1)S(1)} %shard_map.101), channel_id=1, replica_groups=mesh['dp'=32,'seq'=16] {'seq'}, dimensions={0} | all-to-all | bytes 3145728 | tf_op jit(solution)/shard_map/all_to_all | solution.py:240
  41.5 0.0 copy-start.5
  41.5 0.0 copy-done.15
  41.5 0.8 tile.2
  42.3 14.7 %all-to-all-start.1 = ((bf16[32,2,1024]{2,1,0:T(2,128)(2,1)}), bf16[32,2,1024]{2,1,0:T(2,128)(2,1)S(1)}, u32[]{:S(2)}, u32[]{:S(2)}) async-start(bf16[32,2,1024]{2,1,0:T(2,128)(2,1)} %tile.2), calls=%async_computation.1 | async-start | bytes 262144 | tf_op jit(solution)/shard_map/all_to_all | solution.py:240
  57.0 0.0 all-gather.2.cloned.1.call-start
  57.0 0.0 copy-done.16
  57.0 0.1 copy.11.layout_ref
  57.1 14.0 %shard_map.102 = (bf16[2048,128]{1,0:T(8,128)(2,1)}, f32[32,2,128]{2,1,0:T(2,128)S(1)}, bf16[32,128,128]{2,1,0:T(8,128)(2,1)S(1)}) custom-call(s32[32,4]{1,0:T(8,128)S(1)} %copy.11.layout_ref, bf16[6144,128]{1,0:T(8,128)(2,1)S(1)} %bitcast.13), custom_call_target="tpu_custom_call" | custom-call | flops 1610612736 | bytes 4194304 | tf_op jit(solution)/shard_map/pallas_call | solution.py:219
  71.1 0.0 copy-done.5
  71.1 0.0 copy-start.13
  71.1 1.0 copy-done.13
  72.0 0.0 copy-start.8
  72.0 0.0 all-to-all-done.1
  72.0 0.7 reshape.159
  72.7 0.0 all-gather.2.cloned.1.call-update
  72.8 6.5 %all-to-all-start.2 = ((bf16[16,128,128]{2,1,0:T(8,128)(2,1)}), bf16[16,128,128]{2,1,0:T(8,128)(2,1)S(1)}, u32[]{:S(2)}, u32[]{:S(2)}) async-start(bf16[16,128,128]{2,1,0:T(8,128)(2,1)} %bitcast.4), calls=%async_computation.2 | async-start | bytes 1048576 | tf_op jit(solution)/shard_map/all_to_all | solution.py:240
  79.3 0.9 fusion.1.perm_ref
  80.2 9.0 %all-to-all-done.2.att_in_ref = bf16[16,128,128]{2,1,0:T(8,128)(2,1)S(1)} async-done(((bf16[16,128,128]{2,1,0:T(8,128)(2,1)}), bf16[16,128,128]{2,1,0:T(8,128)(2,1)S(1)}, u32[]{:S(2)}, u32[]{:S(2)}) %all-to-all-start.2) | async-done | bytes 524320 | tf_op jit(solution)/shard_map/all_to_all | solution.py:240
  89.2 0.0 copy-start.2
  89.2 0.0 copy-done.8
  89.2 1.5 shard_map.105
  90.7 3.1 %collective-permute-start = (bf16[512,1024]{1,0:T(8,128)(2,1)S(1)}, bf16[512,1024]{1,0:T(8,128)(2,1)S(1)}, u32[]{:S(2)}, u32[]{:S(2)}) collective-permute-start(bf16[512,1024]{1,0:T(8,128)(2,1)S(1)} %get-tuple-element.28), channel_id=1, source_target_pairs={{0,1},{1,0},{2,3},{3,2},{4,5},{5,4},{6,7},{7,6},{8,9},{9,8},{10,11... | collective-permute-start | bytes 3145736 | tf_op jit(solution)/shard_map/ppermute | solution.py:287
  93.8 2.3 %collective-permute-done.b_ref = bf16[512,1024]{1,0:T(8,128)(2,1)S(1)} collective-permute-done((bf16[512,1024]{1,0:T(8,128)(2,1)S(1)}, bf16[512,1024]{1,0:T(8,128)(2,1)S(1)}, u32[]{:S(2)}, u32[]{:S(2)}) %collective-permute-start) | collective-permute-done | bytes 1048608 | tf_op jit(solution)/shard_map/ppermute | solution.py:287
  96.0 1.2 shard_map.106
  97.3 0.0 copy-done.2
  97.3 3.6 %all-to-all-start.3 = ((bf16[8,64,1024]{2,1,0:T(8,128)(2,1)}), bf16[8,64,1024]{2,1,0:T(8,128)(2,1)S(1)}, u32[]{:S(2)}, u32[]{:S(2)}) async-start(bf16[8,64,1024]{2,1,0:T(8,128)(2,1)} %bitcast.7), calls=%async_computation.3 | async-start | bytes 2097152 | tf_op jit(solution)/shard_map/all_to_all | solution.py:240
  100.9 0.9 fusion.perm_ref
  101.8 19.6 %all-gather.2.cloned.1.call-done.w_ref = bf16[1024,1024]{1,0:T(8,128)(2,1)} async-done(((bf16[64,1024]{1,0:T(8,128)(2,1)}), bf16[1024,1024]{1,0:T(8,128)(2,1)}) %all-gather.2.cloned.1.call-update) | async-done | bytes 2097168 | tf_op jit(solution)/shard_map/all_gather | solution.py:279
  121.3 1.6 copy-done
  122.9 1.0 copy-done.9
  123.9 1.4 shard_map.104
  125.3 0.0 copy-start.4
  125.3 0.8 copy-done.4
  126.1 0.0 all-to-all-done.3.parts_ref
  126.1 4.4 %all-to-all-start.4 = ((bf16[16,128,128]{2,1,0:T(8,128)(2,1)}), bf16[16,128,128]{2,1,0:T(8,128)(2,1)}, u32[]{:S(2)}, u32[]{:S(2)}) async-start(bf16[16,128,128]{2,1,0:T(8,128)(2,1)} %copy-done.4), calls=%async_computation.4 | async-start | bytes 1048576 | tf_op jit(solution)/shard_map/all_to_all | solution.py:240
  130.5 0.1 shard_map.107
  130.6 0.7 reshape.163
  131.3 9.1 %all-to-all-done.4 = bf16[16,128,128]{2,1,0:T(8,128)(2,1)} async-done(((bf16[16,128,128]{2,1,0:T(8,128)(2,1)}), bf16[16,128,128]{2,1,0:T(8,128)(2,1)}, u32[]{:S(2)}, u32[]{:S(2)}) %all-to-all-start.4) | async-done | bytes 524320 | tf_op jit(solution)/shard_map/all_to_all | solution.py:240
  140.4 17.1 %all-to-all-start.5 = ((bf16[32,2,1024]{2,1,0:T(2,128)(2,1)}), bf16[32,2,1024]{2,1,0:T(2,128)(2,1)S(1)}, u32[]{:S(2)}, u32[]{:S(2)}) async-start(bf16[32,2,1024]{2,1,0:T(2,128)(2,1)} %reshape.163), calls=%async_computation.5 | async-start | bytes 262144 | tf_op jit(solution)/shard_map/all_to_all | solution.py:240
  157.5 0.0 copy-start.6
  157.5 1.4 copy-done.6
  158.9 1.2 copy-done.14
  160.1 12.5 %shard_map.108 = bf16[6144,128]{1,0:T(8,128)(2,1)S(1)} custom-call(s32[32,4]{1,0:T(8,128)S(1)} %copy.11.layout_ref, bf16[6144,128]{1,0:T(8,128)(2,1)S(1)} %bitcast.14, bf16[2048,128]{1,0:T(8,128)(2,1)} %bitcast.8.g_ref, bf16[32,128,128]{2,1,0:T(8,128)(2,1)S(1)} %copy-done.14, f32[32,2,128]{2,1,0:T(2,128)S(1)} %get-tuple-element.32.stat_ref), custom_call_target="tpu_custom_call" | custom-call | flops 3221225472 | bytes 6291456 | tf_op jit(solution)/shard_map/pallas_call | solution.py:229
  172.6 0.0 copy-start.7
  172.6 1.2 copy-done.7
  173.8 0.0 all-to-all-done.5
  173.8 5.9 %all-to-all-start.6 = ((bf16[16,384,128]{2,1,0:T(8,128)(2,1)}), bf16[16,384,128]{2,1,0:T(8,128)(2,1)}, u32[]{:S(2)}, u32[]{:S(2)}) async-start(bf16[16,384,128]{2,1,0:T(8,128)(2,1)} %bitcast.15), calls=%async_computation.6 | async-start | bytes 3145728 | tf_op jit(solution)/shard_map/all_to_all | solution.py:240
  179.7 0.0 copy-done.3
  179.7 0.0 copy-start.1
  179.7 1.6 copy-done.1
  181.3 2.1 %shard_map.103 = bf16[256,1024]{1,0:T(8,128)(2,1)} custom-call(bf16[16,128,128]{2,1,0:T(8,128)(2,1)S(1)} %copy-done.3, bf16[1024,1024]{1,0:T(8,128)(2,1)S(1)} %copy-done.1, bf16[1024,1024]{1,0:T(8,128)(2,1)S(1)} %fusion.perm_ref), custom_call_target="tpu_custom_call" | custom-call | flops 1073741824 | bytes 5242880 | tf_op jit(solution)/shard_map/pallas_call | solution.py:300
  183.4 0.7 convert_reduce_fusion
  184.1 17.2 %all-to-all-done.6.src_ref = bf16[16,384,128]{2,1,0:T(8,128)(2,1)} async-done(((bf16[16,384,128]{2,1,0:T(8,128)(2,1)}), bf16[16,384,128]{2,1,0:T(8,128)(2,1)}, u32[]{:S(2)}, u32[]{:S(2)}) %all-to-all-start.6) | async-done | bytes 1572896 | tf_op jit(solution)/shard_map/all_to_all | solution.py:240
  201.4 3.0 %shard_map.109 = (bf16[256,1024]{1,0:T(8,128)(2,1)}, bf16[256,1024]{1,0:T(8,128)(2,1)}, bf16[256,1024]{1,0:T(8,128)(2,1)}) custom-call(bf16[16,384,128]{2,1,0:T(8,128)(2,1)} %all-to-all-done.6.src_ref), custom_call_target="tpu_custom_call" | custom-call | bytes 3145728 | tf_op jit(solution)/shard_map/pallas_call | solution.py:307
  (6 shorter events, 0.0 us)
Async XLA Ops:
  7.2 1.0 copy-start.10
  8.2 1.0 copy-start.11
  9.3 1.0 copy-start.12
  11.0 30.5 %copy-start.15 = (bf16[2,1024]{1,0:T(2,128)(2,1)S(1)}, bf16[2,1024]{1,0:T(2,128)(2,1)}, u32[]{:S(2)}) copy-start(bf16[2,1024]{1,0:T(2,128)(2,1)} %param.10) | copy-start | bytes 12292
  11.0 46.0 %copy-start.16 = (s32[32,4]{0,1:T(4,128)S(1)}, s32[32,4]{0,1:T(4,128)}, u32[]{:S(2)}) copy-start(s32[32,4]{0,1:T(4,128)} %param.11) | copy-start | bytes 1540
  41.5 29.6 %copy-start.5 = (bf16[16,384,128]{2,1,0:T(8,128)(2,1)}, bf16[16,384,128]{2,1,0:T(8,128)(2,1)S(1)}, u32[]{:S(2)}) copy-start(bf16[16,384,128]{2,1,0:T(8,128)(2,1)S(1)} %all_to_all.35) | copy-start | bytes 4718596
  42.3 29.7 %all-to-all-start.1 = ((bf16[32,2,1024]{2,1,0:T(2,128)(2,1)}), bf16[32,2,1024]{2,1,0:T(2,128)(2,1)S(1)}, u32[]{:S(2)}, u32[]{:S(2)}) async-start(bf16[32,2,1024]{2,1,0:T(2,128)(2,1)} %tile.2), calls=%async_computation.1 | async-start | bytes 262144 | tf_op jit(solution)/shard_map/all_to_all | solution.py:240
  57.0 64.3 %all-gather.2.cloned.1.call-start = ((), (), s32[]{:S(2)}) async-start(), calls=%async_computation.7 | async-start | bytes 2228224 | tf_op jit(solution)/shard_map/all_gather | solution.py:279
  71.1 1.0 copy-start.13
  72.0 17.1 %copy-start.8 = (bf16[1,256,1024]{2,1,0:T(8,128)(2,1)S(1)}, bf16[1,256,1024]{2,1,0:T(8,128)(2,1)}, u32[]{:S(2)}) copy-start(bf16[1,256,1024]{2,1,0:T(8,128)(2,1)} %param.9) | copy-start | bytes 1572868
  72.8 16.4 %all-to-all-start.2 = ((bf16[16,128,128]{2,1,0:T(8,128)(2,1)}), bf16[16,128,128]{2,1,0:T(8,128)(2,1)S(1)}, u32[]{:S(2)}, u32[]{:S(2)}) async-start(bf16[16,128,128]{2,1,0:T(8,128)(2,1)} %bitcast.4), calls=%async_computation.2 | async-start | bytes 1048576 | tf_op jit(solution)/shard_map/all_to_all | solution.py:240
  89.2 8.1 %copy-start.2 = (bf16[16,128,128]{2,1,0:T(8,128)(2,1)}, bf16[16,128,128]{2,1,0:T(8,128)(2,1)S(1)}, u32[]{:S(2)}) copy-start(bf16[16,128,128]{2,1,0:T(8,128)(2,1)S(1)} %all-to-all-done.2.att_in_ref) | copy-start | bytes 1572868
  90.7 5.4 %collective-permute-start = (bf16[512,1024]{1,0:T(8,128)(2,1)S(1)}, bf16[512,1024]{1,0:T(8,128)(2,1)S(1)}, u32[]{:S(2)}, u32[]{:S(2)}) collective-permute-start(bf16[512,1024]{1,0:T(8,128)(2,1)S(1)} %get-tuple-element.28), channel_id=1, source_target_pairs={{0,1},{1,0},{2,3},{3,2},{4,5},{5,4},{6,7},{7,6},{8,9},{9,8},{10,11... | collective-permute-start | bytes 3145736 | tf_op jit(solution)/shard_map/ppermute | solution.py:287
  97.3 28.8 %all-to-all-start.3 = ((bf16[8,64,1024]{2,1,0:T(8,128)(2,1)}), bf16[8,64,1024]{2,1,0:T(8,128)(2,1)S(1)}, u32[]{:S(2)}, u32[]{:S(2)}) async-start(bf16[8,64,1024]{2,1,0:T(8,128)(2,1)} %bitcast.7), calls=%async_computation.3 | async-start | bytes 2097152 | tf_op jit(solution)/shard_map/all_to_all | solution.py:240
  121.3 1.6 copy-start
  122.9 1.0 copy-start.9
  125.3 0.8 copy-start.4
  126.1 14.3 %all-to-all-start.4 = ((bf16[16,128,128]{2,1,0:T(8,128)(2,1)}), bf16[16,128,128]{2,1,0:T(8,128)(2,1)}, u32[]{:S(2)}, u32[]{:S(2)}) async-start(bf16[16,128,128]{2,1,0:T(8,128)(2,1)} %copy-done.4), calls=%async_computation.4 | async-start | bytes 1048576 | tf_op jit(solution)/shard_map/all_to_all | solution.py:240
  140.4 33.4 %all-to-all-start.5 = ((bf16[32,2,1024]{2,1,0:T(2,128)(2,1)}), bf16[32,2,1024]{2,1,0:T(2,128)(2,1)S(1)}, u32[]{:S(2)}, u32[]{:S(2)}) async-start(bf16[32,2,1024]{2,1,0:T(2,128)(2,1)} %reshape.163), calls=%async_computation.5 | async-start | bytes 262144 | tf_op jit(solution)/shard_map/all_to_all | solution.py:240
  157.5 1.4 copy-start.6
  158.9 1.2 copy-start.14
  172.6 1.2 copy-start.7
  173.8 5.9 %copy-start.3 = (bf16[16,128,128]{2,1,0:T(8,128)(2,1)S(1)}, bf16[16,128,128]{2,1,0:T(8,128)(2,1)}, u32[]{:S(2)}) copy-start(bf16[16,128,128]{2,1,0:T(8,128)(2,1)} %copy-done.2) | copy-start | bytes 1572868
  173.8 27.6 %all-to-all-start.6 = ((bf16[16,384,128]{2,1,0:T(8,128)(2,1)}), bf16[16,384,128]{2,1,0:T(8,128)(2,1)}, u32[]{:S(2)}, u32[]{:S(2)}) async-start(bf16[16,384,128]{2,1,0:T(8,128)(2,1)} %bitcast.15), calls=%async_computation.6 | async-start | bytes 3145728 | tf_op jit(solution)/shard_map/all_to_all | solution.py:240
  179.7 1.6 copy-start.1
Sparse Core Ops, SparseCore 0:
  72.9 48.3 all-gather.1

commit v4 on v2

--- a/solution.py
+++ b/solution.py
@@ -55,20 +55,20 @@
             out_ref[2 * pair + 1, rows] = odd.astype(BF)
 
 
-def grad_kernel(og_ref, w_ref, perm_ref, att_ref, out_ref, tmp_ref):
-    out_ref[:, :B] = att_ref[...]
-    for quad in range(H // 4):
-        rows = slice(quad * 4 * E, (quad + 1) * 4 * E)
-        g = lax.dot_general(og_ref[...], w_ref[rows, :], NT, preferred_element_type=F32)
-        tmp_ref[:, rows] = g.astype(BF)
+def grad_kernel(og_ref, w_own_ref, w_other_ref, perm_ref, out_ref, tmp_ref):
+    half = w_own_ref.shape[0]
+    for i, ref in enumerate((w_own_ref, w_other_ref)):
+        for at in range(0, half, 4 * E):
+            g = lax.dot_general(og_ref[...], ref[at:at + 4 * E], NT, preferred_element_type=F32)
+            tmp_ref[:, i * half + at:i * half + at + 4 * E] = g.astype(BF)
     for quad in range(H // 4):
         rows = slice(quad * 4 * E, (quad + 1) * 4 * E)
         g = lax.dot_general(tmp_ref[...], perm_ref[rows, :], NT, preferred_element_type=F32)
         for i in range(2):
             part = g[:, i * 2 * E:(i + 1) * 2 * E]
             even, odd = interleave(part[:B], part[B:])
-            out_ref[4 * quad + 2 * i, B:] = even.astype(BF)
-            out_ref[4 * quad + 2 * i + 1, B:] = odd.astype(BF)
+            out_ref[4 * quad + 2 * i] = even.astype(BF)
+            out_ref[4 * quad + 2 * i + 1] = odd.astype(BF)
 
 
 def forward_kernel(unroll, layout_ref, qkv_ref, att_ref, stat_ref, kvt_ref):
@@ -169,7 +169,7 @@
         ).astype(BF)
 
 
-def partial_kernel(attg_ref, og_ref, perm_ref, own_ref, other_ref, tmp_ref, att_ref):
+def partial_kernel(attg_ref, og_ref, perm_ref, own_ref, other_ref, att_ref, tmp_ref):
     unpack_tokens(attg_ref, tmp_ref)
     reorder(tmp_ref, perm_ref, att_ref)
     half = own_ref.shape[0]
@@ -181,14 +181,17 @@
             ).astype(BF)
 
 
-def mixed_kernel(attg_ref, w_ref, perm_ref, mixed_ref, tmp_ref, att_ref):
-    unpack_tokens(attg_ref, tmp_ref)
-    reorder(tmp_ref, perm_ref, att_ref)
+def mixed_kernel(att_ref, w_own_ref, w_other_ref, mixed_ref):
+    half = w_own_ref.shape[0]
     for i in range(H // 4):
         cols = slice(i * 4 * E, (i + 1) * 4 * E)
-        mixed_ref[:, cols] = lax.dot_general(
-            att_ref[...], w_ref[:, cols], NN, preferred_element_type=F32
-        ).astype(BF)
+        total = lax.dot_general(
+            att_ref[:, :half], w_own_ref[:, cols], NN, preferred_element_type=F32
+        )
+        total += lax.dot_general(
+            att_ref[:, half:], w_other_ref[:, cols], NN, preferred_element_type=F32
+        )
+        mixed_ref[:, cols] = total.astype(BF)
 
 
 def add_kernel(a_ref, b_ref, out_ref):
@@ -248,13 +251,6 @@
     return (feature == rows[None, :]).astype(BF)
 
 
-def gathered_order(width, dp, seq):
-    each = width // (dp * seq)
-    place = jnp.arange(width)
-    owner = (place % (dp * each) // each) * seq + place // (dp * each)
-    return owner * each + place % each
-
-
 def reduced_order(width, dp, seq):
     each = width // (dp * seq)
     place = jnp.arange(width)
@@ -272,33 +268,37 @@
     slabs = call(pack_kernel, [((H, 3 * B, 2 * E), BF)], [VM] * 3, moved=3 * 2**20)(
         queries[0], keys[0], values[0]
     )[0]
+    perm = one_hot(width, reduced_order(width, dp, seq))
+    groups = [list(range(c, seq, 2)) for c in range(2)]
+    swap = [(i, i ^ 1) for i in range(seq)]
     column = exchange(jnp.tile(out_weight[None], (dp, 1, 1)), "dp").reshape(-1, width)
-    column, slabs = lax.optimization_barrier((column, slabs))
-    weight = lax.all_gather(column, "seq", axis=0, tiled=True)
+    column, slabs, perm = lax.optimization_barrier((column, slabs, perm))
+    w_own = exchange(jnp.tile(column[None], (seq // 2, 1, 1)), "seq", groups).reshape(-1, width)
+    w_own, slabs = lax.optimization_barrier((w_own, slabs))
     qkv = exchange(slabs, "seq").reshape(-1, 2 * E)
+    w_other = lax.ppermute(w_own, "seq", swap)
+    g = call(
+        grad_kernel, [((H, B, 2 * E), BF)], [VM] * 4, scratch, flops=2 * square, moved=6 * 2**20
+    )(grad, w_own, w_other, perm)[0]
+    g, qkv = lax.optimization_barrier((g, qkv))
     att, stats, kvt = forward(layout, qkv)
-    gathered = one_hot(width, gathered_order(width, dp, seq))
-    reduced = one_hot(width, reduced_order(width, dp, seq))
-    attg = call(
-        grad_kernel, [((H, 2 * B, 2 * E), BF)], [VM] * 4, scratch, flops=2 * square, moved=6 * 2**20
-    )(grad, weight, gathered, att.reshape(H, B, 2 * E))[0]
+    attg = jnp.concatenate([att.reshape(H, B, 2 * E), g], axis=1)
     attg = exchange(attg, "seq")
     half = (width // 2, width)
-    own, other = call(
-        partial_kernel, [(half, BF)] * 2, [VM] * 3, scratch * 2, flops=2 * square, moved=6 * 2**20
-    )(attg, grad, reduced)
-    other = lax.ppermute(other, "seq", [(i, i ^ 1) for i in range(seq)])
+    own, other, att = call(
+        partial_kernel, [(half, BF)] * 2 + [((tokens, width), BF)], [VM] * 3, scratch,
+        flops=2 * square, moved=6 * 2**20,
+    )(attg, grad, perm)
+    other = lax.ppermute(other, "seq", swap)
     own = call(add_kernel, [(half, BF)], [VM] * 2, moved=3 * 2**20)(own, other)[0]
-    groups = [list(range(c, seq, 2)) for c in range(2)]
     terms = exchange(own.reshape(seq // 2, -1, width), "seq", groups)
     total = add_up(terms, BF).reshape(dp, -1, width)
     attg, total = lax.optimization_barrier((attg, total))
     total = exchange(total, "dp")
     slabs = backward(layout, qkv, attg.reshape(-1, 2 * E), kvt, stats)
     mixed = call(
-        mixed_kernel, [((tokens, width), BF)], [VM] * 3, scratch * 2,
-        flops=2 * square, moved=5 * 2**20,
-    )(attg, weight, gathered)[0]
+        mixed_kernel, [((tokens, width), BF)], [VM] * 3, flops=square, moved=3 * 2**20
+    )(att, w_own, w_other)[0]
     slabs, total = lax.optimization_barrier((slabs, total))
     weight_grad = total.astype(F32).sum(axis=0)
     slabs = exchange(slabs.reshape(H, 3 * B, 2 * E), "seq")

time: 205 us -> 196 us (0.956)
  blocking collectives: 18 us -> 52.5 us
  waiting for transfers between devices: 70.7 us -> 44.2 us
  between operations: 14.2 us -> 0.83 us
  other arithmetic: 3.83 us -> 1.71 us
    all_to_all x1 -> x3, blocking collectives: 18 us -> 52.5 us  [exchange(): lax.all_to_all(x, axis, split_axis=0, concat_axis=0, tiled=True, axis_ind...]
    all_to_all x5 -> x4, waiting for transfers between devices: 68.4 us -> 39.6 us  [exchange(): lax.all_to_all(x, axis, split_axis=0, concat_axis=0, tiled=True, axis_ind...]
    all_to_all x5 -> x4, starting transfers between devices: 43.2 us -> 40.6 us  [exchange(): lax.all_to_all(x, axis, split_axis=0, concat_axis=0, tiled=True, axis_ind...]
    ppermute x1 -> x2, starting transfers between devices: 2.78 us -> 5.26 us  [the longest x1 3.08 us: body(): other = lax.ppermute(other, 'seq', swap)]
    ppermute x1 -> x2, waiting for transfers between devices: 2.26 us -> 4.65 us  [the longest x1 2.38 us: body(): w_other = lax.ppermute(w_own, 'seq', swap)]
    convert_element_type x2 -> x1, other arithmetic: 3.08 us -> 0.88 us  [one_hot(): return (feature == rows[None, :]).astype(BF)]
    unnamed x29 -> x27, local copies, waits for them, and re-layouts: 10.8 us -> 9.43 us
  transfers between devices with their start and end apart: 7 -> 6, of which waited for: 5 -> 5; matrix products, arithmetic and copies ran while one was open for 2% -> 1% of each run, Pallas kernels for 14% -> 10%
where the time goes in v4:
time: 196 us; the launch traced here: 195 us
  blocking collectives  52.5 us (27%)
  starting transfers between devices  45.8 us (23%)
  waiting for transfers between devices  44.2 us (23%)
  Pallas kernels  37.9 us (19%)
  local copies, waits for them, and re-layouts  11.7 us (6%)
    all_to_all x3, blocking collectives, exchange(): lax.all_to_all(x, axis, split_axis=0, concat_axis=0, tiled=True, axis_ind...  52.5 us
    all_to_all x4, starting transfers between devices, exchange(): lax.all_to_all(x, axis, split_axis=0, concat_axis=0, tiled=True, axis_ind...  40.6 us
    all_to_all x4, waiting for transfers between devices, exchange(): lax.all_to_all(x, axis, split_axis=0, concat_axis=0, tiled=True, axis_ind...  39.6 us
    pallas_call x1, Pallas kernels, forward(): call(functools.partial(forward_kernel, 4), [((rows // 3, 2 * E), BF), ((b...  13.8 us
    pallas_call x1, Pallas kernels, backward(): call(functools.partial(backward_kernel, 4), [(qkv.shape, BF)], [SM] + [VM...  12.9 us
    unnamed x27, local copies, waits for them, and re-layouts  9.43 us
  transfers between devices with their start and end apart: 6, of which 5 were waited for; matrix products, arithmetic and copies ran while one was open for 1% of the time, Pallas kernels for 10%

profile of v4, /device:TPU:1, one launch (start us, length us, event | category | flops | bytes accessed | tf_op | source)
XLA Modules:
  0.0 194.7 jit_solution(2049861070190619322)
XLA Ops:
  0.6 1.4 tile.4
  2.0 18.5 %all-to-all-start = ((bf16[32,2,1024]{2,1,0:T(2,128)(2,1)}), bf16[32,2,1024]{2,1,0:T(2,128)(2,1)S(1)}, u32[]{:S(2)}, u32[]{:S(2)}) async-start(bf16[32,2,1024]{2,1,0:T(2,128)(2,1)} %tile.4), calls=%async_computation | async-start | bytes 262144 | tf_op jit(solution)/shard_map/all_to_all | solution.py:244
  20.5 0.0 copy-start.7
  20.6 1.0 copy-done.7
  21.6 0.0 copy-start.8
  21.6 1.0 copy-done.8
  22.6 0.0 copy-start.9
  22.6 1.0 copy-done.9
  23.7 0.7 shard_map.101
  24.4 0.0 copy-start.1
  24.4 1.1 copy-done.1
  25.5 0.9 fusion.perm_ref
  26.4 0.0 copy-start
  26.4 8.9 %all-to-all-done = bf16[32,2,1024]{2,1,0:T(2,128)(2,1)S(1)} async-done(((bf16[32,2,1024]{2,1,0:T(2,128)(2,1)}), bf16[32,2,1024]{2,1,0:T(2,128)(2,1)S(1)}, u32[]{:S(2)}, u32[]{:S(2)}) %all-to-all-start) | async-done | bytes 131104 | tf_op jit(solution)/shard_map/all_to_all | solution.py:244
  35.3 0.1 reshape.126
  35.3 0.1 tile.5
  35.5 15.7 %all_to_all.35 = bf16[8,64,1024]{2,1,0:T(8,128)(2,1)S(1)} all-to-all(bf16[8,64,1024]{2,1,0:T(8,128)(2,1)S(1)} %tile.5), channel_id=1, replica_groups={{0,2,4,6,8,10,12,14},{1,3,5,7,9,11,13,15},{16,18,20,22,24,26,28,30},{17..., dimensions={0} | all-to-all | bytes 2097152 | tf_op jit(solution)/shard_map/all_to_all | solution.py:244
  51.2 0.0 copy-start.12
  51.2 9.2 %all-to-all-start.2 = ((bf16[16,384,128]{2,1,0:T(8,128)(2,1)}), bf16[16,384,128]{2,1,0:T(8,128)(2,1)}, u32[]{:S(2)}, u32[]{:S(2)}) async-start(bf16[16,384,128]{2,1,0:T(8,128)(2,1)} %copy-done.1), calls=%async_computation.2 | async-start | bytes 3145728 | tf_op jit(solution)/shard_map/all_to_all | solution.py:244
  60.4 2.2 %collective-permute-start = (bf16[512,1024]{1,0:T(8,128)(2,1)S(1)}, bf16[512,1024]{1,0:T(8,128)(2,1)}, u32[]{:S(2)}, u32[]{:S(2)}) collective-permute-start(bf16[512,1024]{1,0:T(8,128)(2,1)S(1)} %bitcast.14), channel_id=1, source_target_pairs={{0,1},{1,0},{2,3},{3,2},{4,5},{5,4},{6,7},{7,6},{8,9},{9,8},{10,11... | collective-permute-start | bytes 3145736 | tf_op jit(solution)/shard_map/ppermute | solution.py:279
  62.6 0.0 copy-done.12
  62.6 0.1 copy.11.layout_ref
  62.7 2.4 %collective-permute-done.w_other_ref = bf16[512,1024]{1,0:T(8,128)(2,1)} collective-permute-done((bf16[512,1024]{1,0:T(8,128)(2,1)S(1)}, bf16[512,1024]{1,0:T(8,128)(2,1)}, u32[]{:S(2)}, u32[]{:S(2)}) %collective-permute-start) | collective-permute-done | bytes 1048608 | tf_op jit(solution)/shard_map/ppermute | solution.py:279
  65.1 0.0 copy-done
  65.1 0.0 copy-start.5
  65.1 1.0 copy-done.5
  66.1 2.6 %shard_map.102 = bf16[16,128,128]{2,1,0:T(8,128)(2,1)S(1)} custom-call(bf16[256,1024]{1,0:T(8,128)(2,1)S(1)} %bitcast.20, bf16[512,1024]{1,0:T(8,128)(2,1)S(1)} %bitcast.15, bf16[512,1024]{1,0:T(8,128)(2,1)} %collective-permute-done.w_other_ref, bf16[1024,1024]{1,0:T(8,128)(2,1)S(1)} %fusion.perm_ref), custom_call_target="tpu_custom_call" | custom-call | flops 1073741824 | bytes 6291456 | tf_op jit(solution)/shard_map/pallas_call | solution.py:280
  68.7 0.0 copy-start.2
  68.7 0.8 copy-done.2
  69.5 12.6 %all-to-all-done.2 = bf16[16,384,128]{2,1,0:T(8,128)(2,1)} async-done(((bf16[16,384,128]{2,1,0:T(8,128)(2,1)}), bf16[16,384,128]{2,1,0:T(8,128)(2,1)}, u32[]{:S(2)}, u32[]{:S(2)}) %all-to-all-start.2) | async-done | bytes 1572896 | tf_op jit(solution)/shard_map/all_to_all | solution.py:244
  82.1 0.0 copy-start.3
  82.1 13.8 %shard_map.103 = (bf16[2048,128]{1,0:T(8,128)(2,1)S(1)}, f32[32,2,128]{2,1,0:T(2,128)S(1)}, bf16[32,128,128]{2,1,0:T(8,128)(2,1)S(1)}) custom-call(s32[32,4]{1,0:T(8,128)S(1)} %copy.11.layout_ref, bf16[6144,128]{1,0:T(8,128)(2,1)} %bitcast.5.qkv_ref), custom_call_target="tpu_custom_call" | custom-call | flops 1610612736 | bytes 4194304 | tf_op jit(solution)/shard_map/pallas_call | solution.py:223
  95.9 0.0 copy-start.10
  95.9 0.0 copy-done.3
  96.0 0.0 copy-start.6
  96.0 0.1 pad_maximum_fusion
  96.1 0.9 copy-done.10
  96.9 18.9 %all_to_all.36.attg_ref = bf16[16,256,128]{2,1,0:T(8,128)(2,1)S(1)} all-to-all(bf16[16,256,128]{2,1,0:T(8,128)(2,1)S(1)} %pad_maximum_fusion), channel_id=1, replica_groups=mesh['dp'=32,'seq'=16] {'seq'}, dimensions={0} | all-to-all | bytes 2097152 | tf_op jit(solution)/shard_map/all_to_all | solution.py:244
  115.8 0.0 copy-done.6
  115.8 3.1 %shard_map.104 = (bf16[512,1024]{1,0:T(8,128)(2,1)S(1)}, bf16[512,1024]{1,0:T(8,128)(2,1)S(1)}, bf16[256,1024]{1,0:T(8,128)(2,1)S(1)}) custom-call(bf16[16,256,128]{2,1,0:T(8,128)(2,1)S(1)} %all_to_all.36.attg_ref, bf16[256,1024]{1,0:T(8,128)(2,1)S(1)} %bitcast.21, bf16[1024,1024]{1,0:T(8,128)(2,1)} %copy-done), custom_call_target="tpu_custom_call" | custom-call | flops 1073741824 | bytes 6291456 | tf_op jit(solution)/shard_map/pallas_call | solution.py:288
  119.0 3.1 %collective-permute-start.1 = (bf16[512,1024]{1,0:T(8,128)(2,1)S(1)}, bf16[512,1024]{1,0:T(8,128)(2,1)S(1)}, u32[]{:S(2)}, u32[]{:S(2)}) collective-permute-start(bf16[512,1024]{1,0:T(8,128)(2,1)S(1)} %get-tuple-element.35), channel_id=1, source_target_pairs={{0,1},{1,0},{2,3},{3,2},{4,5},{5,4},{6,7},{7,6},{8,9},{9,8},{10,11... | collective-permute-start | bytes 3145736 | tf_op jit(solution)/shard_map/ppermute | solution.py:292
  122.0 2.3 %collective-permute-done.1.b_ref = bf16[512,1024]{1,0:T(8,128)(2,1)S(1)} collective-permute-done((bf16[512,1024]{1,0:T(8,128)(2,1)S(1)}, bf16[512,1024]{1,0:T(8,128)(2,1)S(1)}, u32[]{:S(2)}, u32[]{:S(2)}) %collective-permute-start.1) | collective-permute-done | bytes 1048608 | tf_op jit(solution)/shard_map/ppermute | solution.py:292
  124.3 0.2 shard_map.106
  124.6 17.9 %all_to_all.37.parts_ref = bf16[8,64,1024]{2,1,0:T(8,128)(2,1)S(1)} all-to-all(bf16[8,64,1024]{2,1,0:T(8,128)(2,1)S(1)} %bitcast.17), channel_id=1, replica_groups={{0,2,4,6,8,10,12,14},{1,3,5,7,9,11,13,15},{16,18,20,22,24,26,28,30},{17..., dimensions={0} | all-to-all | bytes 2097152 | tf_op jit(solution)/shard_map/all_to_all | solution.py:244
  142.4 0.1 shard_map.107
  142.6 0.7 reshape.131
  143.3 6.4 %all-to-all-start.5 = ((bf16[32,2,1024]{2,1,0:T(2,128)(2,1)}), bf16[32,2,1024]{2,1,0:T(2,128)(2,1)S(1)}, u32[]{:S(2)}, u32[]{:S(2)}) async-start(bf16[32,2,1024]{2,1,0:T(2,128)(2,1)} %reshape.131), calls=%async_computation.5 | async-start | bytes 262144 | tf_op jit(solution)/shard_map/all_to_all | solution.py:244
  149.7 0.0 copy-start.11
  149.7 1.2 copy-done.11
  150.9 12.9 %shard_map.108 = bf16[6144,128]{1,0:T(8,128)(2,1)S(1)} custom-call(s32[32,4]{1,0:T(8,128)S(1)} %copy.11.layout_ref, bf16[6144,128]{1,0:T(8,128)(2,1)} %bitcast.5.qkv_ref, bf16[4096,128]{1,0:T(8,128)(2,1)S(1)} %bitcast.19, bf16[32,128,128]{2,1,0:T(8,128)(2,1)S(1)} %copy-done.11, f32[32,2,128]{2,1,0:T(2,128)S(1)} %get-tuple-element.38.stat_ref), custom_call_target="tpu_custom_call" | custom-call | flops 3221225472 | bytes 6291456 | tf_op jit(solution)/shard_map/pallas_call | solution.py:233
  163.8 0.0 copy-start.4
  163.8 1.2 copy-done.4
  165.0 0.0 all-to-all-done.5
  165.0 6.5 %all-to-all-start.6 = ((bf16[16,384,128]{2,1,0:T(8,128)(2,1)}), bf16[16,384,128]{2,1,0:T(8,128)(2,1)S(1)}, u32[]{:S(2)}, u32[]{:S(2)}) async-start(bf16[16,384,128]{2,1,0:T(8,128)(2,1)} %bitcast.18), calls=%async_computation.6 | async-start | bytes 3145728 | tf_op jit(solution)/shard_map/all_to_all | solution.py:244
  171.4 2.7 %shard_map.105 = bf16[256,1024]{1,0:T(8,128)(2,1)} custom-call(bf16[256,1024]{1,0:T(8,128)(2,1)S(1)} %get-tuple-element.33.att_ref, bf16[512,1024]{1,0:T(8,128)(2,1)S(1)} %bitcast.16, bf16[512,1024]{1,0:T(8,128)(2,1)} %collective-permute-done.w_other_ref), custom_call_target="tpu_custom_call" | custom-call | flops 536870912 | bytes 3145728 | tf_op jit(solution)/shard_map/pallas_call | solution.py:299
  174.2 0.7 convert_reduce_fusion
  174.9 18.1 %all-to-all-done.6.src_ref = bf16[16,384,128]{2,1,0:T(8,128)(2,1)S(1)} async-done(((bf16[16,384,128]{2,1,0:T(8,128)(2,1)}), bf16[16,384,128]{2,1,0:T(8,128)(2,1)S(1)}, u32[]{:S(2)}, u32[]{:S(2)}) %all-to-all-start.6) | async-done | bytes 1572896 | tf_op jit(solution)/shard_map/all_to_all | solution.py:244
  193.0 1.7 shard_map.109
  (1 shorter events, 0.0 us)
Async XLA Ops:
  2.0 33.2 %all-to-all-start = ((bf16[32,2,1024]{2,1,0:T(2,128)(2,1)}), bf16[32,2,1024]{2,1,0:T(2,128)(2,1)S(1)}, u32[]{:S(2)}, u32[]{:S(2)}) async-start(bf16[32,2,1024]{2,1,0:T(2,128)(2,1)} %tile.4), calls=%async_computation | async-start | bytes 262144 | tf_op jit(solution)/shard_map/all_to_all | solution.py:244
  20.5 1.0 copy-start.7
  21.6 1.0 copy-start.8
  22.6 1.0 copy-start.9
  24.4 1.2 copy-start.1
  26.4 38.7 %copy-start = (bf16[1024,1024]{1,0:T(8,128)(2,1)}, bf16[1024,1024]{1,0:T(8,128)(2,1)S(1)}, u32[]{:S(2)}) copy-start(bf16[1024,1024]{1,0:T(8,128)(2,1)S(1)} %fusion.perm_ref) | copy-start | bytes 6291460
  51.2 11.4 %copy-start.12 = (s32[32,4]{0,1:T(4,128)S(1)}, s32[32,4]{0,1:T(4,128)}, u32[]{:S(2)}) copy-start(s32[32,4]{0,1:T(4,128)} %param.11) | copy-start | bytes 1540
  51.2 30.9 %all-to-all-start.2 = ((bf16[16,384,128]{2,1,0:T(8,128)(2,1)}), bf16[16,384,128]{2,1,0:T(8,128)(2,1)}, u32[]{:S(2)}, u32[]{:S(2)}) async-start(bf16[16,384,128]{2,1,0:T(8,128)(2,1)} %copy-done.1), calls=%async_computation.2 | async-start | bytes 3145728 | tf_op jit(solution)/shard_map/all_to_all | solution.py:244
  60.4 4.7 %collective-permute-start = (bf16[512,1024]{1,0:T(8,128)(2,1)S(1)}, bf16[512,1024]{1,0:T(8,128)(2,1)}, u32[]{:S(2)}, u32[]{:S(2)}) collective-permute-start(bf16[512,1024]{1,0:T(8,128)(2,1)S(1)} %bitcast.14), channel_id=1, source_target_pairs={{0,1},{1,0},{2,3},{3,2},{4,5},{5,4},{6,7},{7,6},{8,9},{9,8},{10,11... | collective-permute-start | bytes 3145736 | tf_op jit(solution)/shard_map/ppermute | solution.py:279
  65.1 1.0 copy-start.5
  68.7 0.8 copy-start.2
  82.1 13.8 %copy-start.3 = (bf16[16,128,128]{2,1,0:T(8,128)(2,1)S(1)}, bf16[16,128,128]{2,1,0:T(8,128)(2,1)}, u32[]{:S(2)}) copy-start(bf16[16,128,128]{2,1,0:T(8,128)(2,1)} %copy-done.2) | copy-start | bytes 1572868
  95.9 1.0 copy-start.10
  96.0 19.9 %copy-start.6 = (bf16[1,256,1024]{2,1,0:T(8,128)(2,1)S(1)}, bf16[1,256,1024]{2,1,0:T(8,128)(2,1)}, u32[]{:S(2)}) copy-start(bf16[1,256,1024]{2,1,0:T(8,128)(2,1)} %param.9) | copy-start | bytes 1572868
  119.0 5.3 %collective-permute-start.1 = (bf16[512,1024]{1,0:T(8,128)(2,1)S(1)}, bf16[512,1024]{1,0:T(8,128)(2,1)S(1)}, u32[]{:S(2)}, u32[]{:S(2)}) collective-permute-start(bf16[512,1024]{1,0:T(8,128)(2,1)S(1)} %get-tuple-element.35), channel_id=1, source_target_pairs={{0,1},{1,0},{2,3},{3,2},{4,5},{5,4},{6,7},{7,6},{8,9},{9,8},{10,11... | collective-permute-start | bytes 3145736 | tf_op jit(solution)/shard_map/ppermute | solution.py:292
  143.3 21.7 %all-to-all-start.5 = ((bf16[32,2,1024]{2,1,0:T(2,128)(2,1)}), bf16[32,2,1024]{2,1,0:T(2,128)(2,1)S(1)}, u32[]{:S(2)}, u32[]{:S(2)}) async-start(bf16[32,2,1024]{2,1,0:T(2,128)(2,1)} %reshape.131), calls=%async_computation.5 | async-start | bytes 262144 | tf_op jit(solution)/shard_map/all_to_all | solution.py:244
  149.7 1.2 copy-start.11
  163.8 1.2 copy-start.4
  165.0 28.0 %all-to-all-start.6 = ((bf16[16,384,128]{2,1,0:T(8,128)(2,1)}), bf16[16,384,128]{2,1,0:T(8,128)(2,1)S(1)}, u32[]{:S(2)}, u32[]{:S(2)}) async-start(bf16[16,384,128]{2,1,0:T(8,128)(2,1)} %bitcast.18), calls=%async_computation.6 | async-start | bytes 3145728 | tf_op jit(solution)/shard_map/all_to_all | solution.py:244

commit v5 on v4

--- a/solution.py
+++ b/solution.py
@@ -71,7 +71,7 @@
             out_ref[4 * quad + 2 * i + 1] = odd.astype(BF)
 
 
-def forward_kernel(unroll, layout_ref, qkv_ref, att_ref, stat_ref, kvt_ref):
+def forward_kernel(group, layout_ref, qkv_ref, g_ref, attg_ref, stat_ref, kvt_ref):
     blocks = layout_ref.shape[0]
     scale = 1.0 / E**0.5
     log2e = 1.4426950408889634
@@ -80,73 +80,88 @@
         kvt_ref[b] = qkv_ref[pl.ds(key_rows(b), B), :].T
         return carry
 
-    lax.fori_loop(0, blocks, prepare, 0, unroll=4)
-
-    def per_pair(s, carry):
-        at = pl.multiple_of(s * B, B)
-        qt = qkv_ref[pl.ds(pl.multiple_of(s * 3 * B, B), B), :].T
+    lax.fori_loop(0, blocks, prepare, 0, unroll=8)
+
+    def step(n, carry):
+        pairs = [n * group + i for i in range(group)]
         zero = jnp.zeros((E, B), BF)
-        att_t = []
-        for p in range(2):
-            ids = [layout_ref[2 * s + p, j] for j in range(4)]
-            rhs = jnp.concatenate([qt[p * E:(p + 1) * E], zero], axis=0)
-            kv = jnp.concatenate([qkv_ref[pl.ds(key_rows(i), B), :] for i in ids], axis=0)
-            scores = lax.dot_general(kv, rhs, NN, preferred_element_type=F32)
-            top = jnp.max(scores, axis=0, keepdims=True)
-            expo = jnp.exp2((scores - top) * (scale * log2e))
-            inverse = 1.0 / jnp.sum(expo, axis=0, keepdims=True)
-            probs = (expo * inverse).astype(BF)
-            stat_ref[2 * s + p] = jnp.concatenate([top, inverse], axis=0)
-            vt = jnp.concatenate([kvt_ref[i, E:, :] for i in ids], axis=1)
-            att_t.append(lax.dot_general(vt, probs, NN, preferred_element_type=F32))
-        att_ref[pl.ds(at, B), :] = jnp.concatenate(att_t, axis=0).T.astype(BF)
+        qts = [qkv_ref[pl.ds(pl.multiple_of(s * 3 * B, B), B), :].T for s in pairs]
+        work = [(s, p, [layout_ref[2 * s + p, j] for j in range(4)]) for s in pairs for p in range(2)]
+        scores = []
+        for i, (s, p, ids) in enumerate(work):
+            rhs = jnp.concatenate([qts[i // 2][p * E:(p + 1) * E], zero], axis=0)
+            kv = jnp.concatenate([qkv_ref[pl.ds(key_rows(j), B), :] for j in ids], axis=0)
+            scores.append(lax.dot_general(kv, rhs, NN, preferred_element_type=F32))
+        tops = [jnp.max(x, axis=0, keepdims=True) for x in scores]
+        expos = [jnp.exp2((x - t) * (scale * log2e)) for x, t in zip(scores, tops)]
+        inverses = [1.0 / jnp.sum(x, axis=0, keepdims=True) for x in expos]
+        probs = [(x * y).astype(BF) for x, y in zip(expos, inverses)]
+        outs = []
+        for i, (s, p, ids) in enumerate(work):
+            vt = jnp.concatenate([kvt_ref[j, E:, :] for j in ids], axis=1)
+            outs.append(lax.dot_general(vt, probs[i], NN, preferred_element_type=F32))
+        for i, (s, p, ids) in enumerate(work):
+            stat_ref[2 * s + p] = jnp.concatenate([tops[i], inverses[i]], axis=0)
+        for i, s in enumerate(pairs):
+            att = jnp.concatenate([outs[2 * i], outs[2 * i + 1]], axis=0).astype(BF)
+            attg_ref[s, :B] = att.T
+            attg_ref[s, B:] = g_ref[s]
         return carry
 
-    lax.fori_loop(0, blocks // 2, per_pair, 0, unroll=unroll)
-
-
-def backward_kernel(unroll, layout_ref, qkv_ref, attg_ref, kvt_ref, stat_ref, out_ref, acc_ref):
+    lax.fori_loop(0, blocks // 2 // group, step, 0)
+
+
+def backward_kernel(
+    group, layout_ref, qkv_ref, attg_ref, kvt_ref, stat_ref, out_ref, acc_ref
+):
     blocks = layout_ref.shape[0]
     scale = 1.0 / E**0.5
     log2e = 1.4426950408889634
     acc_ref[...] = jnp.zeros(acc_ref.shape, F32)
 
-    def per_pair(s, carry):
-        at = pl.multiple_of(s * 3 * B, B)
-        qt = qkv_ref[pl.ds(at, B), :].T
-        gt = attg_ref[pl.ds(pl.multiple_of(s * 2 * B + B, B), B), :].T
+    def step(n, carry):
+        pairs = [n * group + i for i in range(group)]
         zero = jnp.zeros((E, B), BF)
-        dq_t = []
-        for p in range(2):
-            ids = [layout_ref[2 * s + p, j] for j in range(4)]
-            starts = [key_rows(i) for i in ids]
+        qts = [qkv_ref[pl.ds(pl.multiple_of(s * 3 * B, B), B), :].T for s in pairs]
+        gts = [attg_ref[s, B:].T for s in pairs]
+        work = [(s, p, [layout_ref[2 * s + p, j] for j in range(4)]) for s in pairs for p in range(2)]
+        xts, boths = [], []
+        for i, (s, p, ids) in enumerate(work):
             rows = slice(p * E, (p + 1) * E)
-            left = jnp.concatenate([qt[rows], zero], axis=0)
-            right = jnp.concatenate([zero, gt[rows]], axis=0)
-            kv = jnp.concatenate([qkv_ref[pl.ds(i, B), :] for i in starts], axis=0)
+            left = jnp.concatenate([qts[i // 2][rows], zero], axis=0)
+            right = jnp.concatenate([zero, gts[i // 2][rows]], axis=0)
             xt = jnp.concatenate([left, right], axis=1)
-            both = lax.dot_general(kv, xt, NN, preferred_element_type=F32)
-            scores, dprob = both[:, :B], both[:, B:]
+            kv = jnp.concatenate([qkv_ref[pl.ds(key_rows(j), B), :] for j in ids], axis=0)
+            xts.append(xt)
+            boths.append(lax.dot_general(kv, xt, NN, preferred_element_type=F32))
+        yts = []
+        for i, (s, p, ids) in enumerate(work):
+            scores, dprob = boths[i][:, :B], boths[i][:, B:]
             stat = stat_ref[2 * s + p]
             expo = jnp.exp2((scores - stat[:1]) * (scale * log2e))
             inverse = stat[1:]
             inner = jnp.sum(expo * dprob, axis=0, keepdims=True) * inverse
             probs = (expo * inverse).astype(BF)
             dscore = (expo * ((dprob - inner) * (inverse * scale))).astype(BF)
-            kt = jnp.concatenate([kvt_ref[i, :E, :] for i in ids], axis=1)
-            dq_t.append(lax.dot_general(kt, dscore, NN, preferred_element_type=F32))
-            yt = jnp.concatenate([dscore, probs], axis=1)
-            part = lax.dot_general(yt, xt, NT, preferred_element_type=F32)
+            yts.append(jnp.concatenate([dscore, probs], axis=1))
+        outs, parts = [], []
+        for i, (s, p, ids) in enumerate(work):
+            kt = jnp.concatenate([kvt_ref[j, :E, :] for j in ids], axis=1)
+            outs.append(lax.dot_general(kt, yts[i][:, :B], NN, preferred_element_type=F32))
+            parts.append(lax.dot_general(yts[i], xts[i], NT, preferred_element_type=F32))
+        for i, (s, p, ids) in enumerate(work):
             for j in range(4):
-                acc_ref[pl.ds(starts[j], B), :] += part[j * B:(j + 1) * B]
-        out_ref[pl.ds(at, B), :] = jnp.concatenate(dq_t, axis=0).T.astype(BF)
+                acc_ref[pl.ds(pl.multiple_of(ids[j] * B, B), B), :] += parts[i][j * B:(j + 1) * B]
+        for i, s in enumerate(pairs):
+            dq = jnp.concatenate([outs[2 * i], outs[2 * i + 1]], axis=0).astype(BF)
+            out_ref[s, :B] = dq.T
         return carry
 
-    lax.fori_loop(0, blocks // 2, per_pair, 0, unroll=unroll)
+    lax.fori_loop(0, blocks // 2 // group, step, 0)
 
     def finish(s, carry):
-        at = pl.multiple_of(s * 3 * B + B, B)
-        out_ref[pl.ds(at, 2 * B), :] = acc_ref[pl.ds(at, 2 * B), :].astype(BF)
+        at = pl.multiple_of(s * 2 * B, B)
+        out_ref[s, B:] = acc_ref[pl.ds(at, 2 * B), :].astype(BF)
         return carry
 
     lax.fori_loop(0, blocks // 2, finish, 0, unroll=4)
@@ -217,25 +232,25 @@
     return call(sum_kernel, [(parts.shape[1:], dtype)], [VM], moved=2 * parts.size)(parts)[0]
 
 
-def forward(layout, qkv):
-    rows = qkv.shape[0]
+def forward(layout, qkv, g):
     blocks = layout.shape[0]
     return call(
         functools.partial(forward_kernel, 4),
-        [((rows // 3, 2 * E), BF), ((blocks, 2, B), F32), ((blocks, 2 * E, B), BF)],
-        [SM, VM],
-        flops=2 * rows * 512 * 128 * 2,
+        [((H, 2 * B, 2 * E), BF), ((blocks, 2, B), F32), ((blocks, 2 * E, B), BF)],
+        [SM, VM, VM],
+        flops=2 * qkv.shape[0] * 512 * 128,
         moved=4 * 2**20,
-    )(layout, qkv)
+    )(layout, qkv, g)
 
 
 def backward(layout, qkv, attg, kvt, stats):
+    blocks = layout.shape[0]
     return call(
         functools.partial(backward_kernel, 4),
-        [(qkv.shape, BF)],
+        [((H, 3 * B, 2 * E), BF)],
         [SM] + [VM] * 4,
-        [pltpu.VMEM(qkv.shape, F32)],
-        flops=4 * qkv.shape[0] * 512 * 128 * 2,
+        [pltpu.VMEM((blocks * B, 2 * E), F32)],
+        flops=4 * qkv.shape[0] * 512 * 128,
         moved=6 * 2**20,
     )(layout, qkv, attg, kvt, stats)[0]
 
@@ -281,8 +296,7 @@
         grad_kernel, [((H, B, 2 * E), BF)], [VM] * 4, scratch, flops=2 * square, moved=6 * 2**20
     )(grad, w_own, w_other, perm)[0]
     g, qkv = lax.optimization_barrier((g, qkv))
-    att, stats, kvt = forward(layout, qkv)
-    attg = jnp.concatenate([att.reshape(H, B, 2 * E), g], axis=1)
+    attg, stats, kvt = forward(layout, qkv, g)
     attg = exchange(attg, "seq")
     half = (width // 2, width)
     own, other, att = call(
@@ -295,13 +309,13 @@
     total = add_up(terms, BF).reshape(dp, -1, width)
     attg, total = lax.optimization_barrier((attg, total))
     total = exchange(total, "dp")
-    slabs = backward(layout, qkv, attg.reshape(-1, 2 * E), kvt, stats)
+    slabs = backward(layout, qkv, attg, kvt, stats)
     mixed = call(
         mixed_kernel, [((tokens, width), BF)], [VM] * 3, flops=square, moved=3 * 2**20
     )(att, w_own, w_other)[0]
     slabs, total = lax.optimization_barrier((slabs, total))
     weight_grad = total.astype(F32).sum(axis=0)
-    slabs = exchange(slabs.reshape(H, 3 * B, 2 * E), "seq")
+    slabs = exchange(slabs, "seq")
     dq, dk, dv = call(unpack_kernel, [((tokens, width), BF)] * 3, [VM], moved=3 * 2**20)(slabs)
     return mixed[None], dq[None], dk[None], dv[None], weight_grad
 

time: 196 us -> 189 us (0.964)
  Pallas kernels: 37.9 us -> 26.4 us
  waiting for transfers between devices: 44.2 us -> 48 us
    pallas_call x2, Pallas kernels: 26.7 us -> 15.2 us  [the longest x1 8.65 us: backward(): call(functools.partial(backward_kernel, 4), [((H, 3 * B, 2 * E), BF)], [S...]
    all_to_all x4, waiting for transfers between devices: 39.6 us -> 43.3 us  [exchange(): lax.all_to_all(x, axis, split_axis=0, concat_axis=0, tiled=True, axis_ind...]
  transfers between devices with their start and end apart: 6 -> 6, of which waited for: 5 -> 6; matrix products, arithmetic and copies ran while one was open for 1% -> 1% of each run, Pallas kernels for 10% -> 8%
where the time goes in v5:
time: 189 us; the launch traced here: 188 us
  blocking collectives  52.5 us (28%)
  waiting for transfers between devices  48 us (25%)
  starting transfers between devices  46.3 us (24%)
  Pallas kernels  26.4 us (14%)
  local copies, waits for them, and re-layouts  11.9 us (6%)
    all_to_all x3, blocking collectives, exchange(): lax.all_to_all(x, axis, split_axis=0, concat_axis=0, tiled=True, axis_ind...  52.5 us
    all_to_all x4, waiting for transfers between devices, exchange(): lax.all_to_all(x, axis, split_axis=0, concat_axis=0, tiled=True, axis_ind...  43.3 us
    all_to_all x4, starting transfers between devices, exchange(): lax.all_to_all(x, axis, split_axis=0, concat_axis=0, tiled=True, axis_ind...  41.1 us
    unnamed x27, local copies, waits for them, and re-layouts  9.61 us
    pallas_call x1, Pallas kernels, backward(): call(functools.partial(backward_kernel, 4), [((H, 3 * B, 2 * E), BF)], [S...  8.65 us
    pallas_call x1, Pallas kernels, forward(): call(functools.partial(forward_kernel, 4), [((H, 2 * B, 2 * E), BF), ((bl...  6.55 us
  transfers between devices with their start and end apart: 6, of which 6 were waited for; matrix products, arithmetic and copies ran while one was open for 1% of the time, Pallas kernels for 8%

profile of v5, /device:TPU:1, one launch (start us, length us, event | category | flops | bytes accessed | tf_op | source)
XLA Modules:
  0.0 187.6 jit_solution(6381469886765242450)
XLA Ops:
  0.6 1.4 tile.4
  2.0 18.5 %all-to-all-start = ((bf16[32,2,1024]{2,1,0:T(2,128)(2,1)}), bf16[32,2,1024]{2,1,0:T(2,128)(2,1)S(1)}, u32[]{:S(2)}, u32[]{:S(2)}) async-start(bf16[32,2,1024]{2,1,0:T(2,128)(2,1)} %tile.4), calls=%async_computation | async-start | bytes 262144 | tf_op jit(solution)/shard_map/all_to_all | solution.py:259
  20.5 0.0 copy-start.7
  20.6 1.0 copy-done.7
  21.6 0.0 copy-start.8
  21.6 1.0 copy-done.8
  22.6 0.0 copy-start.9
  22.6 1.0 copy-done.9
  23.7 0.7 shard_map.101
  24.4 0.0 copy-start.1
  24.4 1.1 copy-done.1
  25.5 0.9 fusion.perm_ref
  26.4 0.0 copy-start
  26.4 8.9 %all-to-all-done = bf16[32,2,1024]{2,1,0:T(2,128)(2,1)S(1)} async-done(((bf16[32,2,1024]{2,1,0:T(2,128)(2,1)}), bf16[32,2,1024]{2,1,0:T(2,128)(2,1)S(1)}, u32[]{:S(2)}, u32[]{:S(2)}) %all-to-all-start) | async-done | bytes 131104 | tf_op jit(solution)/shard_map/all_to_all | solution.py:259
  35.3 0.1 reshape.117
  35.3 0.1 tile.5
  35.5 15.7 %all_to_all.35 = bf16[8,64,1024]{2,1,0:T(8,128)(2,1)S(1)} all-to-all(bf16[8,64,1024]{2,1,0:T(8,128)(2,1)S(1)} %tile.5), channel_id=1, replica_groups={{0,2,4,6,8,10,12,14},{1,3,5,7,9,11,13,15},{16,18,20,22,24,26,28,30},{17..., dimensions={0} | all-to-all | bytes 2097152 | tf_op jit(solution)/shard_map/all_to_all | solution.py:259
  51.2 0.0 copy-start.12
  51.2 9.2 %all-to-all-start.2 = ((bf16[16,384,128]{2,1,0:T(8,128)(2,1)}), bf16[16,384,128]{2,1,0:T(8,128)(2,1)}, u32[]{:S(2)}, u32[]{:S(2)}) async-start(bf16[16,384,128]{2,1,0:T(8,128)(2,1)} %copy-done.1), calls=%async_computation.2 | async-start | bytes 3145728 | tf_op jit(solution)/shard_map/all_to_all | solution.py:259
  60.4 2.2 %collective-permute-start = (bf16[512,1024]{1,0:T(8,128)(2,1)S(1)}, bf16[512,1024]{1,0:T(8,128)(2,1)}, u32[]{:S(2)}, u32[]{:S(2)}) collective-permute-start(bf16[512,1024]{1,0:T(8,128)(2,1)S(1)} %bitcast.11), channel_id=1, source_target_pairs={{0,1},{1,0},{2,3},{3,2},{4,5},{5,4},{6,7},{7,6},{8,9},{9,8},{10,11... | collective-permute-start | bytes 3145736 | tf_op jit(solution)/shard_map/ppermute | solution.py:294
  62.6 0.0 copy-done.12
  62.6 0.1 copy.11.layout_ref
  62.7 2.4 %collective-permute-done.w_other_ref = bf16[512,1024]{1,0:T(8,128)(2,1)} collective-permute-done((bf16[512,1024]{1,0:T(8,128)(2,1)S(1)}, bf16[512,1024]{1,0:T(8,128)(2,1)}, u32[]{:S(2)}, u32[]{:S(2)}) %collective-permute-start) | collective-permute-done | bytes 1048608 | tf_op jit(solution)/shard_map/ppermute | solution.py:294
  65.1 0.0 copy-done
  65.1 0.0 copy-start.3
  65.1 1.0 copy-done.3
  66.1 2.6 %shard_map.102.g_ref = bf16[16,128,128]{2,1,0:T(8,128)(2,1)S(1)} custom-call(bf16[256,1024]{1,0:T(8,128)(2,1)S(1)} %bitcast.15, bf16[512,1024]{1,0:T(8,128)(2,1)S(1)} %bitcast.12, bf16[512,1024]{1,0:T(8,128)(2,1)} %collective-permute-done.w_other_ref, bf16[1024,1024]{1,0:T(8,128)(2,1)S(1)} %fusion.perm_ref), custom_call_target="tpu_custom_call" | custom-call | flops 1073741824 | bytes 6291456 | tf_op jit(solution)/shard_map/pallas_call | solution.py:295
  68.7 0.0 copy-start.5
  68.7 0.8 copy-done.5
  69.5 12.6 %all-to-all-done.2 = bf16[16,384,128]{2,1,0:T(8,128)(2,1)} async-done(((bf16[16,384,128]{2,1,0:T(8,128)(2,1)}), bf16[16,384,128]{2,1,0:T(8,128)(2,1)}, u32[]{:S(2)}, u32[]{:S(2)}) %all-to-all-start.2) | async-done | bytes 1572896 | tf_op jit(solution)/shard_map/all_to_all | solution.py:259
  82.1 0.0 copy-start.6
  82.1 1.0 copy-done.6
  83.1 0.0 copy-start.4
  83.1 6.5 %shard_map.103 = (bf16[16,256,128]{2,1,0:T(8,128)(2,1)S(1)}, f32[32,2,128]{2,1,0:T(2,128)S(1)}, bf16[32,128,128]{2,1,0:T(8,128)(2,1)S(1)}) custom-call(s32[32,4]{1,0:T(8,128)S(1)} %copy.11.layout_ref, bf16[6144,128]{1,0:T(8,128)(2,1)} %bitcast.5.qkv_ref, bf16[16,128,128]{2,1,0:T(8,128)(2,1)S(1)} %copy-done.6), custom_call_target="tpu_custom_call" | custom-call | flops 805306368 | bytes 4194304 | tf_op jit(solution)/shard_map/pallas_call | solution.py:237
  89.7 0.0 copy-start.10
  89.7 18.9 %all_to_all.36.attg_ref = bf16[16,256,128]{2,1,0:T(8,128)(2,1)S(1)} all-to-all(bf16[16,256,128]{2,1,0:T(8,128)(2,1)S(1)} %get-tuple-element.32), channel_id=1, replica_groups=mesh['dp'=32,'seq'=16] {'seq'}, dimensions={0} | all-to-all | bytes 2097152 | tf_op jit(solution)/shard_map/all_to_all | solution.py:259
  108.6 0.0 copy-done.4
  108.6 3.1 %shard_map.104 = (bf16[512,1024]{1,0:T(8,128)(2,1)S(1)}, bf16[512,1024]{1,0:T(8,128)(2,1)S(1)}, bf16[256,1024]{1,0:T(8,128)(2,1)S(1)}) custom-call(bf16[16,256,128]{2,1,0:T(8,128)(2,1)S(1)} %all_to_all.36.attg_ref, bf16[256,1024]{1,0:T(8,128)(2,1)S(1)} %bitcast.16, bf16[1024,1024]{1,0:T(8,128)(2,1)} %copy-done), custom_call_target="tpu_custom_call" | custom-call | flops 1073741824 | bytes 6291456 | tf_op jit(solution)/shard_map/pallas_call | solution.py:302
  111.8 0.0 copy-done.10
  111.8 3.0 %collective-permute-start.1 = (bf16[512,1024]{1,0:T(8,128)(2,1)S(1)}, bf16[512,1024]{1,0:T(8,128)(2,1)S(1)}, u32[]{:S(2)}, u32[]{:S(2)}) collective-permute-start(bf16[512,1024]{1,0:T(8,128)(2,1)S(1)} %get-tuple-element.35), channel_id=1, source_target_pairs={{0,1},{1,0},{2,3},{3,2},{4,5},{5,4},{6,7},{7,6},{8,9},{9,8},{10,11... | collective-permute-start | bytes 3145736 | tf_op jit(solution)/shard_map/ppermute | solution.py:306
  114.8 2.3 %collective-permute-done.1.b_ref = bf16[512,1024]{1,0:T(8,128)(2,1)S(1)} collective-permute-done((bf16[512,1024]{1,0:T(8,128)(2,1)S(1)}, bf16[512,1024]{1,0:T(8,128)(2,1)S(1)}, u32[]{:S(2)}, u32[]{:S(2)}) %collective-permute-start.1) | collective-permute-done | bytes 1048608 | tf_op jit(solution)/shard_map/ppermute | solution.py:306
  117.1 0.2 shard_map.106
  117.3 17.9 %all_to_all.37.parts_ref = bf16[8,64,1024]{2,1,0:T(8,128)(2,1)S(1)} all-to-all(bf16[8,64,1024]{2,1,0:T(8,128)(2,1)S(1)} %bitcast.14), channel_id=1, replica_groups={{0,2,4,6,8,10,12,14},{1,3,5,7,9,11,13,15},{16,18,20,22,24,26,28,30},{17..., dimensions={0} | all-to-all | bytes 2097152 | tf_op jit(solution)/shard_map/all_to_all | solution.py:259
  135.2 0.1 shard_map.107
  135.4 0.7 reshape.121
  136.1 6.5 %all-to-all-start.5 = ((bf16[32,2,1024]{2,1,0:T(2,128)(2,1)}), bf16[32,2,1024]{2,1,0:T(2,128)(2,1)S(1)}, u32[]{:S(2)}, u32[]{:S(2)}) async-start(bf16[32,2,1024]{2,1,0:T(2,128)(2,1)} %reshape.121), calls=%async_computation.5 | async-start | bytes 262144 | tf_op jit(solution)/shard_map/all_to_all | solution.py:259
  142.5 0.0 copy-start.11
  142.5 1.2 copy-done.11
  143.7 8.6 %shard_map.108 = bf16[16,384,128]{2,1,0:T(8,128)(2,1)S(1)} custom-call(s32[32,4]{1,0:T(8,128)S(1)} %copy.11.layout_ref, bf16[6144,128]{1,0:T(8,128)(2,1)} %bitcast.5.qkv_ref, bf16[16,256,128]{2,1,0:T(8,128)(2,1)S(1)} %all_to_all.36.attg_ref, bf16[32,128,128]{2,1,0:T(8,128)(2,1)S(1)} %copy-done.11, f32[32,2,128]{2,1,0:T(2,128)S(1)} %get-tuple-element.38.stat_ref), custom_call_target="tpu_custom_call" | custom-call | flops 1610612736 | bytes 6291456 | tf_op jit(solution)/shard_map/pallas_call | solution.py:248
  152.4 0.0 copy-start.2
  152.4 1.2 copy-done.2
  153.6 3.8 %all-to-all-done.5 = bf16[32,2,1024]{2,1,0:T(2,128)(2,1)S(1)} async-done(((bf16[32,2,1024]{2,1,0:T(2,128)(2,1)}), bf16[32,2,1024]{2,1,0:T(2,128)(2,1)S(1)}, u32[]{:S(2)}, u32[]{:S(2)}) %all-to-all-start.5) | async-done | bytes 131104 | tf_op jit(solution)/shard_map/all_to_all | solution.py:259
  157.3 6.9 %all-to-all-start.6 = ((bf16[16,384,128]{2,1,0:T(8,128)(2,1)}), bf16[16,384,128]{2,1,0:T(8,128)(2,1)S(1)}, u32[]{:S(2)}, u32[]{:S(2)}) async-start(bf16[16,384,128]{2,1,0:T(8,128)(2,1)} %copy-done.2), calls=%async_computation.6 | async-start | bytes 3145728 | tf_op jit(solution)/shard_map/all_to_all | solution.py:259
  164.2 2.7 %shard_map.105 = bf16[256,1024]{1,0:T(8,128)(2,1)} custom-call(bf16[256,1024]{1,0:T(8,128)(2,1)S(1)} %get-tuple-element.33.att_ref, bf16[512,1024]{1,0:T(8,128)(2,1)S(1)} %bitcast.13, bf16[512,1024]{1,0:T(8,128)(2,1)} %collective-permute-done.w_other_ref), custom_call_target="tpu_custom_call" | custom-call | flops 536870912 | bytes 3145728 | tf_op jit(solution)/shard_map/pallas_call | solution.py:313
  167.0 0.7 convert_reduce_fusion
  167.7 18.1 %all-to-all-done.6.src_ref = bf16[16,384,128]{2,1,0:T(8,128)(2,1)S(1)} async-done(((bf16[16,384,128]{2,1,0:T(8,128)(2,1)}), bf16[16,384,128]{2,1,0:T(8,128)(2,1)S(1)}, u32[]{:S(2)}, u32[]{:S(2)}) %all-to-all-start.6) | async-done | bytes 1572896 | tf_op jit(solution)/shard_map/all_to_all | solution.py:259
  185.8 1.7 shard_map.109
  (1 shorter events, 0.0 us)
Async XLA Ops:
  2.0 33.2 %all-to-all-start = ((bf16[32,2,1024]{2,1,0:T(2,128)(2,1)}), bf16[32,2,1024]{2,1,0:T(2,128)(2,1)S(1)}, u32[]{:S(2)}, u32[]{:S(2)}) async-start(bf16[32,2,1024]{2,1,0:T(2,128)(2,1)} %tile.4), calls=%async_computation | async-start | bytes 262144 | tf_op jit(solution)/shard_map/all_to_all | solution.py:259
  20.5 1.0 copy-start.7
  21.6 1.0 copy-start.8
  22.6 1.0 copy-start.9
  24.4 1.2 copy-start.1
  26.4 38.7 %copy-start = (bf16[1024,1024]{1,0:T(8,128)(2,1)}, bf16[1024,1024]{1,0:T(8,128)(2,1)S(1)}, u32[]{:S(2)}) copy-start(bf16[1024,1024]{1,0:T(8,128)(2,1)S(1)} %fusion.perm_ref) | copy-start | bytes 6291460
  51.2 11.4 %copy-start.12 = (s32[32,4]{0,1:T(4,128)S(1)}, s32[32,4]{0,1:T(4,128)}, u32[]{:S(2)}) copy-start(s32[32,4]{0,1:T(4,128)} %param.11) | copy-start | bytes 1540
  51.2 30.9 %all-to-all-start.2 = ((bf16[16,384,128]{2,1,0:T(8,128)(2,1)}), bf16[16,384,128]{2,1,0:T(8,128)(2,1)}, u32[]{:S(2)}, u32[]{:S(2)}) async-start(bf16[16,384,128]{2,1,0:T(8,128)(2,1)} %copy-done.1), calls=%async_computation.2 | async-start | bytes 3145728 | tf_op jit(solution)/shard_map/all_to_all | solution.py:259
  60.4 4.7 %collective-permute-start = (bf16[512,1024]{1,0:T(8,128)(2,1)S(1)}, bf16[512,1024]{1,0:T(8,128)(2,1)}, u32[]{:S(2)}, u32[]{:S(2)}) collective-permute-start(bf16[512,1024]{1,0:T(8,128)(2,1)S(1)} %bitcast.11), channel_id=1, source_target_pairs={{0,1},{1,0},{2,3},{3,2},{4,5},{5,4},{6,7},{7,6},{8,9},{9,8},{10,11... | collective-permute-start | bytes 3145736 | tf_op jit(solution)/shard_map/ppermute | solution.py:294
  65.1 1.0 copy-start.3
  68.7 0.8 copy-start.5
  82.1 1.0 copy-start.6
  83.1 25.5 %copy-start.4 = (bf16[1,256,1024]{2,1,0:T(8,128)(2,1)S(1)}, bf16[1,256,1024]{2,1,0:T(8,128)(2,1)}, u32[]{:S(2)}) copy-start(bf16[1,256,1024]{2,1,0:T(8,128)(2,1)} %param.9) | copy-start | bytes 1572868
  89.7 22.1 %copy-start.10 = (bf16[32,128,128]{2,1,0:T(8,128)(2,1)}, bf16[32,128,128]{2,1,0:T(8,128)(2,1)S(1)}, u32[]{:S(2)}) copy-start(bf16[32,128,128]{2,1,0:T(8,128)(2,1)S(1)} %get-tuple-element.37.kvt_ref) | copy-start | bytes 3145732
  111.8 5.3 %collective-permute-start.1 = (bf16[512,1024]{1,0:T(8,128)(2,1)S(1)}, bf16[512,1024]{1,0:T(8,128)(2,1)S(1)}, u32[]{:S(2)}, u32[]{:S(2)}) collective-permute-start(bf16[512,1024]{1,0:T(8,128)(2,1)S(1)} %get-tuple-element.35), channel_id=1, source_target_pairs={{0,1},{1,0},{2,3},{3,2},{4,5},{5,4},{6,7},{7,6},{8,9},{9,8},{10,11... | collective-permute-start | bytes 3145736 | tf_op jit(solution)/shard_map/ppermute | solution.py:306
  136.1 21.3 %all-to-all-start.5 = ((bf16[32,2,1024]{2,1,0:T(2,128)(2,1)}), bf16[32,2,1024]{2,1,0:T(2,128)(2,1)S(1)}, u32[]{:S(2)}, u32[]{:S(2)}) async-start(bf16[32,2,1024]{2,1,0:T(2,128)(2,1)} %reshape.121), calls=%async_computation.5 | async-start | bytes 262144 | tf_op jit(solution)/shard_map/all_to_all | solution.py:259
  142.5 1.2 copy-start.11
  152.4 1.2 copy-start.2
  157.3 28.5 %all-to-all-start.6 = ((bf16[16,384,128]{2,1,0:T(8,128)(2,1)}), bf16[16,384,128]{2,1,0:T(8,128)(2,1)S(1)}, u32[]{:S(2)}, u32[]{:S(2)}) async-start(bf16[16,384,128]{2,1,0:T(8,128)(2,1)} %copy-done.2), calls=%async_computation.6 | async-start | bytes 3145728 | tf_op jit(solution)/shard_map/all_to_all | solution.py:259

commit v6 on v5

--- a/solution.py
+++ b/solution.py
@@ -41,7 +41,7 @@
 
 
 def key_rows(b):
-    return pl.multiple_of((b // 2) * (3 * B) + B + (b % 2) * B, B)
+    return pl.multiple_of((b // 2) * (5 * B) + B + (b % 2) * B, B)
 
 
 def pack_kernel(q_ref, k_ref, v_ref, out_ref):
@@ -55,23 +55,37 @@
             out_ref[2 * pair + 1, rows] = odd.astype(BF)
 
 
-def grad_kernel(og_ref, w_own_ref, w_other_ref, perm_ref, out_ref, tmp_ref):
-    half = w_own_ref.shape[0]
-    for i, ref in enumerate((w_own_ref, w_other_ref)):
-        for at in range(0, half, 4 * E):
-            g = lax.dot_general(og_ref[...], ref[at:at + 4 * E], NT, preferred_element_type=F32)
-            tmp_ref[:, i * half + at:i * half + at + 4 * E] = g.astype(BF)
+def column_half(ref, core):
+    width = ref.shape[1] // 2
+    return ref[:, pl.ds(pl.multiple_of(core * width, width), width)]
+
+
+def grad_kernel(core_ref, og_ref, own_ref, other_ref, perm_ref, att_ref, out_ref, w_ref, tmp_ref):
+    out_ref[:, :B] = att_ref[...]
+    owners, place = own_ref.shape[0], own_ref.shape[1] // 4
+    for half, ref in enumerate((own_ref, other_ref)):
+        for s in range(owners):
+            for c in range(4):
+                w_ref[s * place:(s + 1) * place, (half * 4 + c) * B:(half * 4 + c + 1) * B] = ref[
+                    s, c * place:(c + 1) * place
+                ]
+    core = core_ref[0]
+    og = jnp.concatenate([column_half(og_ref, core), column_half(og_ref, 1 - core)], axis=1)
+    for quad in range(H // 4):
+        rows = slice(quad * 4 * E, (quad + 1) * 4 * E)
+        g = lax.dot_general(og, w_ref[rows, :], NT, preferred_element_type=F32)
+        tmp_ref[:, rows] = g.astype(BF)
     for quad in range(H // 4):
         rows = slice(quad * 4 * E, (quad + 1) * 4 * E)
         g = lax.dot_general(tmp_ref[...], perm_ref[rows, :], NT, preferred_element_type=F32)
         for i in range(2):
             part = g[:, i * 2 * E:(i + 1) * 2 * E]
             even, odd = interleave(part[:B], part[B:])
-            out_ref[4 * quad + 2 * i] = even.astype(BF)
-            out_ref[4 * quad + 2 * i + 1] = odd.astype(BF)
-
-
-def forward_kernel(group, layout_ref, qkv_ref, g_ref, attg_ref, stat_ref, kvt_ref):
+            out_ref[4 * quad + 2 * i, B:] = even.astype(BF)
+            out_ref[4 * quad + 2 * i + 1, B:] = odd.astype(BF)
+
+
+def forward_kernel(group, layout_ref, qkv_ref, att_ref, stat_ref, kvt_ref):
     blocks = layout_ref.shape[0]
     scale = 1.0 / E**0.5
     log2e = 1.4426950408889634
@@ -85,7 +99,7 @@
     def step(n, carry):
         pairs = [n * group + i for i in range(group)]
         zero = jnp.zeros((E, B), BF)
-        qts = [qkv_ref[pl.ds(pl.multiple_of(s * 3 * B, B), B), :].T for s in pairs]
+        qts = [qkv_ref[pl.ds(pl.multiple_of(s * 5 * B, B), B), :].T for s in pairs]
         work = [(s, p, [layout_ref[2 * s + p, j] for j in range(4)]) for s in pairs for p in range(2)]
         scores = []
         for i, (s, p, ids) in enumerate(work):
@@ -104,8 +118,7 @@
             stat_ref[2 * s + p] = jnp.concatenate([tops[i], inverses[i]], axis=0)
         for i, s in enumerate(pairs):
             att = jnp.concatenate([outs[2 * i], outs[2 * i + 1]], axis=0).astype(BF)
-            attg_ref[s, :B] = att.T
-            attg_ref[s, B:] = g_ref[s]
+            att_ref[s] = att.T
         return carry
 
     lax.fori_loop(0, blocks // 2 // group, step, 0)
@@ -122,7 +135,7 @@
     def step(n, carry):
         pairs = [n * group + i for i in range(group)]
         zero = jnp.zeros((E, B), BF)
-        qts = [qkv_ref[pl.ds(pl.multiple_of(s * 3 * B, B), B), :].T for s in pairs]
+        qts = [qkv_ref[pl.ds(pl.multiple_of(s * 5 * B, B), B), :].T for s in pairs]
         gts = [attg_ref[s, B:].T for s in pairs]
         work = [(s, p, [layout_ref[2 * s + p, j] for j in range(4)]) for s in pairs for p in range(2)]
         xts, boths = [], []
@@ -184,33 +197,45 @@
         ).astype(BF)
 
 
-def partial_kernel(attg_ref, og_ref, perm_ref, own_ref, other_ref, att_ref, tmp_ref):
+def partial_kernel(core_ref, attg_ref, og_ref, perm_ref, own_ref, other_ref, att_ref, tmp_ref):
     unpack_tokens(attg_ref, tmp_ref)
     reorder(tmp_ref, perm_ref, att_ref)
-    half = own_ref.shape[0]
-    for ref, base in ((other_ref, half), (own_ref, 0)):
-        for i in range(half // (4 * E)):
-            cols = slice(base + i * 4 * E, base + (i + 1) * 4 * E)
-            ref[i * 4 * E:(i + 1) * 4 * E, :] = lax.dot_general(
-                att_ref[:, cols], og_ref[...], TN, preferred_element_type=F32
-            ).astype(BF)
-
-
-def mixed_kernel(att_ref, w_own_ref, w_other_ref, mixed_ref):
-    half = w_own_ref.shape[0]
-    for i in range(H // 4):
-        cols = slice(i * 4 * E, (i + 1) * 4 * E)
-        total = lax.dot_general(
-            att_ref[:, :half], w_own_ref[:, cols], NN, preferred_element_type=F32
-        )
-        total += lax.dot_general(
-            att_ref[:, half:], w_other_ref[:, cols], NN, preferred_element_type=F32
-        )
-        mixed_ref[:, cols] = total.astype(BF)
-
-
-def add_kernel(a_ref, b_ref, out_ref):
-    out_ref[...] = (a_ref[...].astype(F32) + b_ref[...].astype(F32)).astype(BF)
+    core = core_ref[0]
+    owners, place = own_ref.shape[0], own_ref.shape[1] // 4
+    each = 4 * E // place
+    for ref, half in ((other_ref, 1 - core), (own_ref, core)):
+        og = column_half(og_ref, half)
+        for i in range(owners // each):
+            cols = slice(i * 4 * E, (i + 1) * 4 * E)
+            part = lax.dot_general(att_ref[:, cols], og, TN, preferred_element_type=F32).astype(BF)
+            for s in range(each):
+                for c in range(4):
+                    ref[i * each + s, c * place:(c + 1) * place] = part[
+                        s * place:(s + 1) * place, c * B:(c + 1) * B
+                    ]
+
+
+def mixed_kernel(core_ref, att_ref, w_ref, mixed_ref):
+    width = w_ref.shape[1] // 2
+    for half in range(2):
+        core = core_ref[0] if half == 0 else 1 - core_ref[0]
+        for i in range(width // (2 * B)):
+            at = half * width + i * 2 * B
+            total = lax.dot_general(
+                att_ref[...], w_ref[:, at:at + 2 * B], NN, preferred_element_type=F32
+            )
+            mixed_ref[:, pl.ds(pl.multiple_of(core * width + i * 2 * B, B), 2 * B)] = total.astype(BF)
+
+
+def sum_kernel(even_ref, even2_ref, odd_ref, odd2_ref, total_ref):
+    place = total_ref.shape[0]
+    width = total_ref.shape[1] // 2
+    for half, refs in enumerate(((even_ref, even2_ref), (odd_ref, odd2_ref))):
+        for n, ref in enumerate(refs):
+            total = jnp.sum(ref[:, 0].astype(F32), axis=0).astype(BF)
+            for c in range(2):
+                at = half * width + (2 * n + c) * B
+                total_ref[:, at:at + B] = total[c * place:(c + 1) * place]
 
 
 def unpack_kernel(src_ref, dq_ref, dk_ref, dv_ref):
@@ -218,29 +243,21 @@
     for pair in range(H // 2):
         cols = slice(pair * 2 * E, (pair + 1) * 2 * E)
         dk, dv = interleave(
-            src_ref[2 * pair, B:].astype(F32), src_ref[2 * pair + 1, B:].astype(F32)
+            src_ref[2 * pair, B:3 * B].astype(F32), src_ref[2 * pair + 1, B:3 * B].astype(F32)
         )
         dk_ref[:, cols] = dk.astype(BF)
         dv_ref[:, cols] = dv.astype(BF)
 
 
-def sum_kernel(parts_ref, total_ref):
-    total_ref[...] = jnp.sum(parts_ref[...].astype(F32), axis=0).astype(total_ref.dtype)
-
-
-def add_up(parts, dtype):
-    return call(sum_kernel, [(parts.shape[1:], dtype)], [VM], moved=2 * parts.size)(parts)[0]
-
-
-def forward(layout, qkv, g):
+def forward(layout, qkv):
     blocks = layout.shape[0]
     return call(
         functools.partial(forward_kernel, 4),
-        [((H, 2 * B, 2 * E), BF), ((blocks, 2, B), F32), ((blocks, 2 * E, B), BF)],
-        [SM, VM, VM],
-        flops=2 * qkv.shape[0] * 512 * 128,
+        [((H, B, 2 * E), BF), ((blocks, 2, B), F32), ((blocks, 2 * E, B), BF)],
+        [SM, VM],
+        flops=4 * 2**30,
         moved=4 * 2**20,
-    )(layout, qkv, g)
+    )(layout, qkv)
 
 
 def backward(layout, qkv, attg, kvt, stats):
@@ -250,7 +267,7 @@
         [((H, 3 * B, 2 * E), BF)],
         [SM] + [VM] * 4,
         [pltpu.VMEM((blocks * B, 2 * E), F32)],
-        flops=4 * qkv.shape[0] * 512 * 128,
+        flops=8 * 2**30,
         moved=6 * 2**20,
     )(layout, qkv, attg, kvt, stats)[0]
 
@@ -266,12 +283,10 @@
     return (feature == rows[None, :]).astype(BF)
 
 
-def reduced_order(width, dp, seq):
+def exchanged_order(width, dp, seq):
     each = width // (dp * seq)
     place = jnp.arange(width)
-    core = (place // (width // 2) + lax.axis_index("seq")) % 2
-    inner = place % (width // 2)
-    owner = (inner % (dp * each) // each) * seq + inner // (dp * each) * 2 + core
+    owner = (place % (dp * each) // each) * seq + place // (dp * each)
     return owner * each + place % each
 
 
@@ -280,43 +295,55 @@
     grad = out_grad[0]
     square = 2 * tokens * width * width
     scratch = [pltpu.VMEM((tokens, width), BF)]
+    core = (lax.axis_index("seq") & 1).reshape(1)
+    swap = [(i, i ^ 1) for i in range(seq)]
     slabs = call(pack_kernel, [((H, 3 * B, 2 * E), BF)], [VM] * 3, moved=3 * 2**20)(
         queries[0], keys[0], values[0]
     )[0]
-    perm = one_hot(width, reduced_order(width, dp, seq))
-    groups = [list(range(c, seq, 2)) for c in range(2)]
-    swap = [(i, i ^ 1) for i in range(seq)]
-    column = exchange(jnp.tile(out_weight[None], (dp, 1, 1)), "dp").reshape(-1, width)
+    perm = one_hot(width, exchanged_order(width, dp, seq))
+    column = exchange(jnp.tile(out_weight[None], (dp, 1, 1)), "dp").reshape(-1, 2, 4, B)
     column, slabs, perm = lax.optimization_barrier((column, slabs, perm))
-    w_own = exchange(jnp.tile(column[None], (seq // 2, 1, 1)), "seq", groups).reshape(-1, width)
-    w_own, slabs = lax.optimization_barrier((w_own, slabs))
-    qkv = exchange(slabs, "seq").reshape(-1, 2 * E)
+    halves = column.transpose(1, 2, 0, 3).reshape(1, 2, 2 * B, B)
+    halves = jnp.tile(halves, (seq // 2, 1, 1, 1)).reshape(seq, 2 * B, B)
+    slabs = exchange(jnp.concatenate([slabs, halves], axis=1), "seq")
+    w_own = slabs[:, 3 * B:]
     w_other = lax.ppermute(w_own, "seq", swap)
-    g = call(
-        grad_kernel, [((H, B, 2 * E), BF)], [VM] * 4, scratch, flops=2 * square, moved=6 * 2**20
-    )(grad, w_own, w_other, perm)[0]
-    g, qkv = lax.optimization_barrier((g, qkv))
-    attg, stats, kvt = forward(layout, qkv, g)
+    qkv = slabs.reshape(-1, B)
+    att, stats, kvt = forward(layout, qkv)
+    attg, weight = call(
+        grad_kernel, [((H, 2 * B, 2 * E), BF), ((width, width), BF)], [SM] + [VM] * 5, scratch,
+        flops=2 * square, moved=8 * 2**20,
+    )(core, grad, w_own, w_other, perm, att)
     attg = exchange(attg, "seq")
-    half = (width // 2, width)
+    half = (seq, 2 * B, B)
     own, other, att = call(
-        partial_kernel, [(half, BF)] * 2 + [((tokens, width), BF)], [VM] * 3, scratch,
+        partial_kernel, [(half, BF)] * 2 + [((tokens, width), BF)], [SM] + [VM] * 3, scratch,
         flops=2 * square, moved=6 * 2**20,
-    )(attg, grad, perm)
+    )(core, attg, grad, perm)
     other = lax.ppermute(other, "seq", swap)
-    own = call(add_kernel, [(half, BF)], [VM] * 2, moved=3 * 2**20)(own, other)[0]
-    terms = exchange(own.reshape(seq // 2, -1, width), "seq", groups)
-    total = add_up(terms, BF).reshape(dp, -1, width)
-    attg, total = lax.optimization_barrier((attg, total))
-    total = exchange(total, "dp")
     slabs = backward(layout, qkv, attg, kvt, stats)
+    terms = (own.astype(F32) + other.astype(F32)).astype(BF)
+    slabs = exchange(jnp.concatenate([slabs, terms], axis=1), "seq")
+    pieces = slabs.reshape(seq // 2, 2, 5 * B, B)
+    total = pl.pallas_call(
+        sum_kernel,
+        grid=(1,),
+        out_shape=jax.ShapeDtypeStruct((2 * dp, width), BF),
+        in_specs=[
+            pl.BlockSpec((seq // 2, 1, B, B), lambda i, c=c, n=n: (0, c, 3 + n, 0))
+            for c in range(2)
+            for n in range(2)
+        ],
+        out_specs=VM,
+        compiler_params=pltpu.CompilerParams(vmem_limit_bytes=48 * 2**20),
+    )(pieces, pieces, pieces, pieces)
+    total = exchange(total.reshape(dp, -1, width), "dp")
     mixed = call(
-        mixed_kernel, [((tokens, width), BF)], [VM] * 3, flops=square, moved=3 * 2**20
-    )(att, w_own, w_other)[0]
-    slabs, total = lax.optimization_barrier((slabs, total))
+        mixed_kernel, [((tokens, width), BF)], [SM] + [VM] * 2, flops=square, moved=3 * 2**20
+    )(core, att, weight)[0]
+    mixed, slabs = lax.optimization_barrier((mixed, slabs))
+    dq, dk, dv = call(unpack_kernel, [((tokens, width), BF)] * 3, [VM], moved=3 * 2**20)(slabs)
     weight_grad = total.astype(F32).sum(axis=0)
-    slabs = exchange(slabs, "seq")
-    dq, dk, dv = call(unpack_kernel, [((tokens, width), BF)] * 3, [VM], moved=3 * 2**20)(slabs)
     return mixed[None], dq[None], dk[None], dv[None], weight_grad
 
 

time: 189 us -> 183 us (0.968)
  blocking collectives: 52.5 us -> 93.1 us
  waiting for transfers between devices: 48 us -> 18.5 us
  starting transfers between devices: 46.3 us -> 28.5 us
  local copies, waits for them, and re-layouts: 11.9 us -> 8.34 us
  other arithmetic: 1.62 us -> 3.66 us
    all_to_all x3, blocking collectives: 52.5 us -> 93.1 us  [exchange(): lax.all_to_all(x, axis, split_axis=0, concat_axis=0, tiled=True, axis_ind...]
    all_to_all x4 -> x2, waiting for transfers between devices: 43.3 us -> 18.5 us  [exchange(): lax.all_to_all(x, axis, split_axis=0, concat_axis=0, tiled=True, axis_ind...]
    all_to_all x4 -> x2, starting transfers between devices: 41.1 us -> 22.3 us  [exchange(): lax.all_to_all(x, axis, split_axis=0, concat_axis=0, tiled=True, axis_ind...]
    unnamed x27 -> x15, local copies, waits for them, and re-layouts: 9.61 us -> 4.8 us
    ppermute x1, waiting for transfers between devices: 2.38 us -> 0.01 us  [body(): w_other = lax.ppermute(w_own, 'seq', swap)]
    ppermute x1, waiting for transfers between devices: 2.26 us -> 0.01 us  [body(): other = lax.ppermute(other, 'seq', swap)]
    pallas_call x6 -> x5, Pallas kernels: 15.4 us -> 15.6 us  [the longest x1 5.88 us: forward(): call(functools.partial(forward_kernel, 4), [((H, B, 2 * E), BF), ((blocks...]
  transfers between devices with their start and end apart: 6 -> 4, of which waited for: 6 -> 2; matrix products, arithmetic and copies ran while one was open for 1% -> 1% of each run, Pallas kernels for 8% -> 10%
where the time goes in v6:
time: 183 us; the launch traced here: 180 us
  blocking collectives  93.1 us (51%)
  starting transfers between devices  28.5 us (16%)
  Pallas kernels  27 us (15%)
  waiting for transfers between devices  18.5 us (10%)
  local copies, waits for them, and re-layouts  8.34 us (5%)
  other arithmetic  3.66 us (2%)
    all_to_all x3, blocking collectives, exchange(): lax.all_to_all(x, axis, split_axis=0, concat_axis=0, tiled=True, axis_ind...  93.1 us
    all_to_all x2, starting transfers between devices, exchange(): lax.all_to_all(x, axis, split_axis=0, concat_axis=0, tiled=True, axis_ind...  22.3 us
    all_to_all x2, waiting for transfers between devices, exchange(): lax.all_to_all(x, axis, split_axis=0, concat_axis=0, tiled=True, axis_ind...  18.5 us
    pallas_call x1, Pallas kernels, backward(): call(functools.partial(backward_kernel, 4), [((H, 3 * B, 2 * E), BF)], [S...  8.96 us
    pallas_call x1, Pallas kernels, forward(): call(functools.partial(forward_kernel, 4), [((H, B, 2 * E), BF), ((blocks...  5.88 us
    pallas_call x1, Pallas kernels, body(): call(grad_kernel, [((H, 2 * B, 2 * E), BF), ((width, width), BF)], [SM] +...  4.99 us
    unnamed x15, local copies, waits for them, and re-layouts  4.8 us
  transfers between devices with their start and end apart: 4, of which 2 were waited for; matrix products, arithmetic and copies ran while one was open for 1% of the time, Pallas kernels for 10%

profile of v6, /device:TPU:1, one launch (start us, length us, event | category | flops | bytes accessed | tf_op | source)
XLA Modules:
  0.0 180.0 jit_solution(16009161155923785970)
XLA Ops:
  0.6 1.4 tile.15
  2.0 18.5 %all-to-all-start = ((bf16[32,2,1024]{2,1,0:T(2,128)(2,1)}), bf16[32,2,1024]{2,1,0:T(2,128)(2,1)S(1)}, u32[]{:S(2)}, u32[]{:S(2)}) async-start(bf16[32,2,1024]{2,1,0:T(2,128)(2,1)} %tile.15), calls=%async_computation | async-start | bytes 262144 | tf_op jit(solution)/shard_map/all_to_all | solution.py:276
  20.5 0.0 copy-start.2
  20.6 1.0 copy-done.2
  21.6 0.0 copy-start.3
  21.6 1.0 copy-done.3
  22.6 0.0 copy-start.4
  22.6 1.0 copy-done.4
  23.7 0.7 shard_map.101
  24.4 2.2 %fusion.perm_ref = bf16[1024,1024]{1,0:T(8,128)(2,1)} fusion(s32[1024]{0:T(1024)S(1)} %fusion.15), kind=kLoop, calls=%fused_computation.1 | loop fusion | flops 2097152 | bytes 2101248 | tf_op jit(solution)/shard_map/convert_element_type | solution.py:283
  26.6 8.7 %all-to-all-done = bf16[32,2,1024]{2,1,0:T(2,128)(2,1)S(1)} async-done(((bf16[32,2,1024]{2,1,0:T(2,128)(2,1)}), bf16[32,2,1024]{2,1,0:T(2,128)(2,1)S(1)}, u32[]{:S(2)}, u32[]{:S(2)}) %all-to-all-start) | async-done | bytes 131104 | tf_op jit(solution)/shard_map/all_to_all | solution.py:276
  35.3 0.1 reshape.79
  35.4 0.2 tile.17
  35.6 0.2 pad_maximum_fusion
  35.8 0.0 copy-start.6
  35.8 40.3 %all_to_all.25 = bf16[16,640,128]{2,1,0:T(8,128)(2,1)S(1)} all-to-all(bf16[16,640,128]{2,1,0:T(8,128)(2,1)S(1)} %pad_maximum_fusion), channel_id=1, replica_groups=mesh['dp'=32,'seq'=16] {'seq'}, dimensions={0} | all-to-all | bytes 5242880 | tf_op jit(solution)/shard_map/all_to_all | solution.py:276
  76.1 0.0 copy-start
  76.1 1.1 slice.4.own_ref
  77.3 3.1 %collective-permute-start = (bf16[16,256,128]{2,1,0:T(8,128)(2,1)}, bf16[16,256,128]{2,1,0:T(8,128)(2,1)}, u32[]{:S(2)}, u32[]{:S(2)}) collective-permute-start(bf16[16,256,128]{2,1,0:T(8,128)(2,1)} %slice.4.own_ref), channel_id=1, source_target_pairs={{0,1},{1,0},{2,3},{3,2},{4,5},{5,4},{6,7},{7,6},{8,9},{9,8},{10,11... | collective-permute-start | bytes 3145736 | tf_op jit(solution)/shard_map/ppermute | solution.py:310
  80.3 0.0 copy-done.6
  80.3 0.1 copy.16.layout_ref
  80.4 0.0 copy-start.5
  80.4 5.9 %shard_map.102 = (bf16[16,128,128]{2,1,0:T(8,128)(2,1)S(1)}, f32[32,2,128]{2,1,0:T(2,128)S(1)}, bf16[32,128,128]{2,1,0:T(8,128)(2,1)S(1)}) custom-call(s32[32,4]{1,0:T(8,128)S(1)} %copy.16.layout_ref, bf16[10240,128]{1,0:T(8,128)(2,1)S(1)} %bitcast.18), custom_call_target="tpu_custom_call" | custom-call | flops 4294967296 | bytes 4194304 | tf_op jit(solution)/shard_map/pallas_call | solution.py:254
  86.3 0.0 copy-done
  86.3 0.0 collective-permute-done.other_ref
  86.3 0.0 copy-done.5
  86.4 5.0 %shard_map.103 = (bf16[16,256,128]{2,1,0:T(8,128)(2,1)S(1)}, bf16[1024,1024]{1,0:T(8,128)(2,1)}) custom-call(s32[1]{0:T(128)} %bitcast.core_ref, bf16[256,1024]{1,0:T(8,128)(2,1)S(1)} %bitcast.23, bf16[16,256,128]{2,1,0:T(8,128)(2,1)} %slice.4.own_ref, bf16[16,256,128]{2,1,0:T(8,128)(2,1)} %collective-permute-done.other_ref, ...), custom_call_target="tpu_custom_call" | custom-call | flops 1073741824 | bytes 8388608 | tf_op jit(solution)/shard_map/pallas_call | solution.py:313
  91.3 18.0 %all_to_all.26.attg_ref = bf16[16,256,128]{2,1,0:T(8,128)(2,1)S(1)} all-to-all(bf16[16,256,128]{2,1,0:T(8,128)(2,1)S(1)} %get-tuple-element.25), channel_id=1, replica_groups=mesh['dp'=32,'seq'=16] {'seq'}, dimensions={0} | all-to-all | bytes 2097152 | tf_op jit(solution)/shard_map/all_to_all | solution.py:276
  109.3 3.0 %shard_map.104 = (bf16[16,256,128]{2,1,0:T(8,128)(2,1)S(1)}, bf16[16,256,128]{2,1,0:T(8,128)(2,1)S(1)}, bf16[256,1024]{1,0:T(8,128)(2,1)S(1)}) custom-call(s32[1]{0:T(128)} %bitcast.core_ref, bf16[16,256,128]{2,1,0:T(8,128)(2,1)S(1)} %all_to_all.26.attg_ref, bf16[256,1024]{1,0:T(8,128)(2,1)S(1)} %bitcast.24, bf16[1024,1024]{1,0:T(8,128)(2,1)} %fusion.perm_ref), custom_call_target="tpu_custom_call" | custom-call | flops 1073741824 | bytes 6291456 | tf_op jit(solution)/shard_map/pallas_call | solution.py:319
  112.3 3.1 %collective-permute-start.1 = (bf16[16,256,128]{2,1,0:T(8,128)(2,1)S(1)}, bf16[16,256,128]{2,1,0:T(8,128)(2,1)S(1)}, u32[]{:S(2)}, u32[]{:S(2)}) collective-permute-start(bf16[16,256,128]{2,1,0:T(8,128)(2,1)S(1)} %get-tuple-element.31), channel_id=1, source_target_pairs={{0,1},{1,0},{2,3},{3,2},{4,5},{5,4},{6,7},{7,6},{8,9},{9,8},{10,11... | collective-permute-start | bytes 3145736 | tf_op jit(solution)/shard_map/ppermute | solution.py:323
  115.4 9.0 %shard_map.106 = bf16[16,384,128]{2,1,0:T(8,128)(2,1)S(1)} custom-call(s32[32,4]{1,0:T(8,128)S(1)} %copy.16.layout_ref, bf16[10240,128]{1,0:T(8,128)(2,1)} %bitcast.19, bf16[16,256,128]{2,1,0:T(8,128)(2,1)S(1)} %all_to_all.26.attg_ref, bf16[32,128,128]{2,1,0:T(8,128)(2,1)S(1)} %get-tuple-element.28.kvt_ref, f32[32,2,128]{2,1,0:T(2,128)S(1)} %get-tuple-element.29.stat_ref), custom_call_target="tpu_custom_call" | custom-call | flops 8589934592 | bytes 6291456 | tf_op jit(solution)/shard_map/pallas_call | solution.py:265
  124.4 0.0 collective-permute-done.1
  124.4 0.3 add_convert_fusion
  124.7 0.2 pad_maximum_fusion.1
  124.9 34.8 %all_to_all.27.src_ref = bf16[16,640,128]{2,1,0:T(8,128)(2,1)S(1)} all-to-all(bf16[16,640,128]{2,1,0:T(8,128)(2,1)S(1)} %pad_maximum_fusion.1), channel_id=1, replica_groups=mesh['dp'=32,'seq'=16] {'seq'}, dimensions={0} | all-to-all | bytes 5242880 | tf_op jit(solution)/shard_map/all_to_all | solution.py:276
  159.7 0.2 shard_map.108
  160.0 0.7 reshape.82
  160.7 3.9 %all-to-all-start.4 = ((bf16[32,2,1024]{2,1,0:T(2,128)(2,1)}), bf16[32,2,1024]{2,1,0:T(2,128)(2,1)S(1)}, u32[]{:S(2)}, u32[]{:S(2)}) async-start(bf16[32,2,1024]{2,1,0:T(2,128)(2,1)} %reshape.82), calls=%async_computation.4 | async-start | bytes 262144 | tf_op jit(solution)/shard_map/all_to_all | solution.py:276
  164.5 0.0 copy-start.1
  164.6 1.6 copy-done.1
  166.1 1.6 shard_map.105
  167.7 1.7 shard_map.107
  169.4 9.8 %all-to-all-done.4 = bf16[32,2,1024]{2,1,0:T(2,128)(2,1)S(1)} async-done(((bf16[32,2,1024]{2,1,0:T(2,128)(2,1)}), bf16[32,2,1024]{2,1,0:T(2,128)(2,1)S(1)}, u32[]{:S(2)}, u32[]{:S(2)}) %all-to-all-start.4) | async-done | bytes 131104 | tf_op jit(solution)/shard_map/all_to_all | solution.py:276
  179.3 0.7 convert_reduce_fusion
  (2 shorter events, 0.0 us)
Async XLA Ops:
  2.0 33.2 %all-to-all-start = ((bf16[32,2,1024]{2,1,0:T(2,128)(2,1)}), bf16[32,2,1024]{2,1,0:T(2,128)(2,1)S(1)}, u32[]{:S(2)}, u32[]{:S(2)}) async-start(bf16[32,2,1024]{2,1,0:T(2,128)(2,1)} %tile.15), calls=%async_computation | async-start | bytes 262144 | tf_op jit(solution)/shard_map/all_to_all | solution.py:276
  20.5 1.0 copy-start.2
  21.6 1.0 copy-start.3
  22.6 1.0 copy-start.4
  35.8 44.5 %copy-start.6 = (s32[32,4]{0,1:T(4,128)S(1)}, s32[32,4]{0,1:T(4,128)}, u32[]{:S(2)}) copy-start(s32[32,4]{0,1:T(4,128)} %param.11) | copy-start | bytes 1540
  76.1 10.2 %copy-start = (bf16[16,640,128]{2,1,0:T(8,128)(2,1)}, bf16[16,640,128]{2,1,0:T(8,128)(2,1)S(1)}, u32[]{:S(2)}) copy-start(bf16[16,640,128]{2,1,0:T(8,128)(2,1)S(1)} %all_to_all.25) | copy-start | bytes 7864324
  77.3 9.1 %collective-permute-start = (bf16[16,256,128]{2,1,0:T(8,128)(2,1)}, bf16[16,256,128]{2,1,0:T(8,128)(2,1)}, u32[]{:S(2)}, u32[]{:S(2)}) collective-permute-start(bf16[16,256,128]{2,1,0:T(8,128)(2,1)} %slice.4.own_ref), channel_id=1, source_target_pairs={{0,1},{1,0},{2,3},{3,2},{4,5},{5,4},{6,7},{7,6},{8,9},{9,8},{10,11... | collective-permute-start | bytes 3145736 | tf_op jit(solution)/shard_map/ppermute | solution.py:310
  80.4 5.9 %copy-start.5 = (bf16[1,256,1024]{2,1,0:T(8,128)(2,1)S(1)}, bf16[1,256,1024]{2,1,0:T(8,128)(2,1)}, u32[]{:S(2)}) copy-start(bf16[1,256,1024]{2,1,0:T(8,128)(2,1)} %param.9) | copy-start | bytes 1572868
  112.3 12.1 %collective-permute-start.1 = (bf16[16,256,128]{2,1,0:T(8,128)(2,1)S(1)}, bf16[16,256,128]{2,1,0:T(8,128)(2,1)S(1)}, u32[]{:S(2)}, u32[]{:S(2)}) collective-permute-start(bf16[16,256,128]{2,1,0:T(8,128)(2,1)S(1)} %get-tuple-element.31), channel_id=1, source_target_pairs={{0,1},{1,0},{2,3},{3,2},{4,5},{5,4},{6,7},{7,6},{8,9},{9,8},{10,11... | collective-permute-start | bytes 3145736 | tf_op jit(solution)/shard_map/ppermute | solution.py:323
  160.7 18.6 %all-to-all-start.4 = ((bf16[32,2,1024]{2,1,0:T(2,128)(2,1)}), bf16[32,2,1024]{2,1,0:T(2,128)(2,1)S(1)}, u32[]{:S(2)}, u32[]{:S(2)}) async-start(bf16[32,2,1024]{2,1,0:T(2,128)(2,1)} %reshape.82), calls=%async_computation.4 | async-start | bytes 262144 | tf_op jit(solution)/shard_map/all_to_all | solution.py:276
  164.5 1.6 copy-start.1

commit v7 on v6

--- a/solution.py
+++ b/solution.py
@@ -252,7 +252,7 @@
 def forward(layout, qkv):
     blocks = layout.shape[0]
     return call(
-        functools.partial(forward_kernel, 4),
+        functools.partial(forward_kernel, 8),
         [((H, B, 2 * E), BF), ((blocks, 2, B), F32), ((blocks, 2 * E, B), BF)],
         [SM, VM],
         flops=4 * 2**30,
@@ -263,7 +263,7 @@
 def backward(layout, qkv, attg, kvt, stats):
     blocks = layout.shape[0]
     return call(
-        functools.partial(backward_kernel, 4),
+        functools.partial(backward_kernel, 8),
         [((H, 3 * B, 2 * E), BF)],
         [SM] + [VM] * 4,
         [pltpu.VMEM((blocks * B, 2 * E), F32)],

time: 183 us -> 181 us (0.989)
  no operation moved by 1% of the time
where the time goes in v7:
time: 181 us; the launch traced here: 179 us
  blocking collectives  93.1 us (51%)
  starting transfers between devices  28.5 us (16%)
  Pallas kernels  25.7 us (14%)
  waiting for transfers between devices  18.5 us (10%)
  local copies, waits for them, and re-layouts  8.34 us (5%)
  other arithmetic  3.66 us (2%)
    all_to_all x3, blocking collectives, exchange(): lax.all_to_all(x, axis, split_axis=0, concat_axis=0, tiled=True, axis_ind...  93.1 us
    all_to_all x2, starting transfers between devices, exchange(): lax.all_to_all(x, axis, split_axis=0, concat_axis=0, tiled=True, axis_ind...  22.3 us
    all_to_all x2, waiting for transfers between devices, exchange(): lax.all_to_all(x, axis, split_axis=0, concat_axis=0, tiled=True, axis_ind...  18.5 us
    pallas_call x1, Pallas kernels, backward(): call(functools.partial(backward_kernel, 8), [((H, 3 * B, 2 * E), BF)], [S...  8.59 us
    pallas_call x1, Pallas kernels, body(): call(grad_kernel, [((H, 2 * B, 2 * E), BF), ((width, width), BF)], [SM] +...  4.99 us
    pallas_call x1, Pallas kernels, forward(): call(functools.partial(forward_kernel, 8), [((H, B, 2 * E), BF), ((blocks...  4.89 us
    unnamed x15, local copies, waits for them, and re-layouts  4.8 us
  transfers between devices with their start and end apart: 4, of which 2 were waited for; matrix products, arithmetic and copies ran while one was open for 1% of the time, Pallas kernels for 10%

profile of v7, /device:TPU:1, one launch (start us, length us, event | category | flops | bytes accessed | tf_op | source)
XLA Modules:
  0.0 178.6 jit_solution(10203575385384503915)
XLA Ops:
  0.6 1.4 tile.15
  2.0 18.5 %all-to-all-start = ((bf16[32,2,1024]{2,1,0:T(2,128)(2,1)}), bf16[32,2,1024]{2,1,0:T(2,128)(2,1)S(1)}, u32[]{:S(2)}, u32[]{:S(2)}) async-start(bf16[32,2,1024]{2,1,0:T(2,128)(2,1)} %tile.15), calls=%async_computation | async-start | bytes 262144 | tf_op jit(solution)/shard_map/all_to_all | solution.py:276
  20.5 0.0 copy-start.2
  20.6 1.0 copy-done.2
  21.6 0.0 copy-start.3
  21.6 1.0 copy-done.3
  22.6 0.0 copy-start.4
  22.6 1.0 copy-done.4
  23.7 0.7 shard_map.101
  24.4 2.2 %fusion.perm_ref = bf16[1024,1024]{1,0:T(8,128)(2,1)} fusion(s32[1024]{0:T(1024)S(1)} %fusion.15), kind=kLoop, calls=%fused_computation.1 | loop fusion | flops 2097152 | bytes 2101248 | tf_op jit(solution)/shard_map/convert_element_type | solution.py:283
  26.6 8.7 %all-to-all-done = bf16[32,2,1024]{2,1,0:T(2,128)(2,1)S(1)} async-done(((bf16[32,2,1024]{2,1,0:T(2,128)(2,1)}), bf16[32,2,1024]{2,1,0:T(2,128)(2,1)S(1)}, u32[]{:S(2)}, u32[]{:S(2)}) %all-to-all-start) | async-done | bytes 131104 | tf_op jit(solution)/shard_map/all_to_all | solution.py:276
  35.3 0.1 reshape.79
  35.4 0.2 tile.17
  35.6 0.2 pad_maximum_fusion
  35.8 0.0 copy-start.6
  35.8 40.3 %all_to_all.25 = bf16[16,640,128]{2,1,0:T(8,128)(2,1)S(1)} all-to-all(bf16[16,640,128]{2,1,0:T(8,128)(2,1)S(1)} %pad_maximum_fusion), channel_id=1, replica_groups=mesh['dp'=32,'seq'=16] {'seq'}, dimensions={0} | all-to-all | bytes 5242880 | tf_op jit(solution)/shard_map/all_to_all | solution.py:276
  76.1 0.0 copy-start
  76.1 1.1 slice.4.own_ref
  77.3 3.1 %collective-permute-start = (bf16[16,256,128]{2,1,0:T(8,128)(2,1)}, bf16[16,256,128]{2,1,0:T(8,128)(2,1)}, u32[]{:S(2)}, u32[]{:S(2)}) collective-permute-start(bf16[16,256,128]{2,1,0:T(8,128)(2,1)} %slice.4.own_ref), channel_id=1, source_target_pairs={{0,1},{1,0},{2,3},{3,2},{4,5},{5,4},{6,7},{7,6},{8,9},{9,8},{10,11... | collective-permute-start | bytes 3145736 | tf_op jit(solution)/shard_map/ppermute | solution.py:310
  80.3 0.0 copy-done.6
  80.3 0.1 copy.16.layout_ref
  80.4 0.0 copy-start.5
  80.4 4.9 %shard_map.102 = (bf16[16,128,128]{2,1,0:T(8,128)(2,1)S(1)}, f32[32,2,128]{2,1,0:T(2,128)S(1)}, bf16[32,128,128]{2,1,0:T(8,128)(2,1)S(1)}) custom-call(s32[32,4]{1,0:T(8,128)S(1)} %copy.16.layout_ref, bf16[10240,128]{1,0:T(8,128)(2,1)S(1)} %bitcast.18), custom_call_target="tpu_custom_call" | custom-call | flops 4294967296 | bytes 4194304 | tf_op jit(solution)/shard_map/pallas_call | solution.py:254
  85.3 0.0 copy-done
  85.3 0.0 collective-permute-done.other_ref
  85.3 0.0 copy-done.5
  85.4 5.0 %shard_map.103 = (bf16[16,256,128]{2,1,0:T(8,128)(2,1)S(1)}, bf16[1024,1024]{1,0:T(8,128)(2,1)}) custom-call(s32[1]{0:T(128)} %bitcast.core_ref, bf16[256,1024]{1,0:T(8,128)(2,1)S(1)} %bitcast.23, bf16[16,256,128]{2,1,0:T(8,128)(2,1)} %slice.4.own_ref, bf16[16,256,128]{2,1,0:T(8,128)(2,1)} %collective-permute-done.other_ref, ...), custom_call_target="tpu_custom_call" | custom-call | flops 1073741824 | bytes 8388608 | tf_op jit(solution)/shard_map/pallas_call | solution.py:313
  90.3 18.0 %all_to_all.26.attg_ref = bf16[16,256,128]{2,1,0:T(8,128)(2,1)S(1)} all-to-all(bf16[16,256,128]{2,1,0:T(8,128)(2,1)S(1)} %get-tuple-element.25), channel_id=1, replica_groups=mesh['dp'=32,'seq'=16] {'seq'}, dimensions={0} | all-to-all | bytes 2097152 | tf_op jit(solution)/shard_map/all_to_all | solution.py:276
  108.3 3.0 %shard_map.104 = (bf16[16,256,128]{2,1,0:T(8,128)(2,1)S(1)}, bf16[16,256,128]{2,1,0:T(8,128)(2,1)S(1)}, bf16[256,1024]{1,0:T(8,128)(2,1)S(1)}) custom-call(s32[1]{0:T(128)} %bitcast.core_ref, bf16[16,256,128]{2,1,0:T(8,128)(2,1)S(1)} %all_to_all.26.attg_ref, bf16[256,1024]{1,0:T(8,128)(2,1)S(1)} %bitcast.24, bf16[1024,1024]{1,0:T(8,128)(2,1)} %fusion.perm_ref), custom_call_target="tpu_custom_call" | custom-call | flops 1073741824 | bytes 6291456 | tf_op jit(solution)/shard_map/pallas_call | solution.py:319
  111.3 3.1 %collective-permute-start.1 = (bf16[16,256,128]{2,1,0:T(8,128)(2,1)S(1)}, bf16[16,256,128]{2,1,0:T(8,128)(2,1)S(1)}, u32[]{:S(2)}, u32[]{:S(2)}) collective-permute-start(bf16[16,256,128]{2,1,0:T(8,128)(2,1)S(1)} %get-tuple-element.31), channel_id=1, source_target_pairs={{0,1},{1,0},{2,3},{3,2},{4,5},{5,4},{6,7},{7,6},{8,9},{9,8},{10,11... | collective-permute-start | bytes 3145736 | tf_op jit(solution)/shard_map/ppermute | solution.py:323
  114.4 8.6 %shard_map.106 = bf16[16,384,128]{2,1,0:T(8,128)(2,1)S(1)} custom-call(s32[32,4]{1,0:T(8,128)S(1)} %copy.16.layout_ref, bf16[10240,128]{1,0:T(8,128)(2,1)} %bitcast.19, bf16[16,256,128]{2,1,0:T(8,128)(2,1)S(1)} %all_to_all.26.attg_ref, bf16[32,128,128]{2,1,0:T(8,128)(2,1)S(1)} %get-tuple-element.28.kvt_ref, f32[32,2,128]{2,1,0:T(2,128)S(1)} %get-tuple-element.29.stat_ref), custom_call_target="tpu_custom_call" | custom-call | flops 8589934592 | bytes 6291456 | tf_op jit(solution)/shard_map/pallas_call | solution.py:265
  123.0 0.0 collective-permute-done.1
  123.0 0.3 add_convert_fusion
  123.3 0.2 pad_maximum_fusion.1
  123.5 34.8 %all_to_all.27.src_ref = bf16[16,640,128]{2,1,0:T(8,128)(2,1)S(1)} all-to-all(bf16[16,640,128]{2,1,0:T(8,128)(2,1)S(1)} %pad_maximum_fusion.1), channel_id=1, replica_groups=mesh['dp'=32,'seq'=16] {'seq'}, dimensions={0} | all-to-all | bytes 5242880 | tf_op jit(solution)/shard_map/all_to_all | solution.py:276
  158.4 0.2 shard_map.108
  158.6 0.7 reshape.82
  159.3 3.9 %all-to-all-start.4 = ((bf16[32,2,1024]{2,1,0:T(2,128)(2,1)}), bf16[32,2,1024]{2,1,0:T(2,128)(2,1)S(1)}, u32[]{:S(2)}, u32[]{:S(2)}) async-start(bf16[32,2,1024]{2,1,0:T(2,128)(2,1)} %reshape.82), calls=%async_computation.4 | async-start | bytes 262144 | tf_op jit(solution)/shard_map/all_to_all | solution.py:276
  163.2 0.0 copy-start.1
  163.2 1.6 copy-done.1
  164.8 1.6 shard_map.105
  166.3 1.7 shard_map.107
  168.1 9.8 %all-to-all-done.4 = bf16[32,2,1024]{2,1,0:T(2,128)(2,1)S(1)} async-done(((bf16[32,2,1024]{2,1,0:T(2,128)(2,1)}), bf16[32,2,1024]{2,1,0:T(2,128)(2,1)S(1)}, u32[]{:S(2)}, u32[]{:S(2)}) %all-to-all-start.4) | async-done | bytes 131104 | tf_op jit(solution)/shard_map/all_to_all | solution.py:276
  177.9 0.7 convert_reduce_fusion
  (2 shorter events, 0.0 us)
Async XLA Ops:
  2.0 33.2 %all-to-all-start = ((bf16[32,2,1024]{2,1,0:T(2,128)(2,1)}), bf16[32,2,1024]{2,1,0:T(2,128)(2,1)S(1)}, u32[]{:S(2)}, u32[]{:S(2)}) async-start(bf16[32,2,1024]{2,1,0:T(2,128)(2,1)} %tile.15), calls=%async_computation | async-start | bytes 262144 | tf_op jit(solution)/shard_map/all_to_all | solution.py:276
  20.5 1.0 copy-start.2
  21.6 1.0 copy-start.3
  22.6 1.0 copy-start.4
  35.8 44.5 %copy-start.6 = (s32[32,4]{0,1:T(4,128)S(1)}, s32[32,4]{0,1:T(4,128)}, u32[]{:S(2)}) copy-start(s32[32,4]{0,1:T(4,128)} %param.11) | copy-start | bytes 1540
  76.1 9.2 %copy-start = (bf16[16,640,128]{2,1,0:T(8,128)(2,1)}, bf16[16,640,128]{2,1,0:T(8,128)(2,1)S(1)}, u32[]{:S(2)}) copy-start(bf16[16,640,128]{2,1,0:T(8,128)(2,1)S(1)} %all_to_all.25) | copy-start | bytes 7864324
  77.3 8.1 %collective-permute-start = (bf16[16,256,128]{2,1,0:T(8,128)(2,1)}, bf16[16,256,128]{2,1,0:T(8,128)(2,1)}, u32[]{:S(2)}, u32[]{:S(2)}) collective-permute-start(bf16[16,256,128]{2,1,0:T(8,128)(2,1)} %slice.4.own_ref), channel_id=1, source_target_pairs={{0,1},{1,0},{2,3},{3,2},{4,5},{5,4},{6,7},{7,6},{8,9},{9,8},{10,11... | collective-permute-start | bytes 3145736 | tf_op jit(solution)/shard_map/ppermute | solution.py:310
  80.4 4.9 %copy-start.5 = (bf16[1,256,1024]{2,1,0:T(8,128)(2,1)S(1)}, bf16[1,256,1024]{2,1,0:T(8,128)(2,1)}, u32[]{:S(2)}) copy-start(bf16[1,256,1024]{2,1,0:T(8,128)(2,1)} %param.9) | copy-start | bytes 1572868
  111.3 11.7 %collective-permute-start.1 = (bf16[16,256,128]{2,1,0:T(8,128)(2,1)S(1)}, bf16[16,256,128]{2,1,0:T(8,128)(2,1)S(1)}, u32[]{:S(2)}, u32[]{:S(2)}) collective-permute-start(bf16[16,256,128]{2,1,0:T(8,128)(2,1)S(1)} %get-tuple-element.31), channel_id=1, source_target_pairs={{0,1},{1,0},{2,3},{3,2},{4,5},{5,4},{6,7},{7,6},{8,9},{9,8},{10,11... | collective-permute-start | bytes 3145736 | tf_op jit(solution)/shard_map/ppermute | solution.py:323
  159.3 18.6 %all-to-all-start.4 = ((bf16[32,2,1024]{2,1,0:T(2,128)(2,1)}), bf16[32,2,1024]{2,1,0:T(2,128)(2,1)S(1)}, u32[]{:S(2)}, u32[]{:S(2)}) async-start(bf16[32,2,1024]{2,1,0:T(2,128)(2,1)} %reshape.82), calls=%async_computation.4 | async-start | bytes 262144 | tf_op jit(solution)/shard_map/all_to_all | solution.py:276
  163.2 1.6 copy-start.1
